TPU v7x, 512 devices: a whole 4x4x16 slice. The times are simulated.
512 devices in a mesh: seq: 16 (over y, z_hi), own: 32 (over z_lo, x, core).
Axes of the slice: x: 4, y: 4, z: 16 (z_hi: 4, z_lo: 4; z = z_hi * 4 + z_lo), core: 2. Of those that a mesh axis runs over, the one named last changes fastest.
Arguments:
- queries: bfloat16 [32, 2048, 1024], P('own', 'seq'), may hold values from -6 to 6
- keys: bfloat16 [32, 2048, 1024], P('own', 'seq'), may hold values from -6 to 6
- values: bfloat16 [32, 2048, 1024], P('own', 'seq'), may hold values from -6 to 6
- gates: bfloat16 [32, 2048, 1024], P('own', 'seq'), may hold values from -6 to 6
- lengths: int32 [32, 4], P('own'), may hold values from 1 to 1024, 2048 in all within a row
- gain: float32 [1024], replicated, may hold values from 0.1 to 1.9
- grad_out: bfloat16 [32, 2048, 1024], P('own', 'seq'), may hold values from -6 to 6
Outputs:
- output: bfloat16 [32, 2048, 1024], P('own', 'seq')
- grad_queries: bfloat16 [32, 2048, 1024], P('own', 'seq')
- grad_keys: bfloat16 [32, 2048, 1024], P('own', 'seq')
- grad_values: bfloat16 [32, 2048, 1024], P('own', 'seq')
- grad_gates: bfloat16 [32, 2048, 1024], P('own', 'seq')
- grad_gain: float32 [1024], replicated
Inputs may be any that keep to these rules, and one draw needn't show every extreme that they name: Each group's 4 lengths sum to 2048; in every group the longest is exactly 1024.
All inputs are finite; a program needn't handle non-finite values.
Results may differ from a plain program's by a relative error of at most 0.0058.
Values may be sent and summed in bfloat16 or wider, within the bound.
No kernel may reach another device: no remote copies, remote signals or barrier semaphores. Data moves between devices by JAX's collectives and lax.ppermute only.
A program may use at most 128 MiB of HBM per device.

v0:
```python
import math

import jax
import jax.numpy as jnp
from jax import lax
from jax.sharding import PartitionSpec as P

H = 8


def shifted(array, axis, by):
    length = lax.axis_size(axis)
    pairs = [(i, i + by) for i in range(length) if 0 <= i + by < length]
    return lax.ppermute(array, axis, pairs)


def positions_info(pos, lens):
    ends = jnp.cumsum(lens)
    seg = jnp.sum((pos[:, None] >= ends[None, :]).astype(jnp.int32), axis=1)
    users = jnp.arange(lens.shape[0], dtype=jnp.int32)
    span = jnp.sum(jnp.where(seg[:, None] == users[None, :], lens[None, :], 0), axis=1)
    return (seg, 1.0 / jnp.maximum(span, 1).astype(jnp.float32))


def pair_weight(row_pos, row_seg, row_inverse, col_pos, col_seg):
    allowed = (row_seg[:, None] == col_seg[None, :]) & (col_pos[None, :] <= row_pos[:, None])
    allowed = allowed & (col_pos[None, :] >= 0) & (row_pos[:, None] >= 0)
    return jnp.where(allowed, row_inverse[:, None], jnp.float32(0.0))


def silu_slope(scores):
    sig = jax.nn.sigmoid(scores)
    return sig * (1.0 + scores * (1.0 - sig))


def per_device(queries, keys, values, gates, lengths, gain, grad_out):
    rows, width = (queries.shape[1], queries.shape[2])
    head_size = width // H
    scale = 1.0 / math.sqrt(head_size)
    lens = lengths[0]
    seq_count = lax.axis_size("seq")
    longest = rows * seq_count // 2
    reach = min(seq_count - 1, (longest - 1) // rows + 1)
    first = lax.axis_index("seq") * rows
    my_pos = first + jnp.arange(rows, dtype=jnp.int32)
    my_seg, my_inverse = positions_info(my_pos, lens)
    q3 = queries[0].reshape(rows, H, head_size)
    k3 = keys[0].reshape(rows, H, head_size)
    v3 = values[0].reshape(rows, H, head_size)

    def piece_info(start, count):
        col_pos = start + jnp.arange(count, dtype=jnp.int32)
        col_seg, col_inverse = positions_info(col_pos, lens)
        return (col_pos, col_seg, col_inverse)

    key_all, value_all = (
        lax.all_gather(keys, "seq", axis=1, tiled=True),
        lax.all_gather(values, "seq", axis=1, tiled=True),
    )
    total = key_all.shape[1]
    ka3 = key_all[0].reshape(total, H, head_size)
    va3 = value_all[0].reshape(total, H, head_size)
    col_pos, col_seg, col_inverse = piece_info(0, total)
    weight = pair_weight(my_pos, my_seg, my_inverse, col_pos, col_seg)
    scores = jnp.einsum("thd,shd->hts", q3, ka3, preferred_element_type=jnp.float32) * scale
    probs = (jax.nn.silu(scores) * weight[None]).astype(jnp.bfloat16)
    attended = jnp.einsum("hts,shd->thd", probs, va3, preferred_element_type=jnp.float32)
    attended = attended.reshape(rows, width)
    center = attended - jnp.mean(attended, axis=1, keepdims=True)
    rstd = lax.rsqrt(jnp.mean(center * center, axis=1, keepdims=True) + 1e-05)
    normed = center * rstd
    gate_f = gates[0].astype(jnp.float32)
    grad_f = grad_out[0].astype(jnp.float32)
    output = (normed * gain[None, :] * gate_f).astype(jnp.bfloat16)
    grad_gate = (grad_f * normed * gain[None, :]).astype(jnp.bfloat16)
    gain_part = jnp.sum(grad_f * gate_f * normed, axis=0)
    dnorm = grad_f * gate_f * gain[None, :]
    grad_att = rstd * (
        dnorm
        - jnp.mean(dnorm, axis=1, keepdims=True)
        - normed * jnp.mean(dnorm * normed, axis=1, keepdims=True)
    )
    grad_att = grad_att.astype(jnp.bfloat16)
    ga3 = grad_att.reshape(rows, H, head_size)
    grad_probs = jnp.einsum("thd,shd->hts", ga3, va3, preferred_element_type=jnp.float32)
    grad_scores = (grad_probs * weight[None] * silu_slope(scores)).astype(jnp.bfloat16)
    result = jnp.einsum("hts,shd->thd", grad_scores, ka3, preferred_element_type=jnp.float32)
    grad_q = (result * scale).reshape(rows, width).astype(jnp.bfloat16)
    query_list = [queries]
    grad_list = [grad_att[None]]
    for ahead in range(1, reach + 1):
        query_piece, grad_piece = shifted((queries, grad_att[None]), "seq", -ahead)
        query_list.append(query_piece)
        grad_list.append(grad_piece)
    query_block = jnp.concatenate(query_list, axis=1)
    grad_block = jnp.concatenate(grad_list, axis=1)
    count = query_block.shape[1]
    qp3 = query_block[0].reshape(count, H, head_size)
    gp3 = grad_block[0].reshape(count, H, head_size)
    row_pos, row_seg, row_inverse = piece_info(first, count)
    weight_piece = pair_weight(row_pos, row_seg, row_inverse, my_pos, my_seg)
    scores_piece = jnp.einsum("phd,khd->hpk", qp3, k3, preferred_element_type=jnp.float32) * scale
    probs_piece = (jax.nn.silu(scores_piece) * weight_piece[None]).astype(jnp.bfloat16)
    grad_probs = jnp.einsum("phd,khd->hpk", gp3, v3, preferred_element_type=jnp.float32)
    grad_scores = (grad_probs * weight_piece[None] * silu_slope(scores_piece)).astype(jnp.bfloat16)
    key_sum = jnp.einsum("hpk,phd->khd", grad_scores, qp3, preferred_element_type=jnp.float32)
    value_sum = jnp.einsum("hpk,phd->khd", probs_piece, gp3, preferred_element_type=jnp.float32)
    key_sum, value_sum = (key_sum, value_sum)
    grad_k = (key_sum * scale).reshape(rows, width).astype(jnp.bfloat16)
    grad_v = value_sum.reshape(rows, width).astype(jnp.bfloat16)
    grad_gain = lax.psum(gain_part, ("seq", "own"))
    return (output[None], grad_q[None], grad_k[None], grad_v[None], grad_gate[None], grad_gain)


def solution(mesh):
    in_specs = (
        P("own", "seq", None),
        P("own", "seq", None),
        P("own", "seq", None),
        P("own", "seq", None),
        P("own", None),
        P(),
        P("own", "seq", None),
    )
    out_specs = (
        P("own", "seq", None),
        P("own", "seq", None),
        P("own", "seq", None),
        P("own", "seq", None),
        P("own", "seq", None),
        P(),
    )
    return jax.shard_map(
        per_device, mesh=mesh, in_specs=in_specs, out_specs=out_specs, check_vma=False
    )
```

profile of v0, /device:TPU:24, one launch (start us, length us, event | category | flops | bytes accessed | tf_op | source)
XLA Modules:
  0.0 621.2 jit_solution(6832073720487988544)
XLA Ops:
  7.2 1.8 copy.92
  9.8 1.8 copy.108
  11.6 12.9 %collective-permute-start = (bf16[1,128,1024]{1,2,0:T(8,128)(2,1)}, bf16[1,128,1024]{1,2,0:T(8,128)(2,1)}, u32[]{:S(2)}, u32[]{:S(2)}) collective-permute-start(bf16[1,128,1024]{1,2,0:T(8,128)(2,1)} %copy.108), channel_id=1, source_target_pairs={{32,0},{64,32},{96,64},{128,96},{160,128},{192,160},{224,192},{256... | collective-permute-start | bytes 786440 | tf_op jit(solution)/shard_map/ppermute | solution.py:14
  24.5 4.9 collective-permute-start.1
  29.4 7.7 %collective-permute-start.2 = (bf16[1,128,1024]{1,2,0:T(8,128)(2,1)}, bf16[1,128,1024]{1,2,0:T(8,128)(2,1)}, u32[]{:S(2)}, u32[]{:S(2)}) collective-permute-start(bf16[1,128,1024]{1,2,0:T(8,128)(2,1)} %copy.108), channel_id=1, source_target_pairs={{96,0},{128,32},{160,64},{192,96},{224,128},{256,160},{288,192},{3... | collective-permute-start | bytes 786440 | tf_op jit(solution)/shard_map/ppermute | solution.py:14
  37.2 3.1 collective-permute-start.3
  40.2 2.0 collective-permute-start.4
  42.2 0.8 reduce-window.8
  44.9 2.1 and_select_fusion
  47.0 1.5 fusion.14
  48.5 1.0 constant_dynamic-update-slice_fusion.8
  49.5 1.1 copy.97
  50.6 1.1 copy.96
  51.8 1.7 copy.137
  53.5 1.7 copy.136
  55.2 39.3 %collective-permute-done = bf16[1,128,1024]{1,2,0:T(8,128)(2,1)} collective-permute-done((bf16[1,128,1024]{1,2,0:T(8,128)(2,1)}, bf16[1,128,1024]{1,2,0:T(8,128)(2,1)}, u32[]{:S(2)}, u32[]{:S(2)}) %collective-permute-start) | collective-permute-done | bytes 262176 | tf_op jit(solution)/shard_map/ppermute | solution.py:14
  94.5 8.2 %collective-permute-start.5 = (bf16[1,128,1024]{1,2,0:T(8,128)(2,1)}, bf16[1,128,1024]{1,2,0:T(8,128)(2,1)S(1)}, u32[]{:S(2)}, u32[]{:S(2)}) collective-permute-start(bf16[1,128,1024]{1,2,0:T(8,128)(2,1)} %copy.108), channel_id=1, source_target_pairs={{192,0},{224,32},{256,64},{288,96},{320,128},{352,160},{384,192},{... | collective-permute-start | bytes 786440 | tf_op jit(solution)/shard_map/ppermute | solution.py:14
  102.7 1.0 constant_dynamic-update-slice_fusion.7
  103.8 1.3 collective-permute-start.6
  105.1 1.0 constant_dynamic-update-slice_fusion.6
  106.1 1.3 collective-permute-start.7
  107.4 1.0 constant_dynamic-update-slice_fusion.5
  108.4 1.0 constant_dynamic-update-slice_fusion.4
  109.5 22.2 %collective-permute-done.4 = bf16[1,128,1024]{1,2,0:T(8,128)(2,1)} collective-permute-done((bf16[1,128,1024]{1,2,0:T(8,128)(2,1)}, bf16[1,128,1024]{1,2,0:T(8,128)(2,1)}, u32[]{:S(2)}, u32[]{:S(2)}) %collective-permute-start.4) | collective-permute-done | bytes 262176 | tf_op jit(solution)/shard_map/ppermute | solution.py:14
  131.7 1.0 constant_dynamic-update-slice_fusion.3
  132.9 95.1 %all-gather.3.cloned.1.call-done = bf16[1,2048,1024]{1,2,0:T(8,128)(2,1)} async-done(((bf16[1,128,1024]{1,2,0:T(8,128)(2,1)}), bf16[1,2048,1024]{1,2,0:T(8,128)(2,1)}) %all-gather.3.cloned.1.call-update) | async-done | bytes 4194320 | tf_op jit(solution)/shard_map/all_gather | solution.py:57
  228.0 6.6 %fusion.25 = f32[8,128,2048]{2,1,0:T(8,128)} fusion(bf16[2048,8,128]{0,2,1:T(8,128)(2,1)} %bitcast.81, bf16[128,8,128]{2,1,0:T(8,128)(2,1)S(1)} %bitcast.88), kind=kOutput, calls=%fused_computation.45 | convolution fusion | flops 536870912 | bytes 12845056 | tf_op jit(solution)/shard_map/thd,shd->hts/dot_general | solution.py:65
  234.6 125.4 %all-gather.5.cloned.1.call-done = bf16[1,2048,1024]{2,1,0:T(8,128)(2,1)} async-done(((bf16[1,128,1024]{2,1,0:T(8,128)(2,1)}), bf16[1,2048,1024]{2,1,0:T(8,128)(2,1)}) %all-gather.5.cloned.1.call-update) | async-done | bytes 4194320 | tf_op jit(solution)/shard_map/all_gather | solution.py:58
  360.1 6.5 %copy.95 = bf16[1,2048,1024]{1,2,0:T(8,128)(2,1)} copy(bf16[1,2048,1024]{2,1,0:T(8,128)(2,1)} %all-gather.5.cloned.1.call-done) | data formatting | bytes 8388608 | tf_op jit(solution)/shard_map/all_gather | solution.py:58
  366.6 8.0 %fusion.43 = (f32[128]{0:T(128)S(1)}, f32[8,128,128]{1,2,0:T(8,128)S(1)}) fusion(bf16[2048,8,128]{0,2,1:T(8,128)(2,1)} %bitcast.84, f32[8,128,2048]{2,1,0:T(8,128)} %fusion.25, f32[128,2048]{1,0:T(8,128)} %fusion.14), kind=kOutput, calls=%fused_computation.94 | convolution fusion | flops 551681920 | bytes 14156288 | tf_op jit(solution)/shard_map/hts,shd->thd/dot_general | solution.py:67
  375.2 1.4 fusion.17
  376.5 4.6 collective-permute-start.8
  381.1 7.7 %collective-permute-start.9 = (bf16[1,128,1024]{1,2,0:T(8,128)(2,1)}, bf16[1,128,1024]{1,2,0:T(8,128)(2,1)S(1)}, u32[]{:S(2)}, u32[]{:S(2)}) collective-permute-start(bf16[1,128,1024]{1,2,0:T(8,128)(2,1)} %get-tuple-element.34), channel_id=1, source_target_pairs={{64,0},{96,32},{128,64},{160,96},{192,128},{224,160},{256,192},{28... | collective-permute-start | bytes 786440 | tf_op jit(solution)/shard_map/ppermute | solution.py:14
  388.9 5.9 collective-permute-start.10
  394.8 3.0 convolution_multiply_fusion
  397.9 2.4 collective-permute-start.11
  400.3 4.3 collective-permute-start.12
  405.0 3.9 collective-permute-start.13
  408.9 22.8 %collective-permute-done.9 = bf16[1,128,1024]{1,2,0:T(8,128)(2,1)S(1)} collective-permute-done((bf16[1,128,1024]{1,2,0:T(8,128)(2,1)}, bf16[1,128,1024]{1,2,0:T(8,128)(2,1)S(1)}, u32[]{:S(2)}, u32[]{:S(2)}) %collective-permute-start.9) | collective-permute-done | bytes 262176 | tf_op jit(solution)/shard_map/ppermute | solution.py:14
  431.7 2.0 collective-permute-start.14
  434.4 12.8 %collective-permute-start.15 = (bf16[1,128,1024]{1,2,0:T(8,128)(2,1)}, bf16[1,128,1024]{1,2,0:T(8,128)(2,1)}, u32[]{:S(2)}, u32[]{:S(2)}) collective-permute-start(bf16[1,128,1024]{1,2,0:T(8,128)(2,1)} %get-tuple-element.34), channel_id=1, source_target_pairs={{256,0},{288,32},{320,64},{352,96},{384,128},{416,160},{448,192},{... | collective-permute-start | bytes 786440 | tf_op jit(solution)/shard_map/ppermute | solution.py:14
  447.2 12.1 %fusion.8 = bf16[8,128,128]{1,2,0:T(8,128)(2,1)} fusion(bf16[2048,8,128]{0,2,1:T(8,128)(2,1)} %bitcast.82, f32[8,128,2048]{2,1,0:T(8,128)} %fusion.25, bf16[2048,8,128]{0,2,1:T(8,128)(2,1)} %bitcast.85, f32[128,2048]{1,0:T(8,128)} %fusion.14, f32[128,8,128]{0,2,1:T(8,128)} %bitcast.94, f32[8,128,128]{1,2,0:T(8,128)S(1)} %get-tuple-element.38, ...), kind=kOutput, calls=%fused_computation.15 | convolution fusion | flops 1098121216 | bytes 19142656 | tf_op jit(solution)/shard_map/hts,shd->thd/dot_general | solution.py:87
  459.3 0.8 copy.124
  460.2 1.8 copy.125
  462.0 1.1 copy.109
  463.1 0.9 copy.128
  464.0 113.9 %psum.7 = f32[1024]{0:T(1024)} all-reduce(f32[1024]{0:T(1024)S(1)} %get-tuple-element.30), channel_id=1, replica_groups=mesh['seq'=16,'own'=32] {'seq','own'}, use_global_device_ids=true, to_apply=%region_11.12 | all-reduce | flops 1024 | bytes 8192 | tf_op jit(solution)/shard_map/psum | solution.py:111
  578.6 1.1 copy.110
  579.7 1.1 copy.111
  580.8 1.1 copy.112
  582.0 1.1 copy.113
  583.1 1.8 copy.114
  584.9 1.8 copy.115
  586.7 1.8 copy.116
  588.5 1.8 copy.117
  593.3 1.7 constant_dynamic-update-slice_fusion.12
  595.0 1.7 constant_dynamic-update-slice_fusion.11
  596.7 1.7 constant_dynamic-update-slice_fusion.10
  598.4 1.7 constant_dynamic-update-slice_fusion.9
  600.1 5.1 fusion.10
  605.2 6.3 %fusion.11 = bf16[128,8,128]{2,0,1:T(8,128)(2,1)} fusion(bf16[1152,8,128]{0,2,1:T(8,128)(2,1)S(1)} %bitcast.87, f32[8,1152,128]{2,1,0:T(8,128)} %convolution_multiply_fusion, bf16[1152,8,128]{2,0,1:T(8,128)(2,1)} %constant_dynamic-update-slice_fusion.9, f32[1152,128]{1,0:T(8,128)S(1)} %copy-done.5, bf16[128,8,128]{2,1,0:T(8,128)(2,1)S(1)} %bitcast.95), kind=kOutput, calls=%fused_computation.18 | convolution fusion | flops 616038400 | bytes 10551296 | tf_op jit(solution)/shard_map/hpk,phd->khd/dot_general | solution.py:106
  611.5 1.1 copy.122
  612.6 0.9 copy.126
  613.5 0.8 copy.127
  (64 shorter events, 8.2 us)
Async XLA Ops:
  7.2 43.4 %copy-start.1 = (bf16[1,128,1024]{2,1,0:T(8,128)(2,1)S(1)}, bf16[1,128,1024]{2,1,0:T(8,128)(2,1)}, u32[]{:S(2)}) copy-start(bf16[1,128,1024]{2,1,0:T(8,128)(2,1)} %param.7) | copy-start | bytes 786436
  7.2 220.8 %all-gather.3.cloned.1.call-start = ((), (), s32[]{:S(2)}) async-start(), calls=%async_computation | async-start | bytes 4456448 | tf_op jit(solution)/shard_map/all_gather | solution.py:57
  9.1 351.0 %all-gather.5.cloned.1.call-start = ((), (), s32[]{:S(2)}) async-start(), calls=%async_computation.1 | async-start | bytes 4456448 | tf_op jit(solution)/shard_map/all_gather | solution.py:58
  11.6 82.9 %collective-permute-start = (bf16[1,128,1024]{1,2,0:T(8,128)(2,1)}, bf16[1,128,1024]{1,2,0:T(8,128)(2,1)}, u32[]{:S(2)}, u32[]{:S(2)}) collective-permute-start(bf16[1,128,1024]{1,2,0:T(8,128)(2,1)} %copy.108), channel_id=1, source_target_pairs={{32,0},{64,32},{96,64},{128,96},{160,128},{192,160},{224,192},{256... | collective-permute-start | bytes 786440 | tf_op jit(solution)/shard_map/ppermute | solution.py:14
  24.5 79.2 %collective-permute-start.1 = (bf16[1,128,1024]{1,2,0:T(8,128)(2,1)}, bf16[1,128,1024]{1,2,0:T(8,128)(2,1)}, u32[]{:S(2)}, u32[]{:S(2)}) collective-permute-start(bf16[1,128,1024]{1,2,0:T(8,128)(2,1)} %copy.108), channel_id=1, source_target_pairs={{64,0},{96,32},{128,64},{160,96},{192,128},{224,160},{256,192},{28... | collective-permute-start | bytes 786440 | tf_op jit(solution)/shard_map/ppermute | solution.py:14
  29.4 76.6 %collective-permute-start.2 = (bf16[1,128,1024]{1,2,0:T(8,128)(2,1)}, bf16[1,128,1024]{1,2,0:T(8,128)(2,1)}, u32[]{:S(2)}, u32[]{:S(2)}) collective-permute-start(bf16[1,128,1024]{1,2,0:T(8,128)(2,1)} %copy.108), channel_id=1, source_target_pairs={{96,0},{128,32},{160,64},{192,96},{224,128},{256,160},{288,192},{3... | collective-permute-start | bytes 786440 | tf_op jit(solution)/shard_map/ppermute | solution.py:14
  37.2 71.3 %collective-permute-start.3 = (bf16[1,128,1024]{1,2,0:T(8,128)(2,1)}, bf16[1,128,1024]{1,2,0:T(8,128)(2,1)}, u32[]{:S(2)}, u32[]{:S(2)}) collective-permute-start(bf16[1,128,1024]{1,2,0:T(8,128)(2,1)} %copy.108), channel_id=1, source_target_pairs={{128,0},{160,32},{192,64},{224,96},{256,128},{288,160},{320,192},{... | collective-permute-start | bytes 786440 | tf_op jit(solution)/shard_map/ppermute | solution.py:14
  40.2 91.4 %collective-permute-start.4 = (bf16[1,128,1024]{1,2,0:T(8,128)(2,1)}, bf16[1,128,1024]{1,2,0:T(8,128)(2,1)}, u32[]{:S(2)}, u32[]{:S(2)}) collective-permute-start(bf16[1,128,1024]{1,2,0:T(8,128)(2,1)} %copy.108), channel_id=1, source_target_pairs={{160,0},{192,32},{224,64},{256,96},{288,128},{320,160},{352,192},{... | collective-permute-start | bytes 786440 | tf_op jit(solution)/shard_map/ppermute | solution.py:14
  94.5 38.2 %collective-permute-start.5 = (bf16[1,128,1024]{1,2,0:T(8,128)(2,1)}, bf16[1,128,1024]{1,2,0:T(8,128)(2,1)S(1)}, u32[]{:S(2)}, u32[]{:S(2)}) collective-permute-start(bf16[1,128,1024]{1,2,0:T(8,128)(2,1)} %copy.108), channel_id=1, source_target_pairs={{192,0},{224,32},{256,64},{288,96},{320,128},{352,160},{384,192},{... | collective-permute-start | bytes 786440 | tf_op jit(solution)/shard_map/ppermute | solution.py:14
  103.8 29.0 %collective-permute-start.6 = (bf16[1,128,1024]{1,2,0:T(8,128)(2,1)}, bf16[1,128,1024]{1,2,0:T(8,128)(2,1)S(1)}, u32[]{:S(2)}, u32[]{:S(2)}) collective-permute-start(bf16[1,128,1024]{1,2,0:T(8,128)(2,1)} %copy.108), channel_id=1, source_target_pairs={{224,0},{256,32},{288,64},{320,96},{352,128},{384,160},{416,192},{... | collective-permute-start | bytes 786440 | tf_op jit(solution)/shard_map/ppermute | solution.py:14
  106.1 26.7 %collective-permute-start.7 = (bf16[1,128,1024]{1,2,0:T(8,128)(2,1)}, bf16[1,128,1024]{1,2,0:T(8,128)(2,1)S(1)}, u32[]{:S(2)}, u32[]{:S(2)}) collective-permute-start(bf16[1,128,1024]{1,2,0:T(8,128)(2,1)} %copy.108), channel_id=1, source_target_pairs={{256,0},{288,32},{320,64},{352,96},{384,128},{416,160},{448,192},{... | collective-permute-start | bytes 786440 | tf_op jit(solution)/shard_map/ppermute | solution.py:14
  366.6 8.2 %copy-start.10 = (f32[1024]{0:T(1024)S(1)}, f32[1024]{0:T(1024)}, u32[]{:S(2)}) copy-start(f32[1024]{0:T(1024)} %param.12) | copy-start | bytes 12292
  366.6 28.2 %copy-start = (bf16[16,8,8,128]{3,2,1,0:T(8,128)(2,1)S(1)}, bf16[16,8,8,128]{3,2,1,0:T(8,128)(2,1)}, u32[]{:S(2)}) copy-start(bf16[16,8,8,128]{3,2,1,0:T(8,128)(2,1)} %copy.137) | copy-start | bytes 786436
  376.5 28.4 %collective-permute-start.8 = (bf16[1,128,1024]{1,2,0:T(8,128)(2,1)}, bf16[1,128,1024]{1,2,0:T(8,128)(2,1)S(1)}, u32[]{:S(2)}, u32[]{:S(2)}) collective-permute-start(bf16[1,128,1024]{1,2,0:T(8,128)(2,1)} %get-tuple-element.34), channel_id=1, source_target_pairs={{32,0},{64,32},{96,64},{128,96},{160,128},{192,160},{224,192},{256... | collective-permute-start | bytes 786440 | tf_op jit(solution)/shard_map/ppermute | solution.py:14
  381.1 50.6 %collective-permute-start.9 = (bf16[1,128,1024]{1,2,0:T(8,128)(2,1)}, bf16[1,128,1024]{1,2,0:T(8,128)(2,1)S(1)}, u32[]{:S(2)}, u32[]{:S(2)}) collective-permute-start(bf16[1,128,1024]{1,2,0:T(8,128)(2,1)} %get-tuple-element.34), channel_id=1, source_target_pairs={{64,0},{96,32},{128,64},{160,96},{192,128},{224,160},{256,192},{28... | collective-permute-start | bytes 786440 | tf_op jit(solution)/shard_map/ppermute | solution.py:14
  388.9 45.5 %collective-permute-start.10 = (bf16[1,128,1024]{1,2,0:T(8,128)(2,1)}, bf16[1,128,1024]{1,2,0:T(8,128)(2,1)S(1)}, u32[]{:S(2)}, u32[]{:S(2)}) collective-permute-start(bf16[1,128,1024]{1,2,0:T(8,128)(2,1)} %get-tuple-element.34), channel_id=1, source_target_pairs={{96,0},{128,32},{160,64},{192,96},{224,128},{256,160},{288,192},{3... | collective-permute-start | bytes 786440 | tf_op jit(solution)/shard_map/ppermute | solution.py:14
  397.9 184.1 %collective-permute-start.11 = (bf16[1,128,1024]{1,2,0:T(8,128)(2,1)}, bf16[1,128,1024]{1,2,0:T(8,128)(2,1)}, u32[]{:S(2)}, u32[]{:S(2)}) collective-permute-start(bf16[1,128,1024]{1,2,0:T(8,128)(2,1)} %get-tuple-element.34), channel_id=1, source_target_pairs={{128,0},{160,32},{192,64},{224,96},{256,128},{288,160},{320,192},{... | collective-permute-start | bytes 786440 | tf_op jit(solution)/shard_map/ppermute | solution.py:14
  400.3 182.8 %collective-permute-start.12 = (bf16[1,128,1024]{1,2,0:T(8,128)(2,1)}, bf16[1,128,1024]{1,2,0:T(8,128)(2,1)}, u32[]{:S(2)}, u32[]{:S(2)}) collective-permute-start(bf16[1,128,1024]{1,2,0:T(8,128)(2,1)} %get-tuple-element.34), channel_id=1, source_target_pairs={{160,0},{192,32},{224,64},{256,96},{288,128},{320,160},{352,192},{... | collective-permute-start | bytes 786440 | tf_op jit(solution)/shard_map/ppermute | solution.py:14
  405.0 42.3 %copy-start.7 = (bf16[1,128,1024]{1,2,0:T(8,128)(2,1)}, bf16[1,128,1024]{1,2,0:T(8,128)(2,1)S(1)}, u32[]{:S(2)}) copy-start(bf16[1,128,1024]{1,2,0:T(8,128)(2,1)S(1)} %collective-permute-done.8) | copy-start | bytes 786436
  405.0 180.0 %collective-permute-start.13 = (bf16[1,128,1024]{1,2,0:T(8,128)(2,1)}, bf16[1,128,1024]{1,2,0:T(8,128)(2,1)}, u32[]{:S(2)}, u32[]{:S(2)}) collective-permute-start(bf16[1,128,1024]{1,2,0:T(8,128)(2,1)} %get-tuple-element.34), channel_id=1, source_target_pairs={{192,0},{224,32},{256,64},{288,96},{320,128},{352,160},{384,192},{... | collective-permute-start | bytes 786440 | tf_op jit(solution)/shard_map/ppermute | solution.py:14
  431.7 15.5 %copy-start.8 = (bf16[1,128,1024]{1,2,0:T(8,128)(2,1)}, bf16[1,128,1024]{1,2,0:T(8,128)(2,1)S(1)}, u32[]{:S(2)}) copy-start(bf16[1,128,1024]{1,2,0:T(8,128)(2,1)S(1)} %collective-permute-done.9) | copy-start | bytes 786436
  431.7 155.0 %collective-permute-start.14 = (bf16[1,128,1024]{1,2,0:T(8,128)(2,1)}, bf16[1,128,1024]{1,2,0:T(8,128)(2,1)}, u32[]{:S(2)}, u32[]{:S(2)}) collective-permute-start(bf16[1,128,1024]{1,2,0:T(8,128)(2,1)} %get-tuple-element.34), channel_id=1, source_target_pairs={{224,0},{256,32},{288,64},{320,96},{352,128},{384,160},{416,192},{... | collective-permute-start | bytes 786440 | tf_op jit(solution)/shard_map/ppermute | solution.py:14
  434.4 12.8 %copy-start.9 = (bf16[1,128,1024]{1,2,0:T(8,128)(2,1)}, bf16[1,128,1024]{1,2,0:T(8,128)(2,1)S(1)}, u32[]{:S(2)}) copy-start(bf16[1,128,1024]{1,2,0:T(8,128)(2,1)S(1)} %collective-permute-done.10) | copy-start | bytes 786436
  434.4 154.1 %collective-permute-start.15 = (bf16[1,128,1024]{1,2,0:T(8,128)(2,1)}, bf16[1,128,1024]{1,2,0:T(8,128)(2,1)}, u32[]{:S(2)}, u32[]{:S(2)}) collective-permute-start(bf16[1,128,1024]{1,2,0:T(8,128)(2,1)} %get-tuple-element.34), channel_id=1, source_target_pairs={{256,0},{288,32},{320,64},{352,96},{384,128},{416,160},{448,192},{... | collective-permute-start | bytes 786440 | tf_op jit(solution)/shard_map/ppermute | solution.py:14
  447.2 12.1 %copy-start.3 = (bf16[1,128,1024]{1,2,0:T(8,128)(2,1)S(1)}, bf16[1,128,1024]{1,2,0:T(8,128)(2,1)}, u32[]{:S(2)}) copy-start(bf16[1,128,1024]{1,2,0:T(8,128)(2,1)} %get-tuple-element.35) | copy-start | bytes 786436
  447.2 15.9 %copy-start.2 = (bf16[1,128,1024]{1,2,0:T(8,128)(2,1)S(1)}, bf16[1,128,1024]{1,2,0:T(8,128)(2,1)}, u32[]{:S(2)}) copy-start(bf16[1,128,1024]{1,2,0:T(8,128)(2,1)} %get-tuple-element.33) | copy-start | bytes 786436
  590.3 9.8 %copy-start.4 = (f32[1152,128]{1,0:T(8,128)S(1)}, f32[1152,128]{1,0:T(8,128)}, u32[]{:S(2)}) copy-start(f32[1152,128]{1,0:T(8,128)} %and_select_fusion) | copy-start | bytes 1769476
  600.1 5.1 copy-start.5
  600.1 5.1 copy-start.6
Sparse Core Ops, SparseCore 0:
  11.6 216.3 all-gather.2
  231.0 129.0 all-gather.4
where the time goes:
time: 625 us; the launch traced here: 621 us
  waiting for transfers between devices  307 us (49%)
  blocking collectives  114 us (18%)
  starting transfers between devices  85.2 us (14%)
  local copies, waits for them, and re-layouts  51.7 us (8%)
  matrix products  41.2 us (7%)
  between operations  14.4 us (2%)
  other arithmetic  8.14 us (1%)
    all_gather x1, waiting for transfers between devices, per_device(): lax.all_gather(values, 'seq', axis=1, tiled=True)  125 us
    psum x1, blocking collectives, per_device(): grad_gain = lax.psum(gain_part, ('seq', 'own'))  114 us
    all_gather x1, waiting for transfers between devices, per_device(): lax.all_gather(keys, 'seq', axis=1, tiled=True)  95.1 us
    ppermute x16, waiting for transfers between devices, shifted(): return lax.ppermute(array, axis, pairs)  85.5 us
    ppermute x16, starting transfers between devices, shifted(): return lax.ppermute(array, axis, pairs)  85.1 us
    unnamed x50, local copies, waits for them, and re-layouts  29.6 us
    concatenate x10, local copies, waits for them, and re-layouts, per_device(): grad_block = jnp.concatenate(grad_list, axis=1)  14.5 us
  transfers between devices with their start and end apart: 18, of which 7 were waited for; matrix products, arithmetic and copies ran while one was open for 9% of the time, Pallas kernels for 0%

commit v1 on v0

v1 whole, which is shorter than its diff:
```python
import math

import jax
import jax.numpy as jnp
from jax import lax
from jax.experimental import pallas as pl
from jax.experimental.pallas import tpu as pltpu
from jax.sharding import PartitionSpec as P


H = 8
HALF = 64
HEAD = 128
TILE = 4
EXTRA = 16
F32 = jnp.float32
BF16 = jnp.bfloat16
VMEM_LIMIT = 48 * 1024 * 1024


def head_half(device):
    y, z = divmod(device, 4)
    return 2 * z + y // 2, y % 2


def dot(a, b, dims):
    return lax.dot_general(a, b, (dims, ((), ())), preferred_element_type=F32)


def iota(shape, dim):
    return lax.broadcasted_iota(jnp.int32, shape, dim)


def offsets(shape, dim):
    index = iota(shape, dim)
    return (index // HALF) * (2 * HALF) + index % HALF


def bounds(pos, info):
    start = jnp.zeros_like(pos)
    end = jnp.full_like(pos, 1 << 30)
    for user in range(info.shape[0] - 1):
        edge = info[1 + user]
        start = jnp.where(pos >= edge, jnp.maximum(start, edge), start)
        end = jnp.where(pos < edge, jnp.minimum(end, edge), end)
    return start, end - start


def tile_rows(ref, tile, first, last):
    block = ref[pl.ds(tile * TILE, TILE), first:last, :]
    return block.reshape(TILE * HALF, HEAD)


def first_key_tile(tile, info):
    start, _ = bounds(tile * (TILE * 2 * HALF) + info[0] * HALF, info)
    return start // (TILE * 2 * HALF)


def spread(column):
    square = iota((HALF, HEAD), 0) == iota((HALF, HEAD), 1)
    return jnp.sum(jnp.where(square, column, 0.0), axis=0, keepdims=True)


def gather_column(row):
    square = iota((HALF, HEAD), 0) == iota((HALF, HEAD), 1)
    return jnp.sum(jnp.where(square, row, 0.0), axis=1, keepdims=True)


def in_three(row):
    high = row.astype(BF16).astype(F32)
    mid = (row - high).astype(BF16).astype(F32)
    low = row - high - mid
    index = iota((EXTRA, HEAD), 0)
    block = jnp.where(index == 0, high, jnp.where(index == 1, mid, jnp.where(index == 2, low, 0.0)))
    return block.astype(BF16)


def pack_kernel(q_ref, k_ref, v_ref, out_ref):
    for device in range(out_ref.shape[0]):
        head, half = head_half(device)
        for part, ref in enumerate((q_ref, k_ref, v_ref)):
            out_ref[device, part * HALF : (part + 1) * HALF, :] = ref[
                half * HALF : (half + 1) * HALF, head * HEAD : (head + 1) * HEAD
            ]


def forward_tile(info, q_ref, kv_ref, kv_first, kv_half, tile, total):
    scale = 0.5 / math.sqrt(HEAD)
    span = TILE * 2 * HALF
    rows = TILE * HALF
    q = tile_rows(q_ref, tile, 0, HALF)
    pos = tile * span + info[0] * HALF + offsets((rows, 1), 0)
    start, _ = bounds(pos, info)
    where = offsets((1, rows), 1)

    def step(key_tile, total):
        k = tile_rows(kv_ref, key_tile, kv_first, kv_first + HALF)
        v = tile_rows(kv_ref, key_tile, kv_first + HALF, kv_first + 2 * HALF)
        base = key_tile * span + kv_half * HALF
        half_score = dot(q, k, ((1,), (1,))) * scale
        silu = half_score + half_score * jnp.tanh(half_score)
        allowed = (where >= start - base) & (where <= pos - base)
        probs = jnp.where(allowed, silu, 0.0).astype(BF16)
        return total + dot(probs, v, ((1,), (0,)))

    return lax.fori_loop(first_key_tile(tile, info), tile + 1, step, total)


def forward_own_kernel(info, mine_ref, sum_ref):
    rows = TILE * HALF
    for tile in range(mine_ref.shape[0] // TILE):
        total = jnp.zeros((rows, HEAD), F32)
        total = forward_tile(info, mine_ref, mine_ref, HALF, info[0], tile, total)
        sum_ref[tile * rows : (tile + 1) * rows, :] = total


def forward_other_kernel(info, mine_ref, other_ref, sum_ref, out_ref):
    rows = TILE * HALF
    for tile in range(mine_ref.shape[0] // TILE):
        total = sum_ref[tile * rows : (tile + 1) * rows, :]
        total = forward_tile(info, mine_ref, other_ref, 0, 1 - info[0], tile, total)
        pos = tile * TILE * 2 * HALF + info[0] * HALF + offsets((rows, 1), 0)
        _, length = bounds(pos, info)
        attended = total * (1.0 / length.astype(F32))
        mean = jnp.mean(attended, axis=1, keepdims=True).astype(BF16).astype(F32)
        rest = (attended - mean).astype(BF16)
        for part in range(TILE):
            span = slice(part * HALF, (part + 1) * HALF)
            slot = tile * TILE + part
            out_ref[slot, 0:HALF, :] = rest[span]
            out_ref[slot, HALF : HALF + EXTRA, :] = jnp.broadcast_to(
                spread(mean[span]), (EXTRA, HEAD)
            ).astype(BF16)


def norm_kernel(info, att_ref, gates_ref, grad_ref, gain_ref, out_ref, gate_grad_ref, att_grad_ref):
    width = H * HEAD
    devices = {head_half(device): device for device in range(att_ref.shape[0])}
    gain_sums = [jnp.zeros((1, HEAD), F32) for _ in range(H)]
    for half in range(2):
        span = slice(half * HALF, (half + 1) * HALF)
        attended = []
        for head in range(H):
            device = devices[head, half]
            mean = gather_column(att_ref[device, HALF : HALF + 1, :].astype(F32))
            attended.append(att_ref[device, 0:HALF, :].astype(F32) + mean)
        mean = jnp.sum(sum(attended), axis=1, keepdims=True) / width
        center = [block - mean for block in attended]
        var = jnp.sum(sum(block * block for block in center), axis=1, keepdims=True) / width
        rstd = lax.rsqrt(var + 1e-05)
        normed = [block * rstd for block in center]
        dnorm = []
        for head in range(H):
            cols = slice(head * HEAD, (head + 1) * HEAD)
            gain = gain_ref[0:1, cols]
            gate = gates_ref[span, cols].astype(F32)
            grad = grad_ref[span, cols].astype(F32)
            out_ref[span, cols] = (normed[head] * gain * gate).astype(BF16)
            gate_grad_ref[span, cols] = (grad * normed[head] * gain).astype(BF16)
            both = grad * gate
            gain_sums[head] = gain_sums[head] + jnp.sum(both * normed[head], axis=0, keepdims=True)
            dnorm.append(both * gain)
        first = jnp.sum(sum(dnorm), axis=1, keepdims=True) / width
        second = jnp.sum(sum(d * n for d, n in zip(dnorm, normed)), axis=1, keepdims=True) / width
        pos = info[info.shape[0] - 1] + half * HALF + iota((HALF, 1), 0)
        _, length = bounds(pos, info.at[0 : info.shape[0] - 1])
        factor = rstd * (1.0 / length.astype(F32))
        for head in range(H):
            grad_att = factor * (dnorm[head] - first - normed[head] * second)
            att_grad_ref[devices[head, half], 0:HALF, :] = grad_att.astype(BF16)
    for device in range(att_ref.shape[0]):
        att_grad_ref[device, HALF : HALF + EXTRA, :] = in_three(gain_sums[device // 2])


def backward_tiles(info, mine_ref, kv_ref, kv_first, kv_half, grad_ref, dq_ref, dk_ref, dv_ref):
    scale = 0.5 / math.sqrt(HEAD)
    span = TILE * 2 * HALF
    rows = TILE * HALF
    dk_ref[...] = jnp.zeros_like(dk_ref)
    dv_ref[...] = jnp.zeros_like(dv_ref)
    where = offsets((rows, 1), 0)
    for tile in range(mine_ref.shape[0] // TILE):
        q = tile_rows(mine_ref, tile, 0, HALF)
        grad = tile_rows(grad_ref, tile, 0, HALF)
        pos = tile * span + info[0] * HALF + offsets((1, rows), 1)
        start, _ = bounds(pos, info)

        def step(key_tile, total):
            k = tile_rows(kv_ref, key_tile, kv_first, kv_first + HALF)
            v = tile_rows(kv_ref, key_tile, kv_first + HALF, kv_first + 2 * HALF)
            base = key_tile * span + kv_half * HALF
            half_score = dot(k, q, ((1,), (1,))) * scale
            grad_probs = dot(v, grad, ((1,), (1,)))
            tanh = jnp.tanh(half_score)
            twice = 1.0 + tanh
            allowed = (where >= start - base) & (where <= pos - base)
            probs = jnp.where(allowed, half_score * twice, 0.0).astype(BF16)
            slope = twice * (1.0 + half_score * (1.0 - tanh))
            grad_scores = jnp.where(allowed, grad_probs * slope, 0.0).astype(BF16)
            here = pl.ds(pl.multiple_of(key_tile * rows, rows), rows)
            dv_ref[here, :] += dot(probs, grad, ((1,), (0,)))
            dk_ref[here, :] += dot(grad_scores, q, ((1,), (0,)))
            return total + dot(grad_scores, k, ((0,), (0,)))

        here = slice(tile * rows, (tile + 1) * rows)
        dq_ref[here, :] = lax.fori_loop(first_key_tile(tile, info), tile + 1, step, dq_ref[here, :])


def backward_other_kernel(info, mine_ref, other_ref, grad_ref, dq_ref, send_ref, gain_ref, dk_ref, dv_ref):
    dq_ref[...] = jnp.zeros_like(dq_ref)
    backward_tiles(info, mine_ref, other_ref, 0, 1 - info[0], grad_ref, dq_ref, dk_ref, dv_ref)
    send_ref[0] = (dk_ref[...] * (0.5 / math.sqrt(HEAD))).astype(BF16)
    send_ref[1] = dv_ref[...].astype(BF16)
    gain = jnp.zeros((EXTRA, HEAD), F32)
    for device in range(grad_ref.shape[0]):
        gain = gain + grad_ref[device, HALF : HALF + EXTRA, :].astype(F32)
    gain = jnp.sum(gain, axis=0, keepdims=True)
    gain_ref[...] = jnp.broadcast_to(gain[None], gain_ref.shape)


def backward_own_kernel(info, mine_ref, grad_ref, dq_in_ref, dq_ref, dk_ref, dv_ref):
    dq_ref[...] = dq_in_ref[...]
    backward_tiles(info, mine_ref, mine_ref, HALF, info[0], grad_ref, dq_ref, dk_ref, dv_ref)


def join_kernel(dq_ref, dk_ref, dv_ref, other_ref, gain_ref, out_ref):
    scale = 0.5 / math.sqrt(HEAD)
    gain = jnp.zeros(gain_ref.shape[1:], F32)
    for device in range(gain_ref.shape[0]):
        gain = gain + gain_ref[device]
    gain = in_three(gain[0:1])
    for slot in range(out_ref.shape[0]):
        here = slice(slot * HALF, (slot + 1) * HALF)
        out_ref[slot, 0:HALF, :] = (dq_ref[here, :] * scale).astype(BF16)
        dk = dk_ref[here, :] * scale + other_ref[0, here, :].astype(F32)
        out_ref[slot, HALF : 2 * HALF, :] = dk.astype(BF16)
        dv = dv_ref[here, :] + other_ref[1, here, :].astype(F32)
        out_ref[slot, 2 * HALF : 3 * HALF, :] = dv.astype(BF16)
        out_ref[slot, 3 * HALF : 3 * HALF + EXTRA, :] = gain


def unpack_kernel(in_ref, dq_ref, dk_ref, dv_ref, gain_ref):
    for device in range(in_ref.shape[0]):
        head, half = head_half(device)
        for part, ref in enumerate((dq_ref, dk_ref, dv_ref)):
            ref[half * HALF : (half + 1) * HALF, head * HEAD : (head + 1) * HEAD] = in_ref[
                device, part * HALF : (part + 1) * HALF, :
            ]
    for head in range(H):
        block = in_ref[2 * head, 3 * HALF : 3 * HALF + EXTRA, :].astype(F32)
        gain_ref[0:1, head * HEAD : (head + 1) * HEAD] = jnp.sum(block, axis=0, keepdims=True)


def call(kernel, outs, *args, scalars=0, scratch=(), flops=0):
    specs = [pl.BlockSpec(memory_space=pltpu.SMEM)] * scalars
    specs += [pl.BlockSpec(memory_space=pltpu.VMEM)] * (len(args) - scalars)
    moved = sum(math.prod(x.shape) * x.dtype.itemsize for x in list(args) + list(outs))
    return pl.pallas_call(
        kernel,
        out_shape=outs,
        in_specs=specs,
        out_specs=[pl.BlockSpec(memory_space=pltpu.VMEM)] * len(outs),
        scratch_shapes=scratch,
        compiler_params=pltpu.CompilerParams(vmem_limit_bytes=VMEM_LIMIT),
        cost_estimate=pl.CostEstimate(flops=flops, bytes_accessed=moved, transcendentals=flops // 512),
    )(*args)


def exchange(array, axis):
    return lax.all_to_all(array, axis, 0, 0, tiled=True)


def per_device(queries, keys, values, gates, lengths, gain, grad_out):
    rows, width = queries.shape[1:]
    devices = lax.axis_size("seq")
    groups = lax.axis_size("own")
    local = devices * HALF
    shape = jax.ShapeDtypeStruct
    me = lax.axis_index("seq")
    ends = jnp.cumsum(lengths[0])
    my_half = (me // 4) % 2
    info = jnp.concatenate([jnp.stack([my_half]), ends]).astype(jnp.int32)
    info_pos = jnp.concatenate([info, jnp.stack([me * rows])]).astype(jnp.int32)
    swap = [(device, device ^ 4) for device in range(devices)]
    work = 2 * local * local * HEAD // 2

    (packed,) = call(
        pack_kernel, [shape((devices, 3 * HALF, HEAD), BF16)], queries[0], keys[0], values[0]
    )
    mine = exchange(packed, "seq")
    other = lax.ppermute(mine[:, HALF:, :], "seq", swap)
    (own_sum,) = call(
        forward_own_kernel, [shape((local, HEAD), F32)], info, mine, scalars=1, flops=2 * work
    )
    (attended,) = call(
        forward_other_kernel,
        [shape((devices, HALF + EXTRA, HEAD), BF16)],
        info,
        mine,
        other,
        own_sum,
        scalars=1,
        flops=2 * work,
    )
    attended = exchange(attended, "seq")
    output, grad_gate, grad_att = call(
        norm_kernel,
        [
            shape((rows, width), BF16),
            shape((rows, width), BF16),
            shape((devices, HALF + EXTRA, HEAD), BF16),
        ],
        info_pos,
        attended,
        gates[0],
        grad_out[0],
        gain[None],
        scalars=1,
    )
    grad_att = exchange(grad_att, "seq")
    grad_sums = [pltpu.VMEM((local, HEAD), F32)] * 2
    dq, to_other, gain_part = call(
        backward_other_kernel,
        [
            shape((local, HEAD), F32),
            shape((2, local, HEAD), BF16),
            shape((groups, 8, HEAD), F32),
        ],
        info,
        mine,
        other,
        grad_att,
        scalars=1,
        scratch=grad_sums,
        flops=5 * work,
    )
    from_other = lax.ppermute(to_other, "seq", swap)
    gain_parts = exchange(gain_part, "own")
    dq, dk, dv = call(
        backward_own_kernel,
        [shape((local, HEAD), F32)] * 3,
        info,
        mine,
        grad_att,
        dq,
        scalars=1,
        flops=5 * work,
    )
    (joined,) = call(
        join_kernel,
        [shape((devices, 3 * HALF + EXTRA, HEAD), BF16)],
        dq,
        dk,
        dv,
        from_other,
        gain_parts,
    )
    grads = exchange(joined, "seq")
    grad_q, grad_k, grad_v, grad_gain = call(
        unpack_kernel,
        [shape((rows, width), BF16)] * 3 + [shape((1, width), F32)],
        grads,
    )
    return (output[None], grad_q[None], grad_k[None], grad_v[None], grad_gate[None], grad_gain[0])


def solution(mesh):
    wide = P("own", "seq", None)
    return jax.shard_map(
        per_device,
        mesh=mesh,
        in_specs=(wide, wide, wide, wide, P("own", None), P(), wide),
        out_specs=(wide, wide, wide, wide, wide, P()),
        check_vma=False,
    )
```

time: 625 us -> 217 us (0.35)
  waiting for transfers between devices: 307 us -> 28.6 us
  starting transfers between devices: 85.2 us -> 26 us
  local copies, waits for them, and re-layouts: 51.7 us -> 5.37 us
  matrix products: 41.2 us -> 0 us
  blocking collectives: 114 us -> 135 us
  Pallas kernels: 0 us -> 20 us
  between operations: 14.4 us -> 0.76 us
  other arithmetic: 8.14 us -> 0.33 us
    all_gather x2 -> x0, waiting for transfers between devices: 221 us -> none  [the longest x1 125 us: per_device(): lax.all_gather(values, 'seq', axis=1, tiled=True)]
    all_to_all x0 -> x3, blocking collectives: none -> 135 us  [exchange(): return lax.all_to_all(array, axis, 0, 0, tiled=True)]
    psum x1 -> x0, blocking collectives: 114 us -> none  [per_device(): grad_gain = lax.psum(gain_part, ('seq', 'own'))]
    ppermute x16 -> x2, starting transfers between devices: 85.1 us -> 5.01 us  [the longest x1 2.56 us: per_device(): other = lax.ppermute(mine[:, HALF:, :], 'seq', swap)]
    ppermute x16 -> x2, waiting for transfers between devices: 85.5 us -> 7.61 us  [the longest x1 7.61 us: per_device(): other = lax.ppermute(mine[:, HALF:, :], 'seq', swap)]
    dot_general x6 -> x0, matrix products: 41.2 us -> none  [the longest x1 12.1 us: per_device(): jnp.einsum('hts,shd->thd', grad_scores, ka3, preferred_element_type=jnp.f...]
    unnamed x50 -> x18, local copies, waits for them, and re-layouts: 29.6 us -> 5.34 us
    all_to_all x0 -> x2, starting transfers between devices: none -> 21 us  [exchange(): return lax.all_to_all(array, axis, 0, 0, tiled=True)]
  transfers between devices with their start and end apart: 18 -> 4, of which waited for: 7 -> 3; matrix products, arithmetic and copies ran while one was open for 9% -> 0% of each run, Pallas kernels for 0% -> 3%
where the time goes in v1:
time: 217 us; the launch traced here: 216 us
  blocking collectives  135 us (62%)
  waiting for transfers between devices  28.6 us (13%)
  starting transfers between devices  26 us (12%)
  Pallas kernels  20 us (9%)
  local copies, waits for them, and re-layouts  5.37 us (2%)
    all_to_all x3, blocking collectives, exchange(): return lax.all_to_all(array, axis, 0, 0, tiled=True)  135 us
    all_to_all x2, starting transfers between devices, exchange(): return lax.all_to_all(array, axis, 0, 0, tiled=True)  21 us
    all_to_all x2, waiting for transfers between devices, exchange(): return lax.all_to_all(array, axis, 0, 0, tiled=True)  21 us
    pallas_call x8, Pallas kernels, call(): pl.pallas_call(kernel, out_shape=outs, in_specs=specs, out_specs=[pl.Bloc...  20 us
    ppermute x1, waiting for transfers between devices, per_device(): other = lax.ppermute(mine[:, HALF:, :], 'seq', swap)  7.61 us
    unnamed x18, local copies, waits for them, and re-layouts  5.34 us
  transfers between devices with their start and end apart: 4, of which 3 were waited for; matrix products, arithmetic and copies ran while one was open for 0% of the time, Pallas kernels for 3%

profile of v1, /device:TPU:24, one launch (start us, length us, event | category | flops | bytes accessed | tf_op | source)
XLA Modules:
  0.0 216.1 jit_solution(8006445295255773715)
XLA Ops:
  0.6 0.0 copy-start.2
  0.6 0.9 copy-done.2
  1.6 0.0 copy-start.3
  1.6 0.9 copy-done.3
  2.5 0.0 copy-start.4
  2.5 0.9 copy-done.4
  3.5 0.1 shard_map.118
  3.6 56.0 %all_to_all.25.mine_ref = bf16[16,192,128]{2,1,0:T(8,128)(2,1)S(1)} all-to-all(bf16[16,192,128]{2,1,0:T(8,128)(2,1)S(1)} %shard_map.118), channel_id=1, replica_groups=mesh['seq'=16,'own'=32] {'seq'}, dimensions={0} | all-to-all | bytes 1572864 | tf_op jit(solution)/shard_map/all_to_all | solution.py:270
  59.7 2.6 %collective-permute-start = (bf16[16,128,128]{2,1,0:T(8,128)(2,1)S(1)}, bf16[16,128,128]{2,1,0:T(8,128)(2,1)S(1)}, u32[]{:S(2)}, u32[]{:S(2)}) collective-permute-start(bf16[16,128,128]{2,1,0:T(8,128)(2,1)S(1)} %slice.4), channel_id=1, source_target_pairs={{0,128},{32,160},{64,192},{96,224},{128,0},{160,32},{192,64},{224,... | collective-permute-start | bytes 1572872 | tf_op jit(solution)/shard_map/ppermute | solution.py:291
  62.3 0.0 copy-start.8
  62.3 0.6 copy-done.8
  63.0 0.2 reduce-window.9
  63.1 0.1 pad_add_fusion.1.info
  63.2 3.1 %shard_map.119.sum_ref = f32[1024,128]{1,0:T(8,128)S(1)} custom-call(s32[5]{0:T(128)S(1)} %pad_add_fusion.1.info, bf16[16,192,128]{2,1,0:T(8,128)(2,1)S(1)} %all_to_all.25.mine_ref), custom_call_target="tpu_custom_call" | custom-call | flops 268435456 | bytes 1310740 | tf_op jit(solution)/shard_map/pallas_call | solution.py:258
  66.3 7.6 %collective-permute-done.other_ref = bf16[16,128,128]{2,1,0:T(8,128)(2,1)S(1)} collective-permute-done((bf16[16,128,128]{2,1,0:T(8,128)(2,1)S(1)}, bf16[16,128,128]{2,1,0:T(8,128)(2,1)S(1)}, u32[]{:S(2)}, u32[]{:S(2)}) %collective-permute-start) | collective-permute-done | bytes 524320 | tf_op jit(solution)/shard_map/ppermute | solution.py:291
  73.9 4.4 %shard_map.120 = bf16[16,80,128]{2,1,0:T(8,128)(2,1)} custom-call(s32[5]{0:T(128)S(1)} %pad_add_fusion.1.info, bf16[16,192,128]{2,1,0:T(8,128)(2,1)S(1)} %all_to_all.25.mine_ref, bf16[16,128,128]{2,1,0:T(8,128)(2,1)S(1)} %collective-permute-done.other_ref, f32[1024,128]{1,0:T(8,128)S(1)} %shard_map.119.sum_ref), custom_call_target="tpu_custom_call" | custom-call | flops 268435456 | bytes 2162708 | tf_op jit(solution)/shard_map/pallas_call | solution.py:258
  78.3 0.0 copy-start
  78.3 0.0 copy-start.1
  78.3 10.3 %all-to-all-start.1 = ((bf16[16,80,128]{2,1,0:T(8,128)(2,1)}), bf16[16,80,128]{2,1,0:T(8,128)(2,1)S(1)}, u32[]{:S(2)}, u32[]{:S(2)}) async-start(bf16[16,80,128]{2,1,0:T(8,128)(2,1)} %shard_map.120), calls=%async_computation.1 | async-start | bytes 655360 | tf_op jit(solution)/shard_map/all_to_all | solution.py:270
  88.7 0.0 copy-start.5
  88.7 0.1 pad_add_fusion.info
  88.8 17.5 %all-to-all-done.1.att_ref = bf16[16,80,128]{2,1,0:T(8,128)(2,1)S(1)} async-done(((bf16[16,80,128]{2,1,0:T(8,128)(2,1)}), bf16[16,80,128]{2,1,0:T(8,128)(2,1)S(1)}, u32[]{:S(2)}, u32[]{:S(2)}) %all-to-all-start.1) | async-done | bytes 327712 | tf_op jit(solution)/shard_map/all_to_all | solution.py:270
  106.2 0.0 copy-done
  106.2 0.0 copy-done.1
  106.2 0.0 copy-done.5
  106.2 2.0 shard_map.121
  108.2 26.0 %all_to_all.26.grad_ref = bf16[16,80,128]{2,1,0:T(8,128)(2,1)S(1)} all-to-all(bf16[16,80,128]{2,1,0:T(8,128)(2,1)S(1)} %get-tuple-element.20), channel_id=1, replica_groups=mesh['seq'=16,'own'=32] {'seq'}, dimensions={0} | all-to-all | bytes 655360 | tf_op jit(solution)/shard_map/all_to_all | solution.py:270
  134.3 5.0 %shard_map.122 = (f32[1024,128]{1,0:T(8,128)S(1)}, bf16[2,1024,128]{2,1,0:T(8,128)(2,1)}, f32[32,8,128]{2,1,0:T(8,128)}) custom-call(s32[5]{0:T(128)S(1)} %pad_add_fusion.1.info, bf16[16,192,128]{2,1,0:T(8,128)(2,1)S(1)} %all_to_all.25.mine_ref, bf16[16,128,128]{2,1,0:T(8,128)(2,1)S(1)} %collective-permute-done.other_ref, ...), custom_call_target="tpu_custom_call" | custom-call | flops 671088640 | bytes 2818068 | tf_op jit(solution)/shard_map/pallas_call | solution.py:258
  139.3 0.0 copy-start.6
  139.3 0.8 copy-done.6
  140.1 2.5 %collective-permute-start.1 = (bf16[2,1024,128]{2,1,0:T(8,128)(2,1)}, bf16[2,1024,128]{2,1,0:T(8,128)(2,1)S(1)}, u32[]{:S(2)}, u32[]{:S(2)}) collective-permute-start(bf16[2,1024,128]{2,1,0:T(8,128)(2,1)} %get-tuple-element.25), channel_id=1, source_target_pairs={{0,128},{32,160},{64,192},{96,224},{128,0},{160,32},{192,64},{224,... | collective-permute-start | bytes 1572872 | tf_op jit(solution)/shard_map/ppermute | solution.py:337
  142.5 10.7 %all-to-all-start.3 = ((f32[32,8,128]{2,1,0:T(8,128)}), f32[32,8,128]{2,1,0:T(8,128)S(1)}, u32[]{:S(2)}, u32[]{:S(2)}) async-start(f32[32,8,128]{2,1,0:T(8,128)} %get-tuple-element.26), calls=%async_computation.3 | async-start | bytes 262144 | tf_op jit(solution)/shard_map/all_to_all | solution.py:270
  153.2 0.0 copy-start.7
  153.2 1.0 copy-done.7
  154.3 4.1 %shard_map.123 = (f32[1024,128]{1,0:T(8,128)S(1)}, f32[1024,128]{1,0:T(8,128)S(1)}, f32[1024,128]{1,0:T(8,128)S(1)}) custom-call(s32[5]{0:T(128)S(1)} %pad_add_fusion.1.info, bf16[16,192,128]{2,1,0:T(8,128)(2,1)S(1)} %all_to_all.25.mine_ref, bf16[16,80,128]{2,1,0:T(8,128)(2,1)S(1)} %all_to_all.26.grad_ref, f32[1024,128]{1,0:T(8,128)S(1)} %copy-done.7), custom_call_target="tpu_custom_call" | custom-call | flops 671088640 | bytes 3211284 | tf_op jit(solution)/shard_map/pallas_call | solution.py:258
  158.4 3.6 %all-to-all-done.3.gain_ref = f32[32,8,128]{2,1,0:T(8,128)S(1)} async-done(((f32[32,8,128]{2,1,0:T(8,128)}), f32[32,8,128]{2,1,0:T(8,128)S(1)}, u32[]{:S(2)}, u32[]{:S(2)}) %all-to-all-start.3) | async-done | bytes 131104 | tf_op jit(solution)/shard_map/all_to_all | solution.py:270
  161.9 0.0 collective-permute-done.1.other_ref
  161.9 0.1 shard_map.124
  162.1 53.0 %all_to_all.27.in_ref = bf16[16,208,128]{2,1,0:T(8,128)(2,1)S(1)} all-to-all(bf16[16,208,128]{2,1,0:T(8,128)(2,1)S(1)} %shard_map.124), channel_id=1, replica_groups=mesh['seq'=16,'own'=32] {'seq'}, dimensions={0} | all-to-all | bytes 1703936 | tf_op jit(solution)/shard_map/all_to_all | solution.py:270
  215.1 1.1 shard_map.125
  (1 shorter events, 0.0 us)
Async XLA Ops:
  0.6 1.0 copy-start.2
  1.6 0.9 copy-start.3
  2.5 0.9 copy-start.4
  59.7 14.2 %collective-permute-start = (bf16[16,128,128]{2,1,0:T(8,128)(2,1)S(1)}, bf16[16,128,128]{2,1,0:T(8,128)(2,1)S(1)}, u32[]{:S(2)}, u32[]{:S(2)}) collective-permute-start(bf16[16,128,128]{2,1,0:T(8,128)(2,1)S(1)} %slice.4), channel_id=1, source_target_pairs={{0,128},{32,160},{64,192},{96,224},{128,0},{160,32},{192,64},{224,... | collective-permute-start | bytes 1572872 | tf_op jit(solution)/shard_map/ppermute | solution.py:291
  62.3 0.7 copy-start.8
  78.3 27.9 %copy-start = (bf16[1,128,1024]{2,1,0:T(8,128)(2,1)S(1)}, bf16[1,128,1024]{2,1,0:T(8,128)(2,1)}, u32[]{:S(2)}) copy-start(bf16[1,128,1024]{2,1,0:T(8,128)(2,1)} %param.10) | copy-start | bytes 786436
  78.3 27.9 %copy-start.1 = (bf16[1,128,1024]{2,1,0:T(8,128)(2,1)S(1)}, bf16[1,128,1024]{2,1,0:T(8,128)(2,1)}, u32[]{:S(2)}) copy-start(bf16[1,128,1024]{2,1,0:T(8,128)(2,1)} %param.13) | copy-start | bytes 786436
  78.3 27.9 %all-to-all-start.1 = ((bf16[16,80,128]{2,1,0:T(8,128)(2,1)}), bf16[16,80,128]{2,1,0:T(8,128)(2,1)S(1)}, u32[]{:S(2)}, u32[]{:S(2)}) async-start(bf16[16,80,128]{2,1,0:T(8,128)(2,1)} %shard_map.120), calls=%async_computation.1 | async-start | bytes 655360 | tf_op jit(solution)/shard_map/all_to_all | solution.py:270
  88.7 17.5 %copy-start.5 = (f32[1024]{0:T(1024)S(1)}, f32[1024]{0:T(1024)}, u32[]{:S(2)}) copy-start(f32[1024]{0:T(1024)} %param.12) | copy-start | bytes 12292
  139.3 0.8 copy-start.6
  140.1 21.9 %collective-permute-start.1 = (bf16[2,1024,128]{2,1,0:T(8,128)(2,1)}, bf16[2,1024,128]{2,1,0:T(8,128)(2,1)S(1)}, u32[]{:S(2)}, u32[]{:S(2)}) collective-permute-start(bf16[2,1024,128]{2,1,0:T(8,128)(2,1)} %get-tuple-element.25), channel_id=1, source_target_pairs={{0,128},{32,160},{64,192},{96,224},{128,0},{160,32},{192,64},{224,... | collective-permute-start | bytes 1572872 | tf_op jit(solution)/shard_map/ppermute | solution.py:337
  142.5 19.4 %all-to-all-start.3 = ((f32[32,8,128]{2,1,0:T(8,128)}), f32[32,8,128]{2,1,0:T(8,128)S(1)}, u32[]{:S(2)}, u32[]{:S(2)}) async-start(f32[32,8,128]{2,1,0:T(8,128)} %get-tuple-element.26), calls=%async_computation.3 | async-start | bytes 262144 | tf_op jit(solution)/shard_map/all_to_all | solution.py:270
  153.2 1.0 copy-start.7

commit v2 on v0

v2 whole, which is shorter than its diff:
```python
import math

import jax
import jax.numpy as jnp
from jax import lax
from jax.experimental import pallas as pl
from jax.experimental.pallas import tpu as pltpu
from jax.sharding import PartitionSpec as P


H = 8
HEAD = 128
ZS = 4
ROWS = 128
PAIR = 2 * HEAD
TILE = 2 * ROWS
BLOCK = ZS * ROWS
EXTRA = 16
F32 = jnp.float32
BF16 = jnp.bfloat16
VMEM_LIMIT = 48 * 1024 * 1024


def dot(a, b, dims):
    return lax.dot_general(a, b, (dims, ((), ())), preferred_element_type=F32)


def iota(shape, dim):
    return lax.broadcasted_iota(jnp.int32, shape, dim)


def bounds(pos, info):
    start = jnp.zeros_like(pos)
    end = jnp.full_like(pos, 1 << 30)
    for user in range(info.shape[0] - 1):
        edge = info[1 + user]
        start = jnp.where(pos >= edge, jnp.maximum(start, edge), start)
        end = jnp.where(pos < edge, jnp.minimum(end, edge), end)
    return start, end - start


def head_cols(head):
    return slice(head * HEAD, (head + 1) * HEAD)


def tile_rows(ref, tile, first, head):
    block = ref[pl.ds(tile * 2, 2), first : first + ROWS, head_cols(head)]
    return block.reshape(TILE, HEAD)


def eye():
    return iota((ROWS, HEAD), 0) == iota((ROWS, HEAD), 1)


def to_row(column):
    return jnp.sum(jnp.where(eye(), column, 0.0), axis=0, keepdims=True)


def to_column(row):
    return jnp.sum(jnp.where(eye(), row, 0.0), axis=1, keepdims=True)


def pack_kv_kernel(k_ref, v_ref, out_ref):
    for z in range(ZS):
        cols = slice(z * PAIR, (z + 1) * PAIR)
        out_ref[z, 0:ROWS, :] = k_ref[:, cols]
        out_ref[z, ROWS : 2 * ROWS, :] = v_ref[:, cols]


def pack_q_kernel(q_ref, gates_ref, grad_ref, gain_ref, out_ref):
    for z in range(ZS):
        cols = slice(z * PAIR, (z + 1) * PAIR)
        out_ref[z, 0:ROWS, :] = q_ref[:, cols]
        dnorm = grad_ref[:, cols].astype(F32) * gates_ref[:, cols].astype(F32) * gain_ref[:, cols]
        out_ref[z, ROWS : 2 * ROWS, :] = dnorm.astype(BF16)


def key_tiles(info, tile, back):
    block = info[0] // ZS
    first, _ = bounds(block * BLOCK + tile * TILE, info)
    low = jnp.maximum(first // TILE - 2 * (block - back), 0)
    return low, (tile + 1 if back == 0 else 2)


def forward_kernel(info, qd_ref, kv0_ref, kv1_ref, kv2_ref, att_ref, stats_ref):
    scale = 0.5 / math.sqrt(HEAD)
    block = info[0] // ZS
    where = iota((1, TILE), 1)
    for tile in range(2):
        q = [tile_rows(qd_ref, tile, 0, head) for head in range(2)]
        pos = block * BLOCK + tile * TILE + iota((TILE, 1), 0)
        start, length = bounds(pos, info)
        total = (jnp.zeros((TILE, HEAD), F32),) * 2
        for back, kv_ref in enumerate((kv0_ref, kv1_ref, kv2_ref)):

            def step(key_tile, total):
                base = (block - back) * BLOCK + key_tile * TILE
                allowed = (where >= start - base) & (where <= pos - base)
                sums = []
                for head in range(2):
                    k = tile_rows(kv_ref, key_tile, 0, head)
                    v = tile_rows(kv_ref, key_tile, ROWS, head)
                    half_score = dot(q[head], k, ((1,), (1,))) * scale
                    silu = half_score + half_score * jnp.tanh(half_score)
                    probs = jnp.where(allowed, silu, 0.0).astype(BF16)
                    sums.append(total[head] + dot(probs, v, ((1,), (0,))))
                return tuple(sums)

            low, high = key_tiles(info, tile, back)
            total = lax.fori_loop(low, high, step, total)
        inverse = 1.0 / length.astype(F32)
        attended = [part * inverse for part in total]
        dnorm = [tile_rows(qd_ref, tile, ROWS, head).astype(F32) for head in range(2)]
        mean = jnp.sum(attended[0] + attended[1], axis=1, keepdims=True) / PAIR
        center = [part - mean for part in attended]
        square = jnp.sum(center[0] * center[0] + center[1] * center[1], axis=1, keepdims=True)
        plain = jnp.sum(dnorm[0] + dnorm[1], axis=1, keepdims=True)
        mixed = jnp.sum(dnorm[0] * center[0] + dnorm[1] * center[1], axis=1, keepdims=True)
        for part in range(2):
            span = slice(part * ROWS, (part + 1) * ROWS)
            slot = tile * 2 + part
            for index, column in enumerate((mean, square, plain, mixed)):
                row = to_row(column[span])
                for z in range(ZS):
                    stats_ref[z, index * ZS + slot : index * ZS + slot + 1, :] = row
        for head in range(2):
            att_ref[tile * TILE : (tile + 1) * TILE, head_cols(head)] = attended[head]


def part_cols(info, by, head):
    z = (info[0] - by) % ZS
    return pl.ds(pl.multiple_of(z * PAIR + head * HEAD, HEAD), HEAD)


def norm_kernel(info, in0_ref, in1_ref, in2_ref, in3_ref, *refs):
    gates_ref, grad_ref, gain_ref, out_ref, gate_grad_ref, gain_sum_ref = refs
    width = H * HEAD
    heads = [(by, ref, head) for by, ref in enumerate((in0_ref, in1_ref, in2_ref, in3_ref)) for head in range(2)]
    attended = []
    for by, ref, head in heads:
        mean = to_column(ref[ROWS : ROWS + 1, head_cols(head)].astype(F32))
        attended.append(ref[0:ROWS, head_cols(head)].astype(F32) + mean)
    mean = jnp.sum(sum(attended), axis=1, keepdims=True) / width
    center = [block - mean for block in attended]
    var = jnp.sum(sum(block * block for block in center), axis=1, keepdims=True) / width
    rstd = lax.rsqrt(var + 1e-05)
    for (by, ref, head), block in zip(heads, center):
        cols = part_cols(info, by, head)
        scaled = block * rstd * gain_ref[0:1, cols]
        out_ref[:, cols] = (scaled * gates_ref[:, cols].astype(F32)).astype(BF16)
        gate_grad_ref[:, cols] = (scaled * grad_ref[:, cols].astype(F32)).astype(BF16)
        three = ref[ROWS : ROWS + EXTRA, head_cols(head)].astype(F32)
        gain_sum_ref[0:1, cols] = three[1:2] + three[2:3] + three[3:4]


def make_grad_att(info, qd_ref, att_ref, stats_ref, grad_ref, gain_ref):
    width = H * HEAD
    block = info[0] // ZS
    sums = [jnp.zeros((1, HEAD), F32) for _ in range(2)]
    for slot in range(ZS):
        stat = [
            [stats_ref[z, index * ZS + slot : index * ZS + slot + 1, :] for z in range(ZS)]
            for index in range(4)
        ]
        means, squares, plains, mixeds = stat
        mean = sum(means) / ZS
        var = (sum(squares) + PAIR * sum((m - mean) * (m - mean) for m in means)) / width
        rstd = lax.rsqrt(var + 1e-05)
        first = sum(plains) / width
        second = rstd * sum(x + (m - mean) * p for x, m, p in zip(mixeds, means, plains)) / width
        _, length = bounds(block * BLOCK + slot * ROWS + iota((1, ROWS), 1), info)
        factor = rstd * (1.0 / length.astype(F32))
        mean, rstd, first, second, factor = (
            to_column(row) for row in (mean, rstd, first, second, factor)
        )
        rows = slice(slot * ROWS, (slot + 1) * ROWS)
        for head in range(2):
            normed = (att_ref[rows, head_cols(head)] - mean) * rstd
            dnorm = qd_ref[slot, ROWS : 2 * ROWS, head_cols(head)].astype(F32)
            sums[head] = sums[head] + jnp.sum(dnorm * normed, axis=0, keepdims=True)
            grad_att = factor * (dnorm - first - normed * second)
            grad_ref[slot, :, head_cols(head)] = grad_att.astype(BF16)
    for head in range(2):
        gain_ref[head : head + 1, :] = sums[head]


def make_back(info, att_ref, gain_ref, back_refs):
    index = iota((EXTRA, HEAD), 0)
    for head in range(2):
        cols = head_cols(head)
        gain = gain_ref[head : head + 1, :]
        high = gain.astype(BF16).astype(F32)
        mid = (gain - high).astype(BF16).astype(F32)
        low = gain - high - mid
        three = jnp.where(index == 1, high, jnp.where(index == 2, mid, low))
        for by, back_ref in enumerate(back_refs):
            slot = (info[0] + by) % ZS
            attended = att_ref[pl.ds(pl.multiple_of(slot * ROWS, ROWS), ROWS), cols]
            middle = jnp.mean(attended, axis=1, keepdims=True).astype(BF16).astype(F32)
            back_ref[0:ROWS, cols] = (attended - middle).astype(BF16)
            extra = jnp.where(index == 0, to_row(middle), three)
            back_ref[ROWS : ROWS + EXTRA, cols] = extra.astype(BF16)


def backward_tiles(info, back, q_ref, kv_ref, grad_ref, dq_ref, dkv_ref):
    scale = 0.5 / math.sqrt(HEAD)
    block = info[0] // ZS
    where = iota((TILE, 1), 0)
    dkv_ref[...] = jnp.zeros_like(dkv_ref)
    for tile in range(2):
        q = [tile_rows(q_ref, tile, 0, head) for head in range(2)]
        grad = [tile_rows(grad_ref, tile, 0, head) for head in range(2)]
        pos = block * BLOCK + tile * TILE + iota((1, TILE), 1)
        start, _ = bounds(pos, info)
        here = slice(tile * TILE, (tile + 1) * TILE)

        def step(key_tile, total):
            base = (block - back) * BLOCK + key_tile * TILE
            allowed = (where >= start - base) & (where <= pos - base)
            sums = []
            for head in range(2):
                k = tile_rows(kv_ref, key_tile, 0, head)
                v = tile_rows(kv_ref, key_tile, ROWS, head)
                half_score = dot(k, q[head], ((1,), (1,))) * scale
                grad_probs = dot(v, grad[head], ((1,), (1,)))
                tanh = jnp.tanh(half_score)
                twice = 1.0 + tanh
                probs = jnp.where(allowed, half_score * twice, 0.0).astype(BF16)
                slope = twice * (1.0 + half_score * (1.0 - tanh))
                grad_scores = jnp.where(allowed, grad_probs * slope, 0.0).astype(BF16)
                slots = pl.ds(key_tile * 2, 2)
                dk = dot(grad_scores, q[head], ((1,), (0,))).reshape(2, ROWS, HEAD)
                dv = dot(probs, grad[head], ((1,), (0,))).reshape(2, ROWS, HEAD)
                dkv_ref[slots, 0:ROWS, head_cols(head)] += dk
                dkv_ref[slots, ROWS : 2 * ROWS, head_cols(head)] += dv
                sums.append(total[head] + dot(grad_scores, k, ((0,), (0,))))
            return tuple(sums)

        low, high = key_tiles(info, tile, back)
        total = tuple(dq_ref[here, head_cols(head)] for head in range(2))
        total = lax.fori_loop(low, high, step, total)
        for head in range(2):
            dq_ref[here, head_cols(head)] = total[head]


def send_sums(dkv_ref, send_ref):
    scale = 0.5 / math.sqrt(HEAD)
    for slot in range(ZS):
        send_ref[slot, 0:ROWS, :] = (dkv_ref[slot, 0:ROWS, :] * scale).astype(BF16)
        send_ref[slot, ROWS : 2 * ROWS, :] = dkv_ref[slot, ROWS : 2 * ROWS, :].astype(BF16)


def backward_far_kernel(
    info, qd_ref, kv2_ref, att_ref, stats_ref, send_ref, grad_ref, dq_ref, gain_ref, dkv_ref
):
    make_grad_att(info, qd_ref, att_ref, stats_ref, grad_ref, gain_ref)
    dq_ref[...] = jnp.zeros_like(dq_ref)
    backward_tiles(info, 2, qd_ref, kv2_ref, grad_ref, dq_ref, dkv_ref)
    send_sums(dkv_ref, send_ref)


def backward_near_kernel(info, qd_ref, kv1_ref, grad_ref, dq_in_ref, send_ref, dq_ref, dkv_ref):
    dq_ref[...] = dq_in_ref[...]
    backward_tiles(info, 1, qd_ref, kv1_ref, grad_ref, dq_ref, dkv_ref)
    send_sums(dkv_ref, send_ref)


def backward_own_kernel(info, qd_ref, kv0_ref, grad_ref, att_ref, gain_ref, dq_in_ref, dq_ref, dkv_ref, *back_refs):
    make_back(info, att_ref, gain_ref, back_refs)
    dq_ref[...] = dq_in_ref[...]
    backward_tiles(info, 0, qd_ref, kv0_ref, grad_ref, dq_ref, dkv_ref)


def join_kernel(dq_ref, dkv_ref, other1_ref, other2_ref, out_ref):
    scale = 0.5 / math.sqrt(HEAD)
    for slot in range(ZS):
        others = other1_ref[slot].astype(F32) + other2_ref[slot].astype(F32)
        dk = dkv_ref[slot, 0:ROWS, :] * scale + others[0:ROWS]
        dv = dkv_ref[slot, ROWS : 2 * ROWS, :] + others[ROWS : 2 * ROWS]
        out_ref[slot, 0:ROWS, :] = dk.astype(BF16)
        out_ref[slot, ROWS : 2 * ROWS, :] = dv.astype(BF16)
        dq = dq_ref[slot * ROWS : (slot + 1) * ROWS, :] * scale
        out_ref[slot, 2 * ROWS : 3 * ROWS, :] = dq.astype(BF16)


def unpack_kernel(in_ref, dq_ref, dk_ref, dv_ref):
    for z in range(ZS):
        cols = slice(z * PAIR, (z + 1) * PAIR)
        dk_ref[:, cols] = in_ref[z, 0:ROWS, :]
        dv_ref[:, cols] = in_ref[z, ROWS : 2 * ROWS, :]
        dq_ref[:, cols] = in_ref[z, 2 * ROWS : 3 * ROWS, :]


def call(kernel, outs, *args, scalars=0, scratch=(), flops=1):
    specs = [pl.BlockSpec(memory_space=pltpu.SMEM)] * scalars
    specs += [pl.BlockSpec(memory_space=pltpu.VMEM)] * (len(args) - scalars)
    return pl.pallas_call(
        kernel,
        out_shape=outs,
        in_specs=specs,
        out_specs=[pl.BlockSpec(memory_space=pltpu.VMEM)] * len(outs),
        scratch_shapes=scratch,
        compiler_params=pltpu.CompilerParams(vmem_limit_bytes=VMEM_LIMIT),
        cost_estimate=pl.CostEstimate(flops=flops, bytes_accessed=0, transcendentals=0),
    )(*args)


def along_z(array):
    groups = [[y * ZS + z for z in range(ZS)] for y in range(ZS)]
    return lax.all_to_all(array, "seq", 0, 0, axis_index_groups=groups, tiled=True)


def shift_z(array, by):
    pairs = [(y * ZS + z, y * ZS + (z + by) % ZS) for y in range(ZS) for z in range(ZS)]
    return lax.ppermute(array, "seq", pairs)


def add_over(array, axis, bits):
    size = lax.axis_size(axis)
    for bit in bits:
        if bit < size:
            array = array + lax.ppermute(array, axis, [(i, i ^ bit) for i in range(size)])
    return array


def shift_y(array, by):
    devices = lax.axis_size("seq")
    pairs = [(i, i + ZS * by) for i in range(devices) if 0 <= i + ZS * by < devices]
    return lax.ppermute(array, "seq", pairs)


def per_device(queries, keys, values, gates, lengths, gain, grad_out):
    rows, width = queries.shape[1:]
    shape = jax.ShapeDtypeStruct
    ends = jnp.cumsum(lengths[0])
    info = jnp.concatenate([jnp.stack([lax.axis_index("seq")]), ends]).astype(jnp.int32)
    pair = shape((ZS, 2 * ROWS, PAIR), BF16)
    pair_sums = shape((ZS, 2 * ROWS, PAIR), F32)
    block = shape((BLOCK, PAIR), F32)
    sums_scratch = [pltpu.VMEM(pair_sums.shape, F32)]

    (kv,) = call(pack_kv_kernel, [pair], keys[0], values[0])
    kv0 = along_z(kv)
    kv2 = shift_y(kv0, 2)
    kv1 = shift_y(kv0, 1)
    (qd,) = call(pack_q_kernel, [pair], queries[0], gates[0], grad_out[0], gain[None])
    qd = along_z(qd)
    attended, stats = call(
        forward_kernel,
        [block, shape((ZS, 4 * ZS, ROWS), F32)],
        info,
        qd,
        kv0,
        kv1,
        kv2,
        scalars=1,
    )
    stats = along_z(stats)
    to2, grad_att, dq, gain_sum = call(
        backward_far_kernel,
        [pair, shape((ZS, ROWS, PAIR), BF16), block, shape((2, HEAD), F32)],
        info,
        qd,
        kv2,
        attended,
        stats,
        scalars=1,
        scratch=sums_scratch,
    )
    from2 = shift_y(to2, -2)
    to1, dq = call(
        backward_near_kernel,
        [pair, block],
        info,
        qd,
        kv1,
        grad_att,
        dq,
        scalars=1,
        scratch=sums_scratch,
    )
    from1 = shift_y(to1, -1)
    gain_sum, to1 = lax.optimization_barrier((gain_sum, to1))
    gain_sum = add_over(gain_sum, "own", (1,))
    dq, dkv, *back = call(
        backward_own_kernel,
        [block, pair_sums] + [shape((ROWS + EXTRA, PAIR), BF16)] * ZS,
        info,
        qd,
        kv0,
        grad_att,
        attended,
        gain_sum,
        dq,
        scalars=1,
    )
    back[2] = shift_z(back[2], 2)
    back[1] = shift_z(back[1], 1)
    back[3] = shift_z(back[3], 3)
    output, grad_gate, gain_sum = call(
        norm_kernel,
        [shape((rows, width), BF16)] * 2 + [shape((1, width), F32)],
        info,
        *back,
        gates[0],
        grad_out[0],
        gain[None],
        scalars=1,
    )
    (joined,) = call(join_kernel, [shape((ZS, 3 * ROWS, PAIR), BF16)], dq, dkv, from1, from2)
    gain_sum, joined = lax.optimization_barrier((gain_sum, joined))
    gain_sum = add_over(add_over(add_over(gain_sum, "own", (2, 4)), "seq", (4, 8)), "own", (8, 16))
    grad_gain = gain_sum.reshape(width) / gain
    grad_q, grad_k, grad_v = call(
        unpack_kernel, [shape((rows, width), BF16)] * 3, along_z(joined)
    )
    return (output[None], grad_q[None], grad_k[None], grad_v[None], grad_gate[None], grad_gain)


def solution(mesh):
    wide = P("own", "seq", None)
    return jax.shard_map(
        per_device,
        mesh=mesh,
        in_specs=(wide, wide, wide, wide, P("own", None), P(), wide),
        out_specs=(wide, wide, wide, wide, wide, P()),
        check_vma=False,
    )
```

time: 625 us -> 201 us (0.32)
  waiting for transfers between devices: 307 us -> 70.2 us
  blocking collectives: 114 us -> 25.2 us
  local copies, waits for them, and re-layouts: 51.7 us -> 3.22 us
  matrix products: 41.2 us -> 0 us
  Pallas kernels: 0 us -> 20.9 us
  between operations: 14.4 us -> 0.84 us
  starting transfers between devices: 85.2 us -> 76.5 us
  other arithmetic: 8.14 us -> 0.9 us
    all_gather x2 -> x0, waiting for transfers between devices: 221 us -> none  [the longest x1 125 us: per_device(): lax.all_gather(values, 'seq', axis=1, tiled=True)]
    psum x1 -> x0, blocking collectives: 114 us -> none  [per_device(): grad_gain = lax.psum(gain_part, ('seq', 'own'))]
    ppermute x16 -> x14, waiting for transfers between devices: 85.5 us -> 29.8 us  [the longest x7 18.7 us: add_over(): lax.ppermute(array, axis, [(i, i ^ bit) for i in range(size)])]
    ppermute x16 -> x14, starting transfers between devices: 85.1 us -> 42 us  [the longest x7 24.6 us: add_over(): lax.ppermute(array, axis, [(i, i ^ bit) for i in range(size)])]
    dot_general x6 -> x0, matrix products: 41.2 us -> none  [the longest x1 12.1 us: per_device(): jnp.einsum('hts,shd->thd', grad_scores, ka3, preferred_element_type=jnp.f...]
    all_to_all x0 -> x3, waiting for transfers between devices: none -> 40.3 us  [along_z(): lax.all_to_all(array, 'seq', 0, 0, axis_index_groups=groups, tiled=True)]
    all_to_all x0 -> x3, starting transfers between devices: none -> 34.5 us  [along_z(): lax.all_to_all(array, 'seq', 0, 0, axis_index_groups=groups, tiled=True)]
    unnamed x50 -> x14, local copies, waits for them, and re-layouts: 29.6 us -> 3.22 us
  transfers between devices with their start and end apart: 18 -> 17, of which waited for: 7 -> 11; matrix products, arithmetic and copies ran while one was open for 9% -> 0% of each run, Pallas kernels for 0% -> 3%
where the time goes in v2:
time: 201 us; the launch traced here: 198 us
  starting transfers between devices  76.5 us (38%)
  waiting for transfers between devices  70.2 us (35%)
  blocking collectives  25.2 us (13%)
  Pallas kernels  20.9 us (10%)
  local copies, waits for them, and re-layouts  3.22 us (2%)
    all_to_all x3, waiting for transfers between devices, along_z(): lax.all_to_all(array, 'seq', 0, 0, axis_index_groups=groups, tiled=True)  40.3 us
    all_to_all x3, starting transfers between devices, along_z(): lax.all_to_all(array, 'seq', 0, 0, axis_index_groups=groups, tiled=True)  34.5 us
    all_to_all x1, blocking collectives, along_z(): lax.all_to_all(array, 'seq', 0, 0, axis_index_groups=groups, tiled=True)  25.2 us
    ppermute x7, starting transfers between devices, add_over(): lax.ppermute(array, axis, [(i, i ^ bit) for i in range(size)])  24.6 us
    pallas_call x9, Pallas kernels, call(): pl.pallas_call(kernel, out_shape=outs, in_specs=specs, out_specs=[pl.Bloc...  20.9 us
    ppermute x7, waiting for transfers between devices, add_over(): lax.ppermute(array, axis, [(i, i ^ bit) for i in range(size)])  18.7 us
    ppermute x3, starting transfers between devices, shift_z(): return lax.ppermute(array, 'seq', pairs)  12.1 us
    ppermute x3, waiting for transfers between devices, shift_z(): return lax.ppermute(array, 'seq', pairs)  11.2 us
  transfers between devices with their start and end apart: 17, of which 11 were waited for; matrix products, arithmetic and copies ran while one was open for 0% of the time, Pallas kernels for 3%

profile of v2, /device:TPU:24, one launch (start us, length us, event | category | flops | bytes accessed | tf_op | source)
XLA Modules:
  0.0 197.8 jit_solution(12852778060486365281)
XLA Ops:
  0.6 0.0 copy-start.3
  0.6 0.9 copy-done.3
  1.6 0.0 copy-start.4
  1.6 0.9 copy-done.4
  2.5 0.8 shard_map.119
  3.4 0.0 copy-start
  3.4 0.0 copy-start.1
  3.4 0.0 copy-start.2
  3.4 15.2 %all-to-all-start.1 = ((bf16[4,256,256]{2,1,0:T(8,128)(2,1)}), bf16[4,256,256]{2,1,0:T(8,128)(2,1)S(1)}, u32[]{:S(2)}, u32[]{:S(2)}) async-start(bf16[4,256,256]{2,1,0:T(8,128)(2,1)} %shard_map.119), calls=%async_computation.1 | async-start | bytes 1048576 | tf_op jit(solution)/shard_map/all_to_all | solution.py:310
  18.6 0.0 copy-start.5
  18.6 0.0 copy-done
  18.6 0.0 copy-done.1
  18.6 0.0 copy-done.2
  18.6 0.7 copy-done.5
  19.3 0.9 shard_map.118
  20.2 24.3 %all-to-all-done.1.kv0_ref = bf16[4,256,256]{2,1,0:T(8,128)(2,1)S(1)} async-done(((bf16[4,256,256]{2,1,0:T(8,128)(2,1)}), bf16[4,256,256]{2,1,0:T(8,128)(2,1)S(1)}, u32[]{:S(2)}, u32[]{:S(2)}) %all-to-all-start.1) | async-done | bytes 524320 | tf_op jit(solution)/shard_map/all_to_all | solution.py:310
  44.5 9.4 %all-to-all-start = ((bf16[4,256,256]{2,1,0:T(8,128)(2,1)}), bf16[4,256,256]{2,1,0:T(8,128)(2,1)S(1)}, u32[]{:S(2)}, u32[]{:S(2)}) async-start(bf16[4,256,256]{2,1,0:T(8,128)(2,1)} %shard_map.118), calls=%async_computation | async-start | bytes 1048576 | tf_op jit(solution)/shard_map/all_to_all | solution.py:310
  54.0 1.3 collective-permute-start.1
  55.3 1.3 collective-permute-start
  56.6 0.0 copy-start.6
  56.6 0.6 copy-done.6
  57.2 0.2 reduce-window.9
  57.4 0.1 pad_add_fusion.info
  57.5 16.0 %all-to-all-done.qd_ref = bf16[4,256,256]{2,1,0:T(8,128)(2,1)S(1)} async-done(((bf16[4,256,256]{2,1,0:T(8,128)(2,1)}), bf16[4,256,256]{2,1,0:T(8,128)(2,1)S(1)}, u32[]{:S(2)}, u32[]{:S(2)}) %all-to-all-start) | async-done | bytes 524320 | tf_op jit(solution)/shard_map/all_to_all | solution.py:310
  73.5 0.0 collective-permute-done.1.kv1_ref
  73.5 0.0 collective-permute-done.kv2_ref
  73.5 5.5 %shard_map.120 = (f32[512,256]{1,0:T(8,128)S(1)}, f32[4,16,128]{2,1,0:T(8,128)S(1)}) custom-call(s32[5]{0:T(128)S(1)} %pad_add_fusion.info, bf16[4,256,256]{2,1,0:T(8,128)(2,1)S(1)} %all-to-all-done.qd_ref, bf16[4,256,256]{2,1,0:T(8,128)(2,1)S(1)} %all-to-all-done.1.kv0_ref, bf16[4,256,256]{2,1,0:T(8,128)(2,1)S(1)} %collective-permute-done.1.kv1_ref, ...), custom_call_target="tpu_custom_call" | custom-call | flops 1 | tf_op jit(solution)/shard_map/pallas_call | solution.py:297
  79.0 25.2 %all_to_all.20.stats_ref = f32[4,16,128]{2,1,0:T(8,128)S(1)} all-to-all(f32[4,16,128]{2,1,0:T(8,128)S(1)} %get-tuple-element.30), channel_id=1, replica_groups={{0,32,64,96},{128,160,192,224},{256,288,320,352},{384,416,448,480},{1,3..., dimensions={0} | all-to-all | bytes 65536 | tf_op jit(solution)/shard_map/all_to_all | solution.py:310
  104.2 1.3 shard_map.121
  105.5 4.5 %shard_map.122 = (bf16[4,256,256]{2,1,0:T(8,128)(2,1)S(1)}, f32[512,256]{1,0:T(8,128)S(1)}) custom-call(s32[5]{0:T(128)S(1)} %pad_add_fusion.info, bf16[4,256,256]{2,1,0:T(8,128)(2,1)S(1)} %all-to-all-done.qd_ref, bf16[4,256,256]{2,1,0:T(8,128)(2,1)S(1)} %collective-permute-done.1.kv1_ref, bf16[4,128,256]{2,1,0:T(8,128)(2,1)S(1)} %get-tuple-element.31.grad_ref, ...), custom_call_target="tpu_custom_call" | custom-call | flops 1 | tf_op jit(solution)/shard_map/pallas_call | solution.py:297
  110.0 1.3 collective-permute-start.6
  111.4 1.3 collective-permute-start.7
  112.7 1.9 collective-permute-start.2
  114.6 1.1 collective-permute-done.2
  115.7 3.8 %shard_map.123 = (f32[512,256]{1,0:T(8,128)S(1)}, f32[4,256,256]{2,1,0:T(8,128)S(1)}, bf16[144,256]{1,0:T(8,128)(2,1)S(1)}, bf16[144,256]{1,0:T(8,128)(2,1)S(1)}...) custom-call(s32[5]{0:T(128)S(1)} %pad_add_fusion.info, bf16[4,256,256]{2,1,0:T(8,128)(2,1)S(1)} %all-to-all-done.qd_ref, ...), custom_call_target="tpu_custom_call" | custom-call | flops 1 | tf_op jit(solution)/shard_map/pallas_call | solution.py:297
  119.5 2.5 %collective-permute-start.3 = (bf16[144,256]{1,0:T(8,128)(2,1)S(1)}, bf16[144,256]{1,0:T(8,128)(2,1)S(1)}, u32[]{:S(2)}, u32[]{:S(2)}) collective-permute-start(bf16[144,256]{1,0:T(8,128)(2,1)S(1)} %get-tuple-element.38), channel_id=1, source_target_pairs={{0,32},{32,64},{64,96},{96,0},{128,160},{160,192},{192,224},{224,1... | collective-permute-start | bytes 221192 | tf_op jit(solution)/shard_map/ppermute | solution.py:315
  122.0 7.4 %collective-permute-start.4 = (bf16[144,256]{1,0:T(8,128)(2,1)S(1)}, bf16[144,256]{1,0:T(8,128)(2,1)S(1)}, u32[]{:S(2)}, u32[]{:S(2)}) collective-permute-start(bf16[144,256]{1,0:T(8,128)(2,1)S(1)} %get-tuple-element.39), channel_id=1, source_target_pairs={{0,64},{32,96},{64,0},{96,32},{128,192},{160,224},{192,128},{224,1... | collective-permute-start | bytes 221192 | tf_op jit(solution)/shard_map/ppermute | solution.py:315
  129.3 2.3 %collective-permute-start.5 = (bf16[144,256]{1,0:T(8,128)(2,1)S(1)}, bf16[144,256]{1,0:T(8,128)(2,1)S(1)}, u32[]{:S(2)}, u32[]{:S(2)}) collective-permute-start(bf16[144,256]{1,0:T(8,128)(2,1)S(1)} %get-tuple-element.40), channel_id=1, source_target_pairs={{0,96},{32,0},{64,32},{96,64},{128,224},{160,128},{192,160},{224,1... | collective-permute-start | bytes 221192 | tf_op jit(solution)/shard_map/ppermute | solution.py:315
  131.6 0.0 collective-permute-done.3.in1_ref
  131.6 5.7 %collective-permute-done.4.in2_ref = bf16[144,256]{1,0:T(8,128)(2,1)S(1)} collective-permute-done((bf16[144,256]{1,0:T(8,128)(2,1)S(1)}, bf16[144,256]{1,0:T(8,128)(2,1)S(1)}, u32[]{:S(2)}, u32[]{:S(2)}) %collective-permute-start.4) | collective-permute-done | bytes 73760 | tf_op jit(solution)/shard_map/ppermute | solution.py:315
  137.4 5.4 %collective-permute-done.5.in3_ref = bf16[144,256]{1,0:T(8,128)(2,1)S(1)} collective-permute-done((bf16[144,256]{1,0:T(8,128)(2,1)S(1)}, bf16[144,256]{1,0:T(8,128)(2,1)S(1)}, u32[]{:S(2)}, u32[]{:S(2)}) %collective-permute-start.5) | collective-permute-done | bytes 73760 | tf_op jit(solution)/shard_map/ppermute | solution.py:315
  142.8 2.0 %shard_map.124 = (bf16[128,1024]{1,0:T(8,128)(2,1)}, bf16[128,1024]{1,0:T(8,128)(2,1)}, f32[1,1024]{1,0:T(1,128)S(1)}) custom-call(s32[5]{0:T(128)S(1)} %pad_add_fusion.info, bf16[144,256]{1,0:T(8,128)(2,1)S(1)} %get-tuple-element.37.in0_ref, bf16[144,256]{1,0:T(8,128)(2,1)S(1)} %collective-permute-done.3.in1_ref, ...), custom_call_target="tpu_custom_call" | custom-call | flops 1 | tf_op jit(solution)/shard_map/pallas_call | solution.py:297
  144.8 0.0 collective-permute-done.6.other1_ref
  144.8 0.0 collective-permute-done.7.other2_ref
  144.8 1.2 shard_map.125
  146.0 9.9 %all-to-all-start.3 = ((bf16[4,384,256]{2,1,0:T(8,128)(2,1)}), bf16[4,384,256]{2,1,0:T(8,128)(2,1)S(1)}, u32[]{:S(2)}, u32[]{:S(2)}) async-start(bf16[4,384,256]{2,1,0:T(8,128)(2,1)} %shard_map.125), calls=%async_computation.3 | async-start | bytes 1572864 | tf_op jit(solution)/shard_map/all_to_all | solution.py:310
  155.8 1.9 collective-permute-start.8
  157.8 3.6 %collective-permute-done.8 = f32[1,1024]{1,0:T(1,128)S(1)} collective-permute-done((f32[1,1024]{1,0:T(1,128)S(1)}, f32[1,1024]{1,0:T(1,128)S(1)}, u32[]{:S(2)}, u32[]{:S(2)}) %collective-permute-start.8) | collective-permute-done | bytes 4128 | tf_op jit(solution)/shard_map/ppermute | solution.py:322
  161.3 6.5 %collective-permute-start.9 = (f32[1,1024]{1,0:T(1,128)S(1)}, f32[1,1024]{1,0:T(1,128)S(1)}, u32[]{:S(2)}, u32[]{:S(2)}) collective-permute-start(f32[1,1024]{1,0:T(1,128)S(1)} %add.22), channel_id=1, source_target_pairs={{0,4},{1,5},{2,6},{3,7},{4,0},{5,1},{6,2},{7,3},{8,12},{9,13},{10,... | collective-permute-start | bytes 12296 | tf_op jit(solution)/shard_map/ppermute | solution.py:322
  167.9 1.6 collective-permute-done.9
  169.5 1.9 collective-permute-start.10
  171.4 3.6 %collective-permute-done.10 = f32[1,1024]{1,0:T(1,128)S(1)} collective-permute-done((f32[1,1024]{1,0:T(1,128)S(1)}, f32[1,1024]{1,0:T(1,128)S(1)}, u32[]{:S(2)}, u32[]{:S(2)}) %collective-permute-start.10) | collective-permute-done | bytes 4128 | tf_op jit(solution)/shard_map/ppermute | solution.py:322
  175.0 1.9 collective-permute-start.11
  176.9 5.1 %collective-permute-done.11 = f32[1,1024]{1,0:T(1,128)S(1)} collective-permute-done((f32[1,1024]{1,0:T(1,128)S(1)}, f32[1,1024]{1,0:T(1,128)S(1)}, u32[]{:S(2)}, u32[]{:S(2)}) %collective-permute-start.11) | collective-permute-done | bytes 4128 | tf_op jit(solution)/shard_map/ppermute | solution.py:322
  182.0 5.6 %collective-permute-start.12 = (f32[1,1024]{1,0:T(1,128)S(1)}, f32[1,1024]{1,0:T(1,128)S(1)}, u32[]{:S(2)}, u32[]{:S(2)}) collective-permute-start(f32[1,1024]{1,0:T(1,128)S(1)} %add.25), channel_id=1, source_target_pairs={{0,8},{1,9},{2,10},{3,11},{4,12},{5,13},{6,14},{7,15},{8,0},{9,1},... | collective-permute-start | bytes 12296 | tf_op jit(solution)/shard_map/ppermute | solution.py:322
  187.6 2.0 collective-permute-done.12
  189.6 4.8 %collective-permute-start.13 = (f32[1,1024]{1,0:T(1,128)S(1)}, f32[1,1024]{1,0:T(1,128)S(1)}, u32[]{:S(2)}, u32[]{:S(2)}) collective-permute-start(f32[1,1024]{1,0:T(1,128)S(1)} %add.26), channel_id=1, source_target_pairs={{0,16},{1,17},{2,18},{3,19},{4,20},{5,21},{6,22},{7,23},{8,24},{9,... | collective-permute-start | bytes 12296 | tf_op jit(solution)/shard_map/ppermute | solution.py:322
  194.4 1.8 collective-permute-done.13
  196.2 0.6 div.3
  196.8 0.0 all-to-all-done.3.in_ref
  196.8 1.0 shard_map.126
  (7 shorter events, 0.0 us)
Async XLA Ops:
  0.6 1.0 copy-start.3
  1.6 0.9 copy-start.4
  3.4 15.2 %copy-start = (bf16[1,128,1024]{2,1,0:T(8,128)(2,1)S(1)}, bf16[1,128,1024]{2,1,0:T(8,128)(2,1)}, u32[]{:S(2)}) copy-start(bf16[1,128,1024]{2,1,0:T(8,128)(2,1)} %param.10) | copy-start | bytes 786436
  3.4 15.2 %copy-start.1 = (bf16[1,128,1024]{2,1,0:T(8,128)(2,1)S(1)}, bf16[1,128,1024]{2,1,0:T(8,128)(2,1)}, u32[]{:S(2)}) copy-start(bf16[1,128,1024]{2,1,0:T(8,128)(2,1)} %param.13) | copy-start | bytes 786436
  3.4 15.2 %copy-start.2 = (bf16[1,128,1024]{2,1,0:T(8,128)(2,1)S(1)}, bf16[1,128,1024]{2,1,0:T(8,128)(2,1)}, u32[]{:S(2)}) copy-start(bf16[1,128,1024]{2,1,0:T(8,128)(2,1)} %param.7) | copy-start | bytes 786436
  3.4 41.1 %all-to-all-start.1 = ((bf16[4,256,256]{2,1,0:T(8,128)(2,1)}), bf16[4,256,256]{2,1,0:T(8,128)(2,1)S(1)}, u32[]{:S(2)}, u32[]{:S(2)}) async-start(bf16[4,256,256]{2,1,0:T(8,128)(2,1)} %shard_map.119), calls=%async_computation.1 | async-start | bytes 1048576 | tf_op jit(solution)/shard_map/all_to_all | solution.py:310
  18.6 0.7 copy-start.5
  44.5 28.9 %all-to-all-start = ((bf16[4,256,256]{2,1,0:T(8,128)(2,1)}), bf16[4,256,256]{2,1,0:T(8,128)(2,1)S(1)}, u32[]{:S(2)}, u32[]{:S(2)}) async-start(bf16[4,256,256]{2,1,0:T(8,128)(2,1)} %shard_map.118), calls=%async_computation | async-start | bytes 1048576 | tf_op jit(solution)/shard_map/all_to_all | solution.py:310
  54.0 19.5 %collective-permute-start.1 = (bf16[4,256,256]{2,1,0:T(8,128)(2,1)S(1)}, bf16[4,256,256]{2,1,0:T(8,128)(2,1)S(1)}, u32[]{:S(2)}, u32[]{:S(2)}) collective-permute-start(bf16[4,256,256]{2,1,0:T(8,128)(2,1)S(1)} %all-to-all-done.1.kv0_ref), channel_id=1, source_target_pairs={{0,128},{32,160},{64,192},{96,224},{128,256},{160,288},{192,320},{... | collective-permute-start | bytes 1572872 | tf_op jit(solution)/shard_map/ppermute | solution.py:329
  55.3 18.2 %collective-permute-start = (bf16[4,256,256]{2,1,0:T(8,128)(2,1)S(1)}, bf16[4,256,256]{2,1,0:T(8,128)(2,1)S(1)}, u32[]{:S(2)}, u32[]{:S(2)}) collective-permute-start(bf16[4,256,256]{2,1,0:T(8,128)(2,1)S(1)} %all-to-all-done.1.kv0_ref), channel_id=1, source_target_pairs={{0,256},{32,288},{64,320},{96,352},{128,384},{160,416},{192,448},{... | collective-permute-start | bytes 1572872 | tf_op jit(solution)/shard_map/ppermute | solution.py:329
  56.6 0.7 copy-start.6
  110.0 34.8 %collective-permute-start.6 = (bf16[4,256,256]{2,1,0:T(8,128)(2,1)S(1)}, bf16[4,256,256]{2,1,0:T(8,128)(2,1)S(1)}, u32[]{:S(2)}, u32[]{:S(2)}) collective-permute-start(bf16[4,256,256]{2,1,0:T(8,128)(2,1)S(1)} %get-tuple-element.34), channel_id=1, source_target_pairs={{128,0},{160,32},{192,64},{224,96},{256,128},{288,160},{320,192},{... | collective-permute-start | bytes 1572872 | tf_op jit(solution)/shard_map/ppermute | solution.py:329
  111.4 33.4 %collective-permute-start.7 = (bf16[4,256,256]{2,1,0:T(8,128)(2,1)S(1)}, bf16[4,256,256]{2,1,0:T(8,128)(2,1)S(1)}, u32[]{:S(2)}, u32[]{:S(2)}) collective-permute-start(bf16[4,256,256]{2,1,0:T(8,128)(2,1)S(1)} %get-tuple-element.45), channel_id=1, source_target_pairs={{256,0},{288,32},{320,64},{352,96},{384,128},{416,160},{448,192},{... | collective-permute-start | bytes 1572872 | tf_op jit(solution)/shard_map/ppermute | solution.py:329
  112.7 3.0 %collective-permute-start.2 = (f32[2,128]{1,0:T(2,128)S(1)}, f32[2,128]{1,0:T(2,128)S(1)}, u32[]{:S(2)}, u32[]{:S(2)}) collective-permute-start(f32[2,128]{1,0:T(2,128)S(1)} %get-tuple-element.35), channel_id=1, source_target_pairs={{0,1},{1,0},{2,3},{3,2},{4,5},{5,4},{6,7},{7,6},{8,9},{9,8},{10,11... | collective-permute-start | bytes 3080 | tf_op jit(solution)/shard_map/ppermute | solution.py:322
  119.5 12.2 %collective-permute-start.3 = (bf16[144,256]{1,0:T(8,128)(2,1)S(1)}, bf16[144,256]{1,0:T(8,128)(2,1)S(1)}, u32[]{:S(2)}, u32[]{:S(2)}) collective-permute-start(bf16[144,256]{1,0:T(8,128)(2,1)S(1)} %get-tuple-element.38), channel_id=1, source_target_pairs={{0,32},{32,64},{64,96},{96,0},{128,160},{160,192},{192,224},{224,1... | collective-permute-start | bytes 221192 | tf_op jit(solution)/shard_map/ppermute | solution.py:315
  122.0 15.4 %collective-permute-start.4 = (bf16[144,256]{1,0:T(8,128)(2,1)S(1)}, bf16[144,256]{1,0:T(8,128)(2,1)S(1)}, u32[]{:S(2)}, u32[]{:S(2)}) collective-permute-start(bf16[144,256]{1,0:T(8,128)(2,1)S(1)} %get-tuple-element.39), channel_id=1, source_target_pairs={{0,64},{32,96},{64,0},{96,32},{128,192},{160,224},{192,128},{224,1... | collective-permute-start | bytes 221192 | tf_op jit(solution)/shard_map/ppermute | solution.py:315
  129.3 13.5 %collective-permute-start.5 = (bf16[144,256]{1,0:T(8,128)(2,1)S(1)}, bf16[144,256]{1,0:T(8,128)(2,1)S(1)}, u32[]{:S(2)}, u32[]{:S(2)}) collective-permute-start(bf16[144,256]{1,0:T(8,128)(2,1)S(1)} %get-tuple-element.40), channel_id=1, source_target_pairs={{0,96},{32,0},{64,32},{96,64},{128,224},{160,128},{192,160},{224,1... | collective-permute-start | bytes 221192 | tf_op jit(solution)/shard_map/ppermute | solution.py:315
  146.0 50.9 %all-to-all-start.3 = ((bf16[4,384,256]{2,1,0:T(8,128)(2,1)}), bf16[4,384,256]{2,1,0:T(8,128)(2,1)S(1)}, u32[]{:S(2)}, u32[]{:S(2)}) async-start(bf16[4,384,256]{2,1,0:T(8,128)(2,1)} %shard_map.125), calls=%async_computation.3 | async-start | bytes 1572864 | tf_op jit(solution)/shard_map/all_to_all | solution.py:310
  155.8 5.5 %collective-permute-start.8 = (f32[1,1024]{1,0:T(1,128)S(1)}, f32[1,1024]{1,0:T(1,128)S(1)}, u32[]{:S(2)}, u32[]{:S(2)}) collective-permute-start(f32[1,1024]{1,0:T(1,128)S(1)} %get-tuple-element.51), channel_id=1, source_target_pairs={{0,2},{1,3},{2,0},{3,1},{4,6},{5,7},{6,4},{7,5},{8,10},{9,11},{10,... | collective-permute-start | bytes 12296 | tf_op jit(solution)/shard_map/ppermute | solution.py:322
  161.3 8.1 %collective-permute-start.9 = (f32[1,1024]{1,0:T(1,128)S(1)}, f32[1,1024]{1,0:T(1,128)S(1)}, u32[]{:S(2)}, u32[]{:S(2)}) collective-permute-start(f32[1,1024]{1,0:T(1,128)S(1)} %add.22), channel_id=1, source_target_pairs={{0,4},{1,5},{2,6},{3,7},{4,0},{5,1},{6,2},{7,3},{8,12},{9,13},{10,... | collective-permute-start | bytes 12296 | tf_op jit(solution)/shard_map/ppermute | solution.py:322
  169.5 5.5 %collective-permute-start.10 = (f32[1,1024]{1,0:T(1,128)S(1)}, f32[1,1024]{1,0:T(1,128)S(1)}, u32[]{:S(2)}, u32[]{:S(2)}) collective-permute-start(f32[1,1024]{1,0:T(1,128)S(1)} %add.23), channel_id=1, source_target_pairs={{0,128},{32,160},{64,192},{96,224},{128,0},{160,32},{192,64},{224,... | collective-permute-start | bytes 12296 | tf_op jit(solution)/shard_map/ppermute | solution.py:322
  175.0 7.0 %collective-permute-start.11 = (f32[1,1024]{1,0:T(1,128)S(1)}, f32[1,1024]{1,0:T(1,128)S(1)}, u32[]{:S(2)}, u32[]{:S(2)}) collective-permute-start(f32[1,1024]{1,0:T(1,128)S(1)} %add.24), channel_id=1, source_target_pairs={{0,256},{32,288},{64,320},{96,352},{128,384},{160,416},{192,448},{... | collective-permute-start | bytes 12296 | tf_op jit(solution)/shard_map/ppermute | solution.py:322
  182.0 7.6 %collective-permute-start.12 = (f32[1,1024]{1,0:T(1,128)S(1)}, f32[1,1024]{1,0:T(1,128)S(1)}, u32[]{:S(2)}, u32[]{:S(2)}) collective-permute-start(f32[1,1024]{1,0:T(1,128)S(1)} %add.25), channel_id=1, source_target_pairs={{0,8},{1,9},{2,10},{3,11},{4,12},{5,13},{6,14},{7,15},{8,0},{9,1},... | collective-permute-start | bytes 12296 | tf_op jit(solution)/shard_map/ppermute | solution.py:322
  189.6 6.6 %collective-permute-start.13 = (f32[1,1024]{1,0:T(1,128)S(1)}, f32[1,1024]{1,0:T(1,128)S(1)}, u32[]{:S(2)}, u32[]{:S(2)}) collective-permute-start(f32[1,1024]{1,0:T(1,128)S(1)} %add.26), channel_id=1, source_target_pairs={{0,16},{1,17},{2,18},{3,19},{4,20},{5,21},{6,22},{7,23},{8,24},{9,... | collective-permute-start | bytes 12296 | tf_op jit(solution)/shard_map/ppermute | solution.py:322

commit v3 on v2

--- a/solution.py
+++ b/solution.py
@@ -43,9 +43,9 @@
     return slice(head * HEAD, (head + 1) * HEAD)
 
 
-def tile_rows(ref, tile, first, head):
-    block = ref[pl.ds(tile * 2, 2), first : first + ROWS, head_cols(head)]
-    return block.reshape(TILE, HEAD)
+def tile_rows(ref, tile, first, head, tiles=1):
+    block = ref[pl.ds(tile * 2, 2 * tiles), first : first + ROWS, head_cols(head)]
+    return block.reshape(tiles * TILE, HEAD)
 
 
 def eye():
@@ -60,11 +60,21 @@
     return jnp.sum(jnp.where(eye(), row, 0.0), axis=1, keepdims=True)
 
 
-def pack_kv_kernel(k_ref, v_ref, out_ref):
+def pack_kv_kernel(k_ref, v_ref, out_ref, sems):
+    copies = []
     for z in range(ZS):
-        cols = slice(z * PAIR, (z + 1) * PAIR)
-        out_ref[z, 0:ROWS, :] = k_ref[:, cols]
-        out_ref[z, ROWS : 2 * ROWS, :] = v_ref[:, cols]
+        for part, ref in enumerate((k_ref, v_ref)):
+            copies.append(
+                pltpu.make_async_copy(
+                    ref.at[:, z * PAIR : (z + 1) * PAIR],
+                    out_ref.at[z, part * ROWS : (part + 1) * ROWS, :],
+                    sems.at[2 * z + part],
+                )
+            )
+    for copy in copies:
+        copy.start()
+    for copy in copies:
+        copy.wait()
 
 
 def pack_q_kernel(q_ref, gates_ref, grad_ref, gain_ref, out_ref):
@@ -75,39 +85,59 @@
         out_ref[z, ROWS : 2 * ROWS, :] = dnorm.astype(BF16)
 
 
-def key_tiles(info, tile, back):
+def over_keys(info, tile, back, step, total):
+    if back == 0:
+        return step(0, tile + 1, total)
     block = info[0] // ZS
     first, _ = bounds(block * BLOCK + tile * TILE, info)
-    low = jnp.maximum(first // TILE - 2 * (block - back), 0)
-    return low, (tile + 1 if back == 0 else 2)
-
-
-def forward_kernel(info, qd_ref, kv0_ref, kv1_ref, kv2_ref, att_ref, stats_ref):
+    low = jnp.clip(first // TILE - 2 * (block - back), 0, 2)
+    return lax.switch(
+        low, [lambda t: step(0, 2, t), lambda t: step(1, 1, t), lambda t: t], total
+    )
+
+
+def forward_tiles(info, tile, backs, qd_ref, kv_refs, total):
     scale = 0.5 / math.sqrt(HEAD)
     block = info[0] // ZS
-    where = iota((1, TILE), 1)
+    q = [tile_rows(qd_ref, tile, 0, head) for head in range(2)]
+    pos = block * BLOCK + tile * TILE + iota((TILE, 1), 0)
+    start, _ = bounds(pos, info)
+    for back, kv_ref in zip(backs, kv_refs):
+
+        def step(key_tile, tiles, total, back=back, kv_ref=kv_ref):
+            base = (block - back) * BLOCK + key_tile * TILE
+            where = iota((1, tiles * TILE), 1)
+            allowed = (where >= start - base) & (where <= pos - base)
+            sums = []
+            for head in range(2):
+                k = tile_rows(kv_ref, key_tile, 0, head, tiles)
+                v = tile_rows(kv_ref, key_tile, ROWS, head, tiles)
+                half_score = dot(q[head], k, ((1,), (1,))) * scale
+                silu = half_score + half_score * jnp.tanh(half_score)
+                probs = jnp.where(allowed, silu, 0.0).astype(BF16)
+                sums.append(total[head] + dot(probs, v, ((1,), (0,))))
+            return tuple(sums)
+
+        total = over_keys(info, tile, back, step, total)
+    return total
+
+
+def forward_own_kernel(info, qd_ref, kv0_ref, sum_ref):
     for tile in range(2):
-        q = [tile_rows(qd_ref, tile, 0, head) for head in range(2)]
-        pos = block * BLOCK + tile * TILE + iota((TILE, 1), 0)
-        start, length = bounds(pos, info)
         total = (jnp.zeros((TILE, HEAD), F32),) * 2
-        for back, kv_ref in enumerate((kv0_ref, kv1_ref, kv2_ref)):
-
-            def step(key_tile, total):
-                base = (block - back) * BLOCK + key_tile * TILE
-                allowed = (where >= start - base) & (where <= pos - base)
-                sums = []
-                for head in range(2):
-                    k = tile_rows(kv_ref, key_tile, 0, head)
-                    v = tile_rows(kv_ref, key_tile, ROWS, head)
-                    half_score = dot(q[head], k, ((1,), (1,))) * scale
-                    silu = half_score + half_score * jnp.tanh(half_score)
-                    probs = jnp.where(allowed, silu, 0.0).astype(BF16)
-                    sums.append(total[head] + dot(probs, v, ((1,), (0,))))
-                return tuple(sums)
-
-            low, high = key_tiles(info, tile, back)
-            total = lax.fori_loop(low, high, step, total)
+        total = forward_tiles(info, tile, (0,), qd_ref, (kv0_ref,), total)
+        for head in range(2):
+            sum_ref[tile * TILE : (tile + 1) * TILE, head_cols(head)] = total[head]
+
+
+def forward_kernel(info, qd_ref, kv1_ref, kv2_ref, sum_ref, att_ref, stats_ref):
+    block = info[0] // ZS
+    for tile in range(2):
+        total = tuple(
+            sum_ref[tile * TILE : (tile + 1) * TILE, head_cols(head)] for head in range(2)
+        )
+        total = forward_tiles(info, tile, (1, 2), qd_ref, (kv1_ref, kv2_ref), total)
+        _, length = bounds(block * BLOCK + tile * TILE + iota((TILE, 1), 0), info)
         inverse = 1.0 / length.astype(F32)
         attended = [part * inverse for part in total]
         dnorm = [tile_rows(qd_ref, tile, ROWS, head).astype(F32) for head in range(2)]
@@ -133,7 +163,7 @@
 
 
 def norm_kernel(info, in0_ref, in1_ref, in2_ref, in3_ref, *refs):
-    gates_ref, grad_ref, gain_ref, out_ref, gate_grad_ref, gain_sum_ref = refs
+    gates_ref, grad_ref, gain_ref, out_ref, gate_grad_ref = refs
     width = H * HEAD
     heads = [(by, ref, head) for by, ref in enumerate((in0_ref, in1_ref, in2_ref, in3_ref)) for head in range(2)]
     attended = []
@@ -149,8 +179,13 @@
         scaled = block * rstd * gain_ref[0:1, cols]
         out_ref[:, cols] = (scaled * gates_ref[:, cols].astype(F32)).astype(BF16)
         gate_grad_ref[:, cols] = (scaled * grad_ref[:, cols].astype(F32)).astype(BF16)
-        three = ref[ROWS : ROWS + EXTRA, head_cols(head)].astype(F32)
-        gain_sum_ref[0:1, cols] = three[1:2] + three[2:3] + three[3:4]
+
+
+def gain_kernel(info, in0_ref, in1_ref, in2_ref, in3_ref, sum_ref):
+    for by, ref in enumerate((in0_ref, in1_ref, in2_ref, in3_ref)):
+        for head in range(2):
+            three = ref[ROWS : ROWS + EXTRA, head_cols(head)].astype(F32)
+            sum_ref[0:1, part_cols(info, by, head)] = three[1:2] + three[2:3] + three[3:4]
 
 
 def make_grad_att(info, qd_ref, att_ref, stats_ref, grad_ref, gain_ref):
@@ -184,7 +219,7 @@
         gain_ref[head : head + 1, :] = sums[head]
 
 
-def make_back(info, att_ref, gain_ref, back_refs):
+def back_kernel(info, att_ref, gain_ref, *back_refs):
     index = iota((EXTRA, HEAD), 0)
     for head in range(2):
         cols = head_cols(head)
@@ -205,7 +240,6 @@
 def backward_tiles(info, back, q_ref, kv_ref, grad_ref, dq_ref, dkv_ref):
     scale = 0.5 / math.sqrt(HEAD)
     block = info[0] // ZS
-    where = iota((TILE, 1), 0)
     dkv_ref[...] = jnp.zeros_like(dkv_ref)
     for tile in range(2):
         q = [tile_rows(q_ref, tile, 0, head) for head in range(2)]
@@ -214,13 +248,14 @@
         start, _ = bounds(pos, info)
         here = slice(tile * TILE, (tile + 1) * TILE)
 
-        def step(key_tile, total):
+        def step(key_tile, tiles, total):
             base = (block - back) * BLOCK + key_tile * TILE
+            where = iota((tiles * TILE, 1), 0)
             allowed = (where >= start - base) & (where <= pos - base)
             sums = []
             for head in range(2):
-                k = tile_rows(kv_ref, key_tile, 0, head)
-                v = tile_rows(kv_ref, key_tile, ROWS, head)
+                k = tile_rows(kv_ref, key_tile, 0, head, tiles)
+                v = tile_rows(kv_ref, key_tile, ROWS, head, tiles)
                 half_score = dot(k, q[head], ((1,), (1,))) * scale
                 grad_probs = dot(v, grad[head], ((1,), (1,)))
                 tanh = jnp.tanh(half_score)
@@ -228,17 +263,16 @@
                 probs = jnp.where(allowed, half_score * twice, 0.0).astype(BF16)
                 slope = twice * (1.0 + half_score * (1.0 - tanh))
                 grad_scores = jnp.where(allowed, grad_probs * slope, 0.0).astype(BF16)
-                slots = pl.ds(key_tile * 2, 2)
-                dk = dot(grad_scores, q[head], ((1,), (0,))).reshape(2, ROWS, HEAD)
-                dv = dot(probs, grad[head], ((1,), (0,))).reshape(2, ROWS, HEAD)
+                slots = pl.ds(key_tile * 2, 2 * tiles)
+                dk = dot(grad_scores, q[head], ((1,), (0,))).reshape(2 * tiles, ROWS, HEAD)
+                dv = dot(probs, grad[head], ((1,), (0,))).reshape(2 * tiles, ROWS, HEAD)
                 dkv_ref[slots, 0:ROWS, head_cols(head)] += dk
                 dkv_ref[slots, ROWS : 2 * ROWS, head_cols(head)] += dv
                 sums.append(total[head] + dot(grad_scores, k, ((0,), (0,))))
             return tuple(sums)
 
-        low, high = key_tiles(info, tile, back)
         total = tuple(dq_ref[here, head_cols(head)] for head in range(2))
-        total = lax.fori_loop(low, high, step, total)
+        total = over_keys(info, tile, back, step, total)
         for head in range(2):
             dq_ref[here, head_cols(head)] = total[head]
 
@@ -265,8 +299,7 @@
     send_sums(dkv_ref, send_ref)
 
 
-def backward_own_kernel(info, qd_ref, kv0_ref, grad_ref, att_ref, gain_ref, dq_in_ref, dq_ref, dkv_ref, *back_refs):
-    make_back(info, att_ref, gain_ref, back_refs)
+def backward_own_kernel(info, qd_ref, kv0_ref, grad_ref, dq_in_ref, dq_ref, dkv_ref):
     dq_ref[...] = dq_in_ref[...]
     backward_tiles(info, 0, qd_ref, kv0_ref, grad_ref, dq_ref, dkv_ref)
 
@@ -283,7 +316,8 @@
         out_ref[slot, 2 * ROWS : 3 * ROWS, :] = dq.astype(BF16)
 
 
-def unpack_kernel(in_ref, dq_ref, dk_ref, dv_ref):
+def unpack_kernel(in_ref, gain_sum_ref, gain_ref, dq_ref, dk_ref, dv_ref, grad_gain_ref):
+    grad_gain_ref[...] = gain_sum_ref[...] / gain_ref[...]
     for z in range(ZS):
         cols = slice(z * PAIR, (z + 1) * PAIR)
         dk_ref[:, cols] = in_ref[z, 0:ROWS, :]
@@ -291,9 +325,9 @@
         dq_ref[:, cols] = in_ref[z, 2 * ROWS : 3 * ROWS, :]
 
 
-def call(kernel, outs, *args, scalars=0, scratch=(), flops=1):
+def call(kernel, outs, *args, scalars=0, scratch=(), flops=1, space=pltpu.VMEM):
     specs = [pl.BlockSpec(memory_space=pltpu.SMEM)] * scalars
-    specs += [pl.BlockSpec(memory_space=pltpu.VMEM)] * (len(args) - scalars)
+    specs += [pl.BlockSpec(memory_space=space)] * (len(args) - scalars)
     return pl.pallas_call(
         kernel,
         out_shape=outs,
@@ -315,12 +349,22 @@
     return lax.ppermute(array, "seq", pairs)
 
 
-def add_over(array, axis, bits):
+def add_over(array, axis, low):
     size = lax.axis_size(axis)
-    for bit in bits:
-        if bit < size:
-            array = array + lax.ppermute(array, axis, [(i, i ^ bit) for i in range(size)])
-    return array
+    if 2 * low >= size:
+        return array
+    others = [
+        lax.ppermute(array, axis, [(i, i ^ bits) for i in range(size)])
+        for bits in (low, 2 * low, 3 * low)
+    ]
+    return (array + others[0]) + (others[1] + others[2])
+
+
+def add_pairs(array, axis):
+    size = lax.axis_size(axis)
+    if size == 1:
+        return array
+    return array + lax.ppermute(array, axis, [(i, i ^ 1) for i in range(size)])
 
 
 def shift_y(array, by):
@@ -339,20 +383,28 @@
     block = shape((BLOCK, PAIR), F32)
     sums_scratch = [pltpu.VMEM(pair_sums.shape, F32)]
 
-    (kv,) = call(pack_kv_kernel, [pair], keys[0], values[0])
+    (kv,) = call(
+        pack_kv_kernel,
+        [pair],
+        keys[0],
+        values[0],
+        space=pltpu.HBM,
+        scratch=[pltpu.SemaphoreType.DMA((2 * ZS,))],
+    )
     kv0 = along_z(kv)
     kv2 = shift_y(kv0, 2)
     kv1 = shift_y(kv0, 1)
     (qd,) = call(pack_q_kernel, [pair], queries[0], gates[0], grad_out[0], gain[None])
     qd = along_z(qd)
+    (own_sum,) = call(forward_own_kernel, [block], info, qd, kv0, scalars=1)
     attended, stats = call(
         forward_kernel,
         [block, shape((ZS, 4 * ZS, ROWS), F32)],
         info,
         qd,
-        kv0,
         kv1,
         kv2,
+        own_sum,
         scalars=1,
     )
     stats = along_z(stats)
@@ -381,25 +433,25 @@
     )
     from1 = shift_y(to1, -1)
     gain_sum, to1 = lax.optimization_barrier((gain_sum, to1))
-    gain_sum = add_over(gain_sum, "own", (1,))
-    dq, dkv, *back = call(
-        backward_own_kernel,
-        [block, pair_sums] + [shape((ROWS + EXTRA, PAIR), BF16)] * ZS,
+    back = call(
+        back_kernel,
+        [shape((ROWS + EXTRA, PAIR), BF16)] * ZS,
         info,
-        qd,
-        kv0,
-        grad_att,
         attended,
         gain_sum,
-        dq,
         scalars=1,
     )
+    back = list(back)
     back[2] = shift_z(back[2], 2)
     back[1] = shift_z(back[1], 1)
     back[3] = shift_z(back[3], 3)
-    output, grad_gate, gain_sum = call(
+    dq, dkv = call(
+        backward_own_kernel, [block, pair_sums], info, qd, kv0, grad_att, dq, scalars=1
+    )
+    (gain_sum,) = call(gain_kernel, [shape((1, width), F32)], info, *back, scalars=1)
+    output, grad_gate = call(
         norm_kernel,
-        [shape((rows, width), BF16)] * 2 + [shape((1, width), F32)],
+        [shape((rows, width), BF16)] * 2,
         info,
         *back,
         gates[0],
@@ -409,12 +461,16 @@
     )
     (joined,) = call(join_kernel, [shape((ZS, 3 * ROWS, PAIR), BF16)], dq, dkv, from1, from2)
     gain_sum, joined = lax.optimization_barrier((gain_sum, joined))
-    gain_sum = add_over(add_over(add_over(gain_sum, "own", (2, 4)), "seq", (4, 8)), "own", (8, 16))
-    grad_gain = gain_sum.reshape(width) / gain
-    grad_q, grad_k, grad_v = call(
-        unpack_kernel, [shape((rows, width), BF16)] * 3, along_z(joined)
-    )
-    return (output[None], grad_q[None], grad_k[None], grad_v[None], grad_gate[None], grad_gain)
+    gain_sum = add_pairs(gain_sum, "own")
+    gain_sum = add_over(add_over(add_over(gain_sum, "own", 2), "seq", 4), "own", 8)
+    grad_q, grad_k, grad_v, grad_gain = call(
+        unpack_kernel,
+        [shape((rows, width), BF16)] * 3 + [shape((1, width), F32)],
+        along_z(joined),
+        gain_sum,
+        gain[None],
+    )
+    return (output[None], grad_q[None], grad_k[None], grad_v[None], grad_gate[None], grad_gain[0])
 
 
 def solution(mesh):

time: 201 us -> 195 us (0.970)
  waiting for transfers between devices: 70.2 us -> 59.3 us
  starting transfers between devices: 76.5 us -> 84.4 us
    ppermute x7 -> x10, waiting for transfers between devices: 18.7 us -> 7.53 us  [the longest x9 6.4 us: add_over(): lax.ppermute(array, axis, [(i, i ^ bits) for i in range(size)])]
    ppermute x7 -> x10, starting transfers between devices: 24.6 us -> 33.7 us  [the longest x9 31.7 us: add_over(): lax.ppermute(array, axis, [(i, i ^ bits) for i in range(size)])]
    all_to_all x3, starting transfers between devices: 34.5 us -> 28.2 us  [along_z(): lax.all_to_all(array, 'seq', 0, 0, axis_index_groups=groups, tiled=True)]
    ppermute x4, starting transfers between devices: 5.22 us -> 10.5 us  [shift_y(): return lax.ppermute(array, 'seq', pairs)]
    pallas_call x9 -> x12, Pallas kernels: 20.9 us -> 19.2 us  [call(): pl.pallas_call(kernel, out_shape=outs, in_specs=specs, out_specs=[pl.Bloc...]
  transfers between devices with their start and end apart: 17 -> 20, of which waited for: 11 -> 9; matrix products, arithmetic and copies ran while one was open for 0% -> 0% of each run, Pallas kernels for 3% -> 4%
where the time goes in v3:
time: 195 us; the launch traced here: 193 us
  starting transfers between devices  84.4 us (43%)
  waiting for transfers between devices  59.3 us (30%)
  blocking collectives  25.2 us (13%)
  Pallas kernels  19.2 us (10%)
  local copies, waits for them, and re-layouts  3.23 us (2%)
    all_to_all x3, waiting for transfers between devices, along_z(): lax.all_to_all(array, 'seq', 0, 0, axis_index_groups=groups, tiled=True)  40.3 us
    ppermute x9, starting transfers between devices, add_over(): lax.ppermute(array, axis, [(i, i ^ bits) for i in range(size)])  31.7 us
    all_to_all x3, starting transfers between devices, along_z(): lax.all_to_all(array, 'seq', 0, 0, axis_index_groups=groups, tiled=True)  28.2 us
    all_to_all x1, blocking collectives, along_z(): lax.all_to_all(array, 'seq', 0, 0, axis_index_groups=groups, tiled=True)  25.2 us
    pallas_call x12, Pallas kernels, call(): pl.pallas_call(kernel, out_shape=outs, in_specs=specs, out_specs=[pl.Bloc...  19.2 us
    ppermute x3, starting transfers between devices, shift_z(): return lax.ppermute(array, 'seq', pairs)  12.1 us
    ppermute x3, waiting for transfers between devices, shift_z(): return lax.ppermute(array, 'seq', pairs)  11.5 us
    ppermute x4, starting transfers between devices, shift_y(): return lax.ppermute(array, 'seq', pairs)  10.5 us
  transfers between devices with their start and end apart: 20, of which 9 were waited for; matrix products, arithmetic and copies ran while one was open for 0% of the time, Pallas kernels for 4%

profile of v3, /device:TPU:24, one launch (start us, length us, event | category | flops | bytes accessed | tf_op | source)
XLA Modules:
  0.0 192.7 jit_solution(14932375361991692238)
XLA Ops:
  0.6 0.9 copy-done.3
  1.6 0.9 copy-done.4
  2.5 1.0 shard_map.119
  3.5 0.0 copy-start
  3.5 0.0 copy-start.1
  3.5 0.0 copy-start.2
  3.5 15.2 %all-to-all-start.1 = ((bf16[4,256,256]{2,1,0:T(8,128)(2,1)}), bf16[4,256,256]{2,1,0:T(8,128)(2,1)S(1)}, u32[]{:S(2)}, u32[]{:S(2)}) async-start(bf16[4,256,256]{2,1,0:T(8,128)(2,1)} %shard_map.119), calls=%async_computation.1 | async-start | bytes 1048576 | tf_op jit(solution)/shard_map/all_to_all | solution.py:344
  18.8 0.0 copy-done.2
  18.8 0.7 copy-done.5
  19.4 0.9 shard_map.118
  20.3 24.4 %all-to-all-done.1.kv0_ref = bf16[4,256,256]{2,1,0:T(8,128)(2,1)S(1)} async-done(((bf16[4,256,256]{2,1,0:T(8,128)(2,1)}), bf16[4,256,256]{2,1,0:T(8,128)(2,1)S(1)}, u32[]{:S(2)}, u32[]{:S(2)}) %all-to-all-start.1) | async-done | bytes 524320 | tf_op jit(solution)/shard_map/all_to_all | solution.py:344
  44.7 9.4 %all-to-all-start = ((bf16[4,256,256]{2,1,0:T(8,128)(2,1)}), bf16[4,256,256]{2,1,0:T(8,128)(2,1)S(1)}, u32[]{:S(2)}, u32[]{:S(2)}) async-start(bf16[4,256,256]{2,1,0:T(8,128)(2,1)} %shard_map.118), calls=%async_computation | async-start | bytes 1048576 | tf_op jit(solution)/shard_map/all_to_all | solution.py:344
  54.1 1.3 collective-permute-start.1
  55.4 1.3 collective-permute-start
  56.7 0.0 copy-start.6
  56.7 0.6 copy-done.6
  57.4 0.2 reduce-window.9
  57.6 0.1 pad_add_fusion.info
  57.6 16.0 %all-to-all-done.qd_ref = bf16[4,256,256]{2,1,0:T(8,128)(2,1)S(1)} async-done(((bf16[4,256,256]{2,1,0:T(8,128)(2,1)}), bf16[4,256,256]{2,1,0:T(8,128)(2,1)S(1)}, u32[]{:S(2)}, u32[]{:S(2)}) %all-to-all-start) | async-done | bytes 524320 | tf_op jit(solution)/shard_map/all_to_all | solution.py:344
  73.6 1.6 shard_map.120.sum_ref
  75.3 0.0 collective-permute-done.1.kv2_ref
  75.3 0.0 collective-permute-done.kv1_ref
  75.3 3.1 %shard_map.121 = (f32[512,256]{1,0:T(8,128)S(1)}, f32[4,16,128]{2,1,0:T(8,128)S(1)}) custom-call(s32[5]{0:T(128)S(1)} %pad_add_fusion.info, bf16[4,256,256]{2,1,0:T(8,128)(2,1)S(1)} %all-to-all-done.qd_ref, bf16[4,256,256]{2,1,0:T(8,128)(2,1)S(1)} %collective-permute-done.kv1_ref, bf16[4,256,256]{2,1,0:T(8,128)(2,1)S(1)} %collective-permute-done.1.kv2_ref, ...), custom_call_target="tpu_custom_call" | custom-call | flops 1 | tf_op jit(solution)/shard_map/pallas_call | solution.py:331
  78.4 25.2 %all_to_all.20.stats_ref = f32[4,16,128]{2,1,0:T(8,128)S(1)} all-to-all(f32[4,16,128]{2,1,0:T(8,128)S(1)} %get-tuple-element.30), channel_id=1, replica_groups={{0,32,64,96},{128,160,192,224},{256,288,320,352},{384,416,448,480},{1,3..., dimensions={0} | all-to-all | bytes 65536 | tf_op jit(solution)/shard_map/all_to_all | solution.py:344
  103.6 1.3 shard_map.122
  104.9 3.6 %shard_map.123 = (bf16[4,256,256]{2,1,0:T(8,128)(2,1)S(1)}, f32[512,256]{1,0:T(8,128)S(1)}) custom-call(s32[5]{0:T(128)S(1)} %pad_add_fusion.info, bf16[4,256,256]{2,1,0:T(8,128)(2,1)S(1)} %all-to-all-done.qd_ref, bf16[4,256,256]{2,1,0:T(8,128)(2,1)S(1)} %collective-permute-done.kv1_ref, bf16[4,128,256]{2,1,0:T(8,128)(2,1)S(1)} %get-tuple-element.32.grad_ref, ...), custom_call_target="tpu_custom_call" | custom-call | flops 1 | tf_op jit(solution)/shard_map/pallas_call | solution.py:331
  108.5 1.3 collective-permute-start.5
  109.9 6.6 %collective-permute-start.6 = (bf16[4,256,256]{2,1,0:T(8,128)(2,1)S(1)}, bf16[4,256,256]{2,1,0:T(8,128)(2,1)S(1)}, u32[]{:S(2)}, u32[]{:S(2)}) collective-permute-start(bf16[4,256,256]{2,1,0:T(8,128)(2,1)S(1)} %get-tuple-element.44), channel_id=1, source_target_pairs={{256,0},{288,32},{320,64},{352,96},{384,128},{416,160},{448,192},{... | collective-permute-start | bytes 1572872 | tf_op jit(solution)/shard_map/ppermute | solution.py:373
  116.4 0.8 shard_map.124
  117.2 2.5 %collective-permute-start.2 = (bf16[144,256]{1,0:T(8,128)(2,1)S(1)}, bf16[144,256]{1,0:T(8,128)(2,1)S(1)}, u32[]{:S(2)}, u32[]{:S(2)}) collective-permute-start(bf16[144,256]{1,0:T(8,128)(2,1)S(1)} %get-tuple-element.37), channel_id=1, source_target_pairs={{0,32},{32,64},{64,96},{96,0},{128,160},{160,192},{192,224},{224,1... | collective-permute-start | bytes 221192 | tf_op jit(solution)/shard_map/ppermute | solution.py:349
  119.7 7.4 %collective-permute-start.3 = (bf16[144,256]{1,0:T(8,128)(2,1)S(1)}, bf16[144,256]{1,0:T(8,128)(2,1)S(1)}, u32[]{:S(2)}, u32[]{:S(2)}) collective-permute-start(bf16[144,256]{1,0:T(8,128)(2,1)S(1)} %get-tuple-element.38), channel_id=1, source_target_pairs={{0,64},{32,96},{64,0},{96,32},{128,192},{160,224},{192,128},{224,1... | collective-permute-start | bytes 221192 | tf_op jit(solution)/shard_map/ppermute | solution.py:349
  127.1 2.3 %collective-permute-start.4 = (bf16[144,256]{1,0:T(8,128)(2,1)S(1)}, bf16[144,256]{1,0:T(8,128)(2,1)S(1)}, u32[]{:S(2)}, u32[]{:S(2)}) collective-permute-start(bf16[144,256]{1,0:T(8,128)(2,1)S(1)} %get-tuple-element.39), channel_id=1, source_target_pairs={{0,96},{32,0},{64,32},{96,64},{128,224},{160,128},{192,160},{224,1... | collective-permute-start | bytes 221192 | tf_op jit(solution)/shard_map/ppermute | solution.py:349
  129.4 2.3 %shard_map.127 = (f32[512,256]{1,0:T(8,128)S(1)}, f32[4,256,256]{2,1,0:T(8,128)S(1)}) custom-call(s32[5]{0:T(128)S(1)} %pad_add_fusion.info, bf16[4,256,256]{2,1,0:T(8,128)(2,1)S(1)} %all-to-all-done.qd_ref, bf16[4,256,256]{2,1,0:T(8,128)(2,1)S(1)} %all-to-all-done.1.kv0_ref, bf16[4,128,256]{2,1,0:T(8,128)(2,1)S(1)} %get-tuple-element.32.grad_ref, ...), custom_call_target="tpu_custom_call" | custom-call | flops 1 | tf_op jit(solution)/shard_map/pallas_call | solution.py:331
  131.7 0.0 collective-permute-done.2.in1_ref
  131.7 5.0 %collective-permute-done.3.in2_ref = bf16[144,256]{1,0:T(8,128)(2,1)S(1)} collective-permute-done((bf16[144,256]{1,0:T(8,128)(2,1)S(1)}, bf16[144,256]{1,0:T(8,128)(2,1)S(1)}, u32[]{:S(2)}, u32[]{:S(2)}) %collective-permute-start.3) | collective-permute-done | bytes 73760 | tf_op jit(solution)/shard_map/ppermute | solution.py:349
  136.7 6.4 %collective-permute-done.4.in3_ref = bf16[144,256]{1,0:T(8,128)(2,1)S(1)} collective-permute-done((bf16[144,256]{1,0:T(8,128)(2,1)S(1)}, bf16[144,256]{1,0:T(8,128)(2,1)S(1)}, u32[]{:S(2)}, u32[]{:S(2)}) %collective-permute-start.4) | collective-permute-done | bytes 73760 | tf_op jit(solution)/shard_map/ppermute | solution.py:349
  143.2 0.6 shard_map.126
  143.7 0.0 collective-permute-done.5.other1_ref
  143.8 0.0 collective-permute-done.6.other2_ref
  143.8 1.1 shard_map.128
  144.9 3.5 %all-to-all-start.3 = ((bf16[4,384,256]{2,1,0:T(8,128)(2,1)}), bf16[4,384,256]{2,1,0:T(8,128)(2,1)S(1)}, u32[]{:S(2)}, u32[]{:S(2)}) async-start(bf16[4,384,256]{2,1,0:T(8,128)(2,1)} %shard_map.128), calls=%async_computation.3 | async-start | bytes 1572864 | tf_op jit(solution)/shard_map/all_to_all | solution.py:344
  148.4 1.9 collective-permute-start.7
  150.3 1.1 collective-permute-done.7
  151.4 6.4 %collective-permute-start.10 = (f32[1,1024]{1,0:T(1,128)S(1)}, f32[1,1024]{1,0:T(1,128)S(1)}, u32[]{:S(2)}, u32[]{:S(2)}) collective-permute-start(f32[1,1024]{1,0:T(1,128)S(1)} %add.30), channel_id=1, source_target_pairs={{0,6},{1,7},{2,4},{3,5},{4,2},{5,3},{6,0},{7,1},{8,14},{9,15},{10,... | collective-permute-start | bytes 12296 | tf_op jit(solution)/shard_map/ppermute | solution.py:357
  157.9 1.9 collective-permute-start.9
  159.8 2.8 %collective-permute-start.8 = (f32[1,1024]{1,0:T(1,128)S(1)}, f32[1,1024]{1,0:T(1,128)S(1)}, u32[]{:S(2)}, u32[]{:S(2)}) collective-permute-start(f32[1,1024]{1,0:T(1,128)S(1)} %add.30), channel_id=1, source_target_pairs={{0,2},{1,3},{2,0},{3,1},{4,6},{5,7},{6,4},{7,5},{8,10},{9,11},{10,... | collective-permute-start | bytes 12296 | tf_op jit(solution)/shard_map/ppermute | solution.py:357
  162.6 0.0 collective-permute-done.10
  162.6 2.3 %collective-permute-done.9 = f32[1,1024]{1,0:T(1,128)S(1)} collective-permute-done((f32[1,1024]{1,0:T(1,128)S(1)}, f32[1,1024]{1,0:T(1,128)S(1)}, u32[]{:S(2)}, u32[]{:S(2)}) %collective-permute-start.9) | collective-permute-done | bytes 4128 | tf_op jit(solution)/shard_map/ppermute | solution.py:357
  164.9 0.4 collective-permute-done.8
  165.3 1.9 collective-permute-start.13
  167.2 4.5 %collective-permute-start.12 = (f32[1,1024]{1,0:T(1,128)S(1)}, f32[1,1024]{1,0:T(1,128)S(1)}, u32[]{:S(2)}, u32[]{:S(2)}) collective-permute-start(f32[1,1024]{1,0:T(1,128)S(1)} %add_add_fusion.2), channel_id=1, source_target_pairs={{0,256},{32,288},{64,320},{96,352},{128,384},{160,416},{192,448},{... | collective-permute-start | bytes 12296 | tf_op jit(solution)/shard_map/ppermute | solution.py:357
  171.8 3.4 %collective-permute-start.11 = (f32[1,1024]{1,0:T(1,128)S(1)}, f32[1,1024]{1,0:T(1,128)S(1)}, u32[]{:S(2)}, u32[]{:S(2)}) collective-permute-start(f32[1,1024]{1,0:T(1,128)S(1)} %add_add_fusion.2), channel_id=1, source_target_pairs={{0,128},{32,160},{64,192},{96,224},{128,0},{160,32},{192,64},{224,... | collective-permute-start | bytes 12296 | tf_op jit(solution)/shard_map/ppermute | solution.py:357
  175.2 0.0 collective-permute-done.13
  175.2 0.0 collective-permute-done.12
  175.2 2.1 %collective-permute-done.11 = f32[1,1024]{1,0:T(1,128)S(1)} collective-permute-done((f32[1,1024]{1,0:T(1,128)S(1)}, f32[1,1024]{1,0:T(1,128)S(1)}, u32[]{:S(2)}, u32[]{:S(2)}) %collective-permute-start.11) | collective-permute-done | bytes 4128 | tf_op jit(solution)/shard_map/ppermute | solution.py:357
  177.3 2.2 %collective-permute-start.16 = (f32[1,1024]{1,0:T(1,128)S(1)}, f32[1,1024]{1,0:T(1,128)S(1)}, u32[]{:S(2)}, u32[]{:S(2)}) collective-permute-start(f32[1,1024]{1,0:T(1,128)S(1)} %add_add_fusion.1), channel_id=1, source_target_pairs={{0,24},{1,25},{2,26},{3,27},{4,28},{5,29},{6,30},{7,31},{8,16},{9,... | collective-permute-start | bytes 12296 | tf_op jit(solution)/shard_map/ppermute | solution.py:357
  179.5 6.7 %collective-permute-start.15 = (f32[1,1024]{1,0:T(1,128)S(1)}, f32[1,1024]{1,0:T(1,128)S(1)}, u32[]{:S(2)}, u32[]{:S(2)}) collective-permute-start(f32[1,1024]{1,0:T(1,128)S(1)} %add_add_fusion.1), channel_id=1, source_target_pairs={{0,16},{1,17},{2,18},{3,19},{4,20},{5,21},{6,22},{7,23},{8,24},{9,... | collective-permute-start | bytes 12296 | tf_op jit(solution)/shard_map/ppermute | solution.py:357
  186.2 1.9 collective-permute-start.14
  188.1 2.0 %shard_map.125 = (bf16[128,1024]{1,0:T(8,128)(2,1)}, bf16[128,1024]{1,0:T(8,128)(2,1)}) custom-call(s32[5]{0:T(128)S(1)} %pad_add_fusion.info, bf16[144,256]{1,0:T(8,128)(2,1)S(1)} %get-tuple-element.36.in0_ref, bf16[144,256]{1,0:T(8,128)(2,1)S(1)} %collective-permute-done.2.in1_ref, bf16[144,256]{1,0:T(8,128)(2,1)S(1)} %collective-permute-done.3.in2_ref, ...), custom_call_target="tpu_custom_call" | custom-call | flops 1 | tf_op jit(solution)/shard_map/pallas_call | solution.py:331
  190.1 0.0 collective-permute-done.16
  190.1 0.0 collective-permute-done.15
  190.1 1.6 collective-permute-done.14
  191.7 0.0 all-to-all-done.3.in_ref
  191.7 1.0 shard_map.129
  (9 shorter events, 0.0 us)
Async XLA Ops:
  0.6 1.0 copy-start.3
  1.6 0.9 copy-start.4
  3.5 15.3 %copy-start = (bf16[1,128,1024]{2,1,0:T(8,128)(2,1)S(1)}, bf16[1,128,1024]{2,1,0:T(8,128)(2,1)}, u32[]{:S(2)}) copy-start(bf16[1,128,1024]{2,1,0:T(8,128)(2,1)} %param.10) | copy-start | bytes 786436
  3.5 15.3 %copy-start.1 = (bf16[1,128,1024]{2,1,0:T(8,128)(2,1)S(1)}, bf16[1,128,1024]{2,1,0:T(8,128)(2,1)}, u32[]{:S(2)}) copy-start(bf16[1,128,1024]{2,1,0:T(8,128)(2,1)} %param.13) | copy-start | bytes 786436
  3.5 15.3 %copy-start.2 = (bf16[1,128,1024]{2,1,0:T(8,128)(2,1)S(1)}, bf16[1,128,1024]{2,1,0:T(8,128)(2,1)}, u32[]{:S(2)}) copy-start(bf16[1,128,1024]{2,1,0:T(8,128)(2,1)} %param.7) | copy-start | bytes 786436
  3.5 41.2 %all-to-all-start.1 = ((bf16[4,256,256]{2,1,0:T(8,128)(2,1)}), bf16[4,256,256]{2,1,0:T(8,128)(2,1)S(1)}, u32[]{:S(2)}, u32[]{:S(2)}) async-start(bf16[4,256,256]{2,1,0:T(8,128)(2,1)} %shard_map.119), calls=%async_computation.1 | async-start | bytes 1048576 | tf_op jit(solution)/shard_map/all_to_all | solution.py:344
  18.8 0.7 copy-start.5
  44.7 28.9 %all-to-all-start = ((bf16[4,256,256]{2,1,0:T(8,128)(2,1)}), bf16[4,256,256]{2,1,0:T(8,128)(2,1)S(1)}, u32[]{:S(2)}, u32[]{:S(2)}) async-start(bf16[4,256,256]{2,1,0:T(8,128)(2,1)} %shard_map.118), calls=%async_computation | async-start | bytes 1048576 | tf_op jit(solution)/shard_map/all_to_all | solution.py:344
  54.1 21.1 %collective-permute-start.1 = (bf16[4,256,256]{2,1,0:T(8,128)(2,1)S(1)}, bf16[4,256,256]{2,1,0:T(8,128)(2,1)S(1)}, u32[]{:S(2)}, u32[]{:S(2)}) collective-permute-start(bf16[4,256,256]{2,1,0:T(8,128)(2,1)S(1)} %all-to-all-done.1.kv0_ref), channel_id=1, source_target_pairs={{0,256},{32,288},{64,320},{96,352},{128,384},{160,416},{192,448},{... | collective-permute-start | bytes 1572872 | tf_op jit(solution)/shard_map/ppermute | solution.py:373
  55.4 19.8 %collective-permute-start = (bf16[4,256,256]{2,1,0:T(8,128)(2,1)S(1)}, bf16[4,256,256]{2,1,0:T(8,128)(2,1)S(1)}, u32[]{:S(2)}, u32[]{:S(2)}) collective-permute-start(bf16[4,256,256]{2,1,0:T(8,128)(2,1)S(1)} %all-to-all-done.1.kv0_ref), channel_id=1, source_target_pairs={{0,128},{32,160},{64,192},{96,224},{128,256},{160,288},{192,320},{... | collective-permute-start | bytes 1572872 | tf_op jit(solution)/shard_map/ppermute | solution.py:373
  56.7 0.7 copy-start.6
  108.5 35.2 %collective-permute-start.5 = (bf16[4,256,256]{2,1,0:T(8,128)(2,1)S(1)}, bf16[4,256,256]{2,1,0:T(8,128)(2,1)S(1)}, u32[]{:S(2)}, u32[]{:S(2)}) collective-permute-start(bf16[4,256,256]{2,1,0:T(8,128)(2,1)S(1)} %get-tuple-element.34), channel_id=1, source_target_pairs={{128,0},{160,32},{192,64},{224,96},{256,128},{288,160},{320,192},{... | collective-permute-start | bytes 1572872 | tf_op jit(solution)/shard_map/ppermute | solution.py:373
  109.9 33.9 %collective-permute-start.6 = (bf16[4,256,256]{2,1,0:T(8,128)(2,1)S(1)}, bf16[4,256,256]{2,1,0:T(8,128)(2,1)S(1)}, u32[]{:S(2)}, u32[]{:S(2)}) collective-permute-start(bf16[4,256,256]{2,1,0:T(8,128)(2,1)S(1)} %get-tuple-element.44), channel_id=1, source_target_pairs={{256,0},{288,32},{320,64},{352,96},{384,128},{416,160},{448,192},{... | collective-permute-start | bytes 1572872 | tf_op jit(solution)/shard_map/ppermute | solution.py:373
  117.2 14.5 %collective-permute-start.2 = (bf16[144,256]{1,0:T(8,128)(2,1)S(1)}, bf16[144,256]{1,0:T(8,128)(2,1)S(1)}, u32[]{:S(2)}, u32[]{:S(2)}) collective-permute-start(bf16[144,256]{1,0:T(8,128)(2,1)S(1)} %get-tuple-element.37), channel_id=1, source_target_pairs={{0,32},{32,64},{64,96},{96,0},{128,160},{160,192},{192,224},{224,1... | collective-permute-start | bytes 221192 | tf_op jit(solution)/shard_map/ppermute | solution.py:349
  119.7 17.1 %collective-permute-start.3 = (bf16[144,256]{1,0:T(8,128)(2,1)S(1)}, bf16[144,256]{1,0:T(8,128)(2,1)S(1)}, u32[]{:S(2)}, u32[]{:S(2)}) collective-permute-start(bf16[144,256]{1,0:T(8,128)(2,1)S(1)} %get-tuple-element.38), channel_id=1, source_target_pairs={{0,64},{32,96},{64,0},{96,32},{128,192},{160,224},{192,128},{224,1... | collective-permute-start | bytes 221192 | tf_op jit(solution)/shard_map/ppermute | solution.py:349
  127.1 16.1 %collective-permute-start.4 = (bf16[144,256]{1,0:T(8,128)(2,1)S(1)}, bf16[144,256]{1,0:T(8,128)(2,1)S(1)}, u32[]{:S(2)}, u32[]{:S(2)}) collective-permute-start(bf16[144,256]{1,0:T(8,128)(2,1)S(1)} %get-tuple-element.39), channel_id=1, source_target_pairs={{0,96},{32,0},{64,32},{96,64},{128,224},{160,128},{192,160},{224,1... | collective-permute-start | bytes 221192 | tf_op jit(solution)/shard_map/ppermute | solution.py:349
  144.9 46.8 %all-to-all-start.3 = ((bf16[4,384,256]{2,1,0:T(8,128)(2,1)}), bf16[4,384,256]{2,1,0:T(8,128)(2,1)S(1)}, u32[]{:S(2)}, u32[]{:S(2)}) async-start(bf16[4,384,256]{2,1,0:T(8,128)(2,1)} %shard_map.128), calls=%async_computation.3 | async-start | bytes 1572864 | tf_op jit(solution)/shard_map/all_to_all | solution.py:344
  148.4 3.1 %collective-permute-start.7 = (f32[1,1024]{1,0:T(1,128)S(1)}, f32[1,1024]{1,0:T(1,128)S(1)}, u32[]{:S(2)}, u32[]{:S(2)}) collective-permute-start(f32[1,1024]{1,0:T(1,128)S(1)} %shard_map.126), channel_id=1, source_target_pairs={{0,1},{1,0},{2,3},{3,2},{4,5},{5,4},{6,7},{7,6},{8,9},{9,8},{10,11... | collective-permute-start | bytes 12296 | tf_op jit(solution)/shard_map/ppermute | solution.py:367
  151.4 11.1 %collective-permute-start.10 = (f32[1,1024]{1,0:T(1,128)S(1)}, f32[1,1024]{1,0:T(1,128)S(1)}, u32[]{:S(2)}, u32[]{:S(2)}) collective-permute-start(f32[1,1024]{1,0:T(1,128)S(1)} %add.30), channel_id=1, source_target_pairs={{0,6},{1,7},{2,4},{3,5},{4,2},{5,3},{6,0},{7,1},{8,14},{9,15},{10,... | collective-permute-start | bytes 12296 | tf_op jit(solution)/shard_map/ppermute | solution.py:357
  157.9 7.0 %collective-permute-start.9 = (f32[1,1024]{1,0:T(1,128)S(1)}, f32[1,1024]{1,0:T(1,128)S(1)}, u32[]{:S(2)}, u32[]{:S(2)}) collective-permute-start(f32[1,1024]{1,0:T(1,128)S(1)} %add.30), channel_id=1, source_target_pairs={{0,4},{1,5},{2,6},{3,7},{4,0},{5,1},{6,2},{7,3},{8,12},{9,13},{10,... | collective-permute-start | bytes 12296 | tf_op jit(solution)/shard_map/ppermute | solution.py:357
  159.8 5.5 %collective-permute-start.8 = (f32[1,1024]{1,0:T(1,128)S(1)}, f32[1,1024]{1,0:T(1,128)S(1)}, u32[]{:S(2)}, u32[]{:S(2)}) collective-permute-start(f32[1,1024]{1,0:T(1,128)S(1)} %add.30), channel_id=1, source_target_pairs={{0,2},{1,3},{2,0},{3,1},{4,6},{5,7},{6,4},{7,5},{8,10},{9,11},{10,... | collective-permute-start | bytes 12296 | tf_op jit(solution)/shard_map/ppermute | solution.py:357
  165.3 9.8 %collective-permute-start.13 = (f32[1,1024]{1,0:T(1,128)S(1)}, f32[1,1024]{1,0:T(1,128)S(1)}, u32[]{:S(2)}, u32[]{:S(2)}) collective-permute-start(f32[1,1024]{1,0:T(1,128)S(1)} %add_add_fusion.2), channel_id=1, source_target_pairs={{0,384},{32,416},{64,448},{96,480},{128,256},{160,288},{192,320},{... | collective-permute-start | bytes 12296 | tf_op jit(solution)/shard_map/ppermute | solution.py:357
  167.2 7.9 %collective-permute-start.12 = (f32[1,1024]{1,0:T(1,128)S(1)}, f32[1,1024]{1,0:T(1,128)S(1)}, u32[]{:S(2)}, u32[]{:S(2)}) collective-permute-start(f32[1,1024]{1,0:T(1,128)S(1)} %add_add_fusion.2), channel_id=1, source_target_pairs={{0,256},{32,288},{64,320},{96,352},{128,384},{160,416},{192,448},{... | collective-permute-start | bytes 12296 | tf_op jit(solution)/shard_map/ppermute | solution.py:357
  171.8 5.5 %collective-permute-start.11 = (f32[1,1024]{1,0:T(1,128)S(1)}, f32[1,1024]{1,0:T(1,128)S(1)}, u32[]{:S(2)}, u32[]{:S(2)}) collective-permute-start(f32[1,1024]{1,0:T(1,128)S(1)} %add_add_fusion.2), channel_id=1, source_target_pairs={{0,128},{32,160},{64,192},{96,224},{128,0},{160,32},{192,64},{224,... | collective-permute-start | bytes 12296 | tf_op jit(solution)/shard_map/ppermute | solution.py:357
  177.3 12.8 %collective-permute-start.16 = (f32[1,1024]{1,0:T(1,128)S(1)}, f32[1,1024]{1,0:T(1,128)S(1)}, u32[]{:S(2)}, u32[]{:S(2)}) collective-permute-start(f32[1,1024]{1,0:T(1,128)S(1)} %add_add_fusion.1), channel_id=1, source_target_pairs={{0,24},{1,25},{2,26},{3,27},{4,28},{5,29},{6,30},{7,31},{8,16},{9,... | collective-permute-start | bytes 12296 | tf_op jit(solution)/shard_map/ppermute | solution.py:357
  179.5 10.6 %collective-permute-start.15 = (f32[1,1024]{1,0:T(1,128)S(1)}, f32[1,1024]{1,0:T(1,128)S(1)}, u32[]{:S(2)}, u32[]{:S(2)}) collective-permute-start(f32[1,1024]{1,0:T(1,128)S(1)} %add_add_fusion.1), channel_id=1, source_target_pairs={{0,16},{1,17},{2,18},{3,19},{4,20},{5,21},{6,22},{7,23},{8,24},{9,... | collective-permute-start | bytes 12296 | tf_op jit(solution)/shard_map/ppermute | solution.py:357
  186.2 5.5 %collective-permute-start.14 = (f32[1,1024]{1,0:T(1,128)S(1)}, f32[1,1024]{1,0:T(1,128)S(1)}, u32[]{:S(2)}, u32[]{:S(2)}) collective-permute-start(f32[1,1024]{1,0:T(1,128)S(1)} %add_add_fusion.1), channel_id=1, source_target_pairs={{0,8},{1,9},{2,10},{3,11},{4,12},{5,13},{6,14},{7,15},{8,0},{9,1},... | collective-permute-start | bytes 12296 | tf_op jit(solution)/shard_map/ppermute | solution.py:357

commit v4 on v3

--- a/solution.py
+++ b/solution.py
@@ -107,7 +107,9 @@
         def step(key_tile, tiles, total, back=back, kv_ref=kv_ref):
             base = (block - back) * BLOCK + key_tile * TILE
             where = iota((1, tiles * TILE), 1)
-            allowed = (where >= start - base) & (where <= pos - base)
+            allowed = where >= start - base
+            if back == 0:
+                allowed = allowed & (where <= pos - base)
             sums = []
             for head in range(2):
                 k = tile_rows(kv_ref, key_tile, 0, head, tiles)
@@ -251,7 +253,9 @@
         def step(key_tile, tiles, total):
             base = (block - back) * BLOCK + key_tile * TILE
             where = iota((tiles * TILE, 1), 0)
-            allowed = (where >= start - base) & (where <= pos - base)
+            allowed = where >= start - base
+            if back == 0:
+                allowed = allowed & (where <= pos - base)
             sums = []
             for head in range(2):
                 k = tile_rows(kv_ref, key_tile, 0, head, tiles)
@@ -268,13 +272,13 @@
                 dv = dot(probs, grad[head], ((1,), (0,))).reshape(2 * tiles, ROWS, HEAD)
                 dkv_ref[slots, 0:ROWS, head_cols(head)] += dk
                 dkv_ref[slots, ROWS : 2 * ROWS, head_cols(head)] += dv
-                sums.append(total[head] + dot(grad_scores, k, ((0,), (0,))))
+                sums.append(total[head] + dot(k, grad_scores, ((0,), (0,))))
             return tuple(sums)
 
-        total = tuple(dq_ref[here, head_cols(head)] for head in range(2))
+        total = tuple(dq_ref[head_cols(head), here] for head in range(2))
         total = over_keys(info, tile, back, step, total)
         for head in range(2):
-            dq_ref[here, head_cols(head)] = total[head]
+            dq_ref[head_cols(head), here] = total[head]
 
 
 def send_sums(dkv_ref, send_ref):
@@ -312,8 +316,9 @@
         dv = dkv_ref[slot, ROWS : 2 * ROWS, :] + others[ROWS : 2 * ROWS]
         out_ref[slot, 0:ROWS, :] = dk.astype(BF16)
         out_ref[slot, ROWS : 2 * ROWS, :] = dv.astype(BF16)
-        dq = dq_ref[slot * ROWS : (slot + 1) * ROWS, :] * scale
-        out_ref[slot, 2 * ROWS : 3 * ROWS, :] = dq.astype(BF16)
+        for head in range(2):
+            dq = dq_ref[head_cols(head), slot * ROWS : (slot + 1) * ROWS].T * scale
+            out_ref[slot, 2 * ROWS : 3 * ROWS, head_cols(head)] = dq.astype(BF16)
 
 
 def unpack_kernel(in_ref, gain_sum_ref, gain_ref, dq_ref, dk_ref, dv_ref, grad_gain_ref):
@@ -325,7 +330,7 @@
         dq_ref[:, cols] = in_ref[z, 2 * ROWS : 3 * ROWS, :]
 
 
-def call(kernel, outs, *args, scalars=0, scratch=(), flops=1, space=pltpu.VMEM):
+def call(kernel, outs, *args, scalars=0, scratch=(), flops=1, space=pltpu.VMEM, limit=VMEM_LIMIT):
     specs = [pl.BlockSpec(memory_space=pltpu.SMEM)] * scalars
     specs += [pl.BlockSpec(memory_space=space)] * (len(args) - scalars)
     return pl.pallas_call(
@@ -334,7 +339,7 @@
         in_specs=specs,
         out_specs=[pl.BlockSpec(memory_space=pltpu.VMEM)] * len(outs),
         scratch_shapes=scratch,
-        compiler_params=pltpu.CompilerParams(vmem_limit_bytes=VMEM_LIMIT),
+        compiler_params=pltpu.CompilerParams(vmem_limit_bytes=limit),
         cost_estimate=pl.CostEstimate(flops=flops, bytes_accessed=0, transcendentals=0),
     )(*args)
 
@@ -381,6 +386,7 @@
     pair = shape((ZS, 2 * ROWS, PAIR), BF16)
     pair_sums = shape((ZS, 2 * ROWS, PAIR), F32)
     block = shape((BLOCK, PAIR), F32)
+    turned = shape((PAIR, BLOCK), F32)
     sums_scratch = [pltpu.VMEM(pair_sums.shape, F32)]
 
     (kv,) = call(
@@ -389,6 +395,7 @@
         keys[0],
         values[0],
         space=pltpu.HBM,
+        limit=62 * 1024 * 1024,
         scratch=[pltpu.SemaphoreType.DMA((2 * ZS,))],
     )
     kv0 = along_z(kv)
@@ -410,7 +417,7 @@
     stats = along_z(stats)
     to2, grad_att, dq, gain_sum = call(
         backward_far_kernel,
-        [pair, shape((ZS, ROWS, PAIR), BF16), block, shape((2, HEAD), F32)],
+        [pair, shape((ZS, ROWS, PAIR), BF16), turned, shape((2, HEAD), F32)],
         info,
         qd,
         kv2,
@@ -422,7 +429,7 @@
     from2 = shift_y(to2, -2)
     to1, dq = call(
         backward_near_kernel,
-        [pair, block],
+        [pair, turned],
         info,
         qd,
         kv1,
@@ -446,7 +453,7 @@
     back[1] = shift_z(back[1], 1)
     back[3] = shift_z(back[3], 3)
     dq, dkv = call(
-        backward_own_kernel, [block, pair_sums], info, qd, kv0, grad_att, dq, scalars=1
+        backward_own_kernel, [turned, pair_sums], info, qd, kv0, grad_att, dq, scalars=1
     )
     (gain_sum,) = call(gain_kernel, [shape((1, width), F32)], info, *back, scalars=1)
     output, grad_gate = call(

time: 195 us -> 191 us (0.979)
  starting transfers between devices: 84.4 us -> 86.9 us
    ppermute x4, starting transfers between devices: 10.5 us -> 13.8 us  [shift_y(): return lax.ppermute(array, 'seq', pairs)]
    ppermute x9, starting transfers between devices: 31.7 us -> 29.7 us  [add_over(): lax.ppermute(array, axis, [(i, i ^ bits) for i in range(size)])]
where the time goes in v4:
time: 191 us; the launch traced here: 190 us
  starting transfers between devices  86.9 us (45%)
  waiting for transfers between devices  58.2 us (30%)
  blocking collectives  25.2 us (13%)
  Pallas kernels  17.4 us (9%)
    all_to_all x3, waiting for transfers between devices, along_z(): lax.all_to_all(array, 'seq', 0, 0, axis_index_groups=groups, tiled=True)  40.3 us
    ppermute x9, starting transfers between devices, add_over(): lax.ppermute(array, axis, [(i, i ^ bits) for i in range(size)])  29.7 us
    all_to_all x3, starting transfers between devices, along_z(): lax.all_to_all(array, 'seq', 0, 0, axis_index_groups=groups, tiled=True)  29.3 us
    all_to_all x1, blocking collectives, along_z(): lax.all_to_all(array, 'seq', 0, 0, axis_index_groups=groups, tiled=True)  25.2 us
    pallas_call x12, Pallas kernels, call(): pl.pallas_call(kernel, out_shape=outs, in_specs=specs, out_specs=[pl.Bloc...  17.4 us
    ppermute x4, starting transfers between devices, shift_y(): return lax.ppermute(array, 'seq', pairs)  13.8 us
    ppermute x3, starting transfers between devices, shift_z(): return lax.ppermute(array, 'seq', pairs)  12.1 us
    ppermute x3, waiting for transfers between devices, shift_z(): return lax.ppermute(array, 'seq', pairs)  11 us
  transfers between devices with their start and end apart: 20, of which 9 were waited for; matrix products, arithmetic and copies ran while one was open for 0% of the time, Pallas kernels for 4%

profile of v4, /device:TPU:24, one launch (start us, length us, event | category | flops | bytes accessed | tf_op | source)
XLA Modules:
  0.0 190.2 jit_solution(10737422568191347717)
XLA Ops:
  0.6 2.0 %shard_map.119 = bf16[4,256,256]{2,1,0:T(8,128)(2,1)} custom-call(bf16[128,1024]{1,0:T(8,128)(2,1)} %bitcast.23, bf16[128,1024]{1,0:T(8,128)(2,1)} %bitcast.24), custom_call_target="tpu_custom_call" | custom-call | flops 1 | tf_op jit(solution)/shard_map/pallas_call | solution.py:336
  2.6 0.0 copy-start
  2.6 0.0 copy-start.1
  2.6 0.0 copy-start.2
  2.6 15.2 %all-to-all-start.1 = ((bf16[4,256,256]{2,1,0:T(8,128)(2,1)}), bf16[4,256,256]{2,1,0:T(8,128)(2,1)S(1)}, u32[]{:S(2)}, u32[]{:S(2)}) async-start(bf16[4,256,256]{2,1,0:T(8,128)(2,1)} %shard_map.119), calls=%async_computation.1 | async-start | bytes 1048576 | tf_op jit(solution)/shard_map/all_to_all | solution.py:349
  17.9 0.0 copy-done
  17.9 0.0 copy-done.1
  17.9 0.0 copy-done.2
  17.9 0.7 copy-done.3
  18.5 0.9 shard_map.118
  19.4 24.3 %all-to-all-done.1.kv0_ref = bf16[4,256,256]{2,1,0:T(8,128)(2,1)S(1)} async-done(((bf16[4,256,256]{2,1,0:T(8,128)(2,1)}), bf16[4,256,256]{2,1,0:T(8,128)(2,1)S(1)}, u32[]{:S(2)}, u32[]{:S(2)}) %all-to-all-start.1) | async-done | bytes 524320 | tf_op jit(solution)/shard_map/all_to_all | solution.py:349
  43.8 9.4 %all-to-all-start = ((bf16[4,256,256]{2,1,0:T(8,128)(2,1)}), bf16[4,256,256]{2,1,0:T(8,128)(2,1)S(1)}, u32[]{:S(2)}, u32[]{:S(2)}) async-start(bf16[4,256,256]{2,1,0:T(8,128)(2,1)} %shard_map.118), calls=%async_computation | async-start | bytes 1048576 | tf_op jit(solution)/shard_map/all_to_all | solution.py:349
  53.2 1.3 collective-permute-start.1
  54.5 1.3 collective-permute-start
  55.8 0.0 copy-start.4
  55.8 0.6 copy-done.4
  56.5 0.2 reduce-window.9
  56.7 0.1 pad_add_fusion.info
  56.7 16.0 %all-to-all-done.qd_ref = bf16[4,256,256]{2,1,0:T(8,128)(2,1)S(1)} async-done(((bf16[4,256,256]{2,1,0:T(8,128)(2,1)}), bf16[4,256,256]{2,1,0:T(8,128)(2,1)S(1)}, u32[]{:S(2)}, u32[]{:S(2)}) %all-to-all-start) | async-done | bytes 524320 | tf_op jit(solution)/shard_map/all_to_all | solution.py:349
  72.7 1.6 shard_map.120.sum_ref
  74.4 0.0 collective-permute-done.1.kv2_ref
  74.4 0.0 collective-permute-done.kv1_ref
  74.4 2.1 %shard_map.121 = (f32[512,256]{1,0:T(8,128)S(1)}, f32[4,16,128]{2,1,0:T(8,128)S(1)}) custom-call(s32[5]{0:T(128)S(1)} %pad_add_fusion.info, bf16[4,256,256]{2,1,0:T(8,128)(2,1)S(1)} %all-to-all-done.qd_ref, bf16[4,256,256]{2,1,0:T(8,128)(2,1)S(1)} %collective-permute-done.kv1_ref, bf16[4,256,256]{2,1,0:T(8,128)(2,1)S(1)} %collective-permute-done.1.kv2_ref, ...), custom_call_target="tpu_custom_call" | custom-call | flops 1 | tf_op jit(solution)/shard_map/pallas_call | solution.py:336
  76.5 25.2 %all_to_all.20.stats_ref = f32[4,16,128]{2,1,0:T(8,128)S(1)} all-to-all(f32[4,16,128]{2,1,0:T(8,128)S(1)} %get-tuple-element.30), channel_id=1, replica_groups={{0,32,64,96},{128,160,192,224},{256,288,320,352},{384,416,448,480},{1,3..., dimensions={0} | all-to-all | bytes 65536 | tf_op jit(solution)/shard_map/all_to_all | solution.py:349
  101.7 1.3 shard_map.122
  103.1 1.8 shard_map.123
  104.8 10.0 %collective-permute-start.5 = (bf16[4,256,256]{2,1,0:T(8,128)(2,1)S(1)}, bf16[4,256,256]{2,1,0:T(8,128)(2,1)S(1)}, u32[]{:S(2)}, u32[]{:S(2)}) collective-permute-start(bf16[4,256,256]{2,1,0:T(8,128)(2,1)S(1)} %get-tuple-element.34), channel_id=1, source_target_pairs={{128,0},{160,32},{192,64},{224,96},{256,128},{288,160},{320,192},{... | collective-permute-start | bytes 1572872 | tf_op jit(solution)/shard_map/ppermute | solution.py:378
  114.8 1.3 collective-permute-start.6
  116.1 0.8 shard_map.124
  116.9 2.4 %collective-permute-start.2 = (bf16[144,256]{1,0:T(8,128)(2,1)S(1)}, bf16[144,256]{1,0:T(8,128)(2,1)S(1)}, u32[]{:S(2)}, u32[]{:S(2)}) collective-permute-start(bf16[144,256]{1,0:T(8,128)(2,1)S(1)} %get-tuple-element.37), channel_id=1, source_target_pairs={{0,32},{32,64},{64,96},{96,0},{128,160},{160,192},{192,224},{224,1... | collective-permute-start | bytes 221192 | tf_op jit(solution)/shard_map/ppermute | solution.py:354
  119.3 7.4 %collective-permute-start.3 = (bf16[144,256]{1,0:T(8,128)(2,1)S(1)}, bf16[144,256]{1,0:T(8,128)(2,1)S(1)}, u32[]{:S(2)}, u32[]{:S(2)}) collective-permute-start(bf16[144,256]{1,0:T(8,128)(2,1)S(1)} %get-tuple-element.38), channel_id=1, source_target_pairs={{0,64},{32,96},{64,0},{96,32},{128,192},{160,224},{192,128},{224,1... | collective-permute-start | bytes 221192 | tf_op jit(solution)/shard_map/ppermute | solution.py:354
  126.7 2.3 %collective-permute-start.4 = (bf16[144,256]{1,0:T(8,128)(2,1)S(1)}, bf16[144,256]{1,0:T(8,128)(2,1)S(1)}, u32[]{:S(2)}, u32[]{:S(2)}) collective-permute-start(bf16[144,256]{1,0:T(8,128)(2,1)S(1)} %get-tuple-element.39), channel_id=1, source_target_pairs={{0,96},{32,0},{64,32},{96,64},{128,224},{160,128},{192,160},{224,1... | collective-permute-start | bytes 221192 | tf_op jit(solution)/shard_map/ppermute | solution.py:354
  129.0 2.1 %shard_map.127 = (f32[256,512]{1,0:T(8,128)S(1)}, f32[4,256,256]{2,1,0:T(8,128)S(1)}) custom-call(s32[5]{0:T(128)S(1)} %pad_add_fusion.info, bf16[4,256,256]{2,1,0:T(8,128)(2,1)S(1)} %all-to-all-done.qd_ref, bf16[4,256,256]{2,1,0:T(8,128)(2,1)S(1)} %all-to-all-done.1.kv0_ref, bf16[4,128,256]{2,1,0:T(8,128)(2,1)S(1)} %get-tuple-element.32.grad_ref, ...), custom_call_target="tpu_custom_call" | custom-call | flops 1 | tf_op jit(solution)/shard_map/pallas_call | solution.py:336
  131.1 0.0 collective-permute-done.2.in1_ref
  131.1 4.3 %collective-permute-done.3.in2_ref = bf16[144,256]{1,0:T(8,128)(2,1)S(1)} collective-permute-done((bf16[144,256]{1,0:T(8,128)(2,1)S(1)}, bf16[144,256]{1,0:T(8,128)(2,1)S(1)}, u32[]{:S(2)}, u32[]{:S(2)}) %collective-permute-start.3) | collective-permute-done | bytes 73760 | tf_op jit(solution)/shard_map/ppermute | solution.py:354
  135.4 6.7 %collective-permute-done.4.in3_ref = bf16[144,256]{1,0:T(8,128)(2,1)S(1)} collective-permute-done((bf16[144,256]{1,0:T(8,128)(2,1)S(1)}, bf16[144,256]{1,0:T(8,128)(2,1)S(1)}, u32[]{:S(2)}, u32[]{:S(2)}) %collective-permute-start.4) | collective-permute-done | bytes 73760 | tf_op jit(solution)/shard_map/ppermute | solution.py:354
  142.1 0.6 shard_map.126
  142.7 0.0 collective-permute-done.5.other1_ref
  142.7 0.0 collective-permute-done.6.other2_ref
  142.7 1.3 shard_map.128
  144.0 4.7 %all-to-all-start.3 = ((bf16[4,384,256]{2,1,0:T(8,128)(2,1)}), bf16[4,384,256]{2,1,0:T(8,128)(2,1)S(1)}, u32[]{:S(2)}, u32[]{:S(2)}) async-start(bf16[4,384,256]{2,1,0:T(8,128)(2,1)} %shard_map.128), calls=%async_computation.3 | async-start | bytes 1572864 | tf_op jit(solution)/shard_map/all_to_all | solution.py:349
  148.7 1.9 %collective-permute-start.7 = (f32[1,1024]{1,0:T(1,128)S(1)}, f32[1,1024]{1,0:T(1,128)S(1)}, u32[]{:S(2)}, u32[]{:S(2)}) collective-permute-start(f32[1,1024]{1,0:T(1,128)S(1)} %shard_map.126), channel_id=1, source_target_pairs={{0,1},{1,0},{2,3},{3,2},{4,5},{5,4},{6,7},{7,6},{8,9},{9,8},{10,11... | collective-permute-start | bytes 12296 | tf_op jit(solution)/shard_map/ppermute | solution.py:372
  150.6 1.1 collective-permute-done.7
  151.7 2.9 %collective-permute-start.10 = (f32[1,1024]{1,0:T(1,128)S(1)}, f32[1,1024]{1,0:T(1,128)S(1)}, u32[]{:S(2)}, u32[]{:S(2)}) collective-permute-start(f32[1,1024]{1,0:T(1,128)S(1)} %add.30), channel_id=1, source_target_pairs={{0,6},{1,7},{2,4},{3,5},{4,2},{5,3},{6,0},{7,1},{8,14},{9,15},{10,... | collective-permute-start | bytes 12296 | tf_op jit(solution)/shard_map/ppermute | solution.py:362
  154.7 4.3 %collective-permute-start.9 = (f32[1,1024]{1,0:T(1,128)S(1)}, f32[1,1024]{1,0:T(1,128)S(1)}, u32[]{:S(2)}, u32[]{:S(2)}) collective-permute-start(f32[1,1024]{1,0:T(1,128)S(1)} %add.30), channel_id=1, source_target_pairs={{0,4},{1,5},{2,6},{3,7},{4,0},{5,1},{6,2},{7,3},{8,12},{9,13},{10,... | collective-permute-start | bytes 12296 | tf_op jit(solution)/shard_map/ppermute | solution.py:362
  158.9 2.6 %collective-permute-start.8 = (f32[1,1024]{1,0:T(1,128)S(1)}, f32[1,1024]{1,0:T(1,128)S(1)}, u32[]{:S(2)}, u32[]{:S(2)}) collective-permute-start(f32[1,1024]{1,0:T(1,128)S(1)} %add.30), channel_id=1, source_target_pairs={{0,2},{1,3},{2,0},{3,1},{4,6},{5,7},{6,4},{7,5},{8,10},{9,11},{10,... | collective-permute-start | bytes 12296 | tf_op jit(solution)/shard_map/ppermute | solution.py:362
  161.6 0.0 collective-permute-done.10
  161.6 0.1 collective-permute-done.9
  161.7 2.8 %collective-permute-done.8 = f32[1,1024]{1,0:T(1,128)S(1)} collective-permute-done((f32[1,1024]{1,0:T(1,128)S(1)}, f32[1,1024]{1,0:T(1,128)S(1)}, u32[]{:S(2)}, u32[]{:S(2)}) %collective-permute-start.8) | collective-permute-done | bytes 4128 | tf_op jit(solution)/shard_map/ppermute | solution.py:362
  164.4 1.9 %collective-permute-start.13 = (f32[1,1024]{1,0:T(1,128)S(1)}, f32[1,1024]{1,0:T(1,128)S(1)}, u32[]{:S(2)}, u32[]{:S(2)}) collective-permute-start(f32[1,1024]{1,0:T(1,128)S(1)} %add_add_fusion.2), channel_id=1, source_target_pairs={{0,384},{32,416},{64,448},{96,480},{128,256},{160,288},{192,320},{... | collective-permute-start | bytes 12296 | tf_op jit(solution)/shard_map/ppermute | solution.py:362
  166.4 4.1 %collective-permute-start.12 = (f32[1,1024]{1,0:T(1,128)S(1)}, f32[1,1024]{1,0:T(1,128)S(1)}, u32[]{:S(2)}, u32[]{:S(2)}) collective-permute-start(f32[1,1024]{1,0:T(1,128)S(1)} %add_add_fusion.2), channel_id=1, source_target_pairs={{0,256},{32,288},{64,320},{96,352},{128,384},{160,416},{192,448},{... | collective-permute-start | bytes 12296 | tf_op jit(solution)/shard_map/ppermute | solution.py:362
  170.4 3.8 %collective-permute-start.11 = (f32[1,1024]{1,0:T(1,128)S(1)}, f32[1,1024]{1,0:T(1,128)S(1)}, u32[]{:S(2)}, u32[]{:S(2)}) collective-permute-start(f32[1,1024]{1,0:T(1,128)S(1)} %add_add_fusion.2), channel_id=1, source_target_pairs={{0,128},{32,160},{64,192},{96,224},{128,0},{160,32},{192,64},{224,... | collective-permute-start | bytes 12296 | tf_op jit(solution)/shard_map/ppermute | solution.py:362
  174.3 0.0 collective-permute-done.13
  174.3 0.0 collective-permute-done.12
  174.3 1.7 collective-permute-done.11
  176.0 1.9 %collective-permute-start.16 = (f32[1,1024]{1,0:T(1,128)S(1)}, f32[1,1024]{1,0:T(1,128)S(1)}, u32[]{:S(2)}, u32[]{:S(2)}) collective-permute-start(f32[1,1024]{1,0:T(1,128)S(1)} %add_add_fusion.1), channel_id=1, source_target_pairs={{0,24},{1,25},{2,26},{3,27},{4,28},{5,29},{6,30},{7,31},{8,16},{9,... | collective-permute-start | bytes 12296 | tf_op jit(solution)/shard_map/ppermute | solution.py:362
  177.9 5.9 %collective-permute-start.15 = (f32[1,1024]{1,0:T(1,128)S(1)}, f32[1,1024]{1,0:T(1,128)S(1)}, u32[]{:S(2)}, u32[]{:S(2)}) collective-permute-start(f32[1,1024]{1,0:T(1,128)S(1)} %add_add_fusion.1), channel_id=1, source_target_pairs={{0,16},{1,17},{2,18},{3,19},{4,20},{5,21},{6,22},{7,23},{8,24},{9,... | collective-permute-start | bytes 12296 | tf_op jit(solution)/shard_map/ppermute | solution.py:362
  183.8 2.3 %collective-permute-start.14 = (f32[1,1024]{1,0:T(1,128)S(1)}, f32[1,1024]{1,0:T(1,128)S(1)}, u32[]{:S(2)}, u32[]{:S(2)}) collective-permute-start(f32[1,1024]{1,0:T(1,128)S(1)} %add_add_fusion.1), channel_id=1, source_target_pairs={{0,8},{1,9},{2,10},{3,11},{4,12},{5,13},{6,14},{7,15},{8,0},{9,1},... | collective-permute-start | bytes 12296 | tf_op jit(solution)/shard_map/ppermute | solution.py:362
  186.1 2.0 %shard_map.125 = (bf16[128,1024]{1,0:T(8,128)(2,1)}, bf16[128,1024]{1,0:T(8,128)(2,1)}) custom-call(s32[5]{0:T(128)S(1)} %pad_add_fusion.info, bf16[144,256]{1,0:T(8,128)(2,1)S(1)} %get-tuple-element.36.in0_ref, bf16[144,256]{1,0:T(8,128)(2,1)S(1)} %collective-permute-done.2.in1_ref, bf16[144,256]{1,0:T(8,128)(2,1)S(1)} %collective-permute-done.3.in2_ref, ...), custom_call_target="tpu_custom_call" | custom-call | flops 1 | tf_op jit(solution)/shard_map/pallas_call | solution.py:336
  188.1 0.0 collective-permute-done.16
  188.1 0.0 collective-permute-done.15
  188.1 1.1 collective-permute-done.14
  189.3 0.0 all-to-all-done.3.in_ref
  189.3 1.0 shard_map.129
  (5 shorter events, 0.0 us)
Async XLA Ops:
  2.6 15.3 %copy-start = (bf16[1,128,1024]{2,1,0:T(8,128)(2,1)S(1)}, bf16[1,128,1024]{2,1,0:T(8,128)(2,1)}, u32[]{:S(2)}) copy-start(bf16[1,128,1024]{2,1,0:T(8,128)(2,1)} %param.10) | copy-start | bytes 786436
  2.6 15.3 %copy-start.1 = (bf16[1,128,1024]{2,1,0:T(8,128)(2,1)S(1)}, bf16[1,128,1024]{2,1,0:T(8,128)(2,1)}, u32[]{:S(2)}) copy-start(bf16[1,128,1024]{2,1,0:T(8,128)(2,1)} %param.13) | copy-start | bytes 786436
  2.6 15.3 %copy-start.2 = (bf16[1,128,1024]{2,1,0:T(8,128)(2,1)S(1)}, bf16[1,128,1024]{2,1,0:T(8,128)(2,1)}, u32[]{:S(2)}) copy-start(bf16[1,128,1024]{2,1,0:T(8,128)(2,1)} %param.7) | copy-start | bytes 786436
  2.6 41.2 %all-to-all-start.1 = ((bf16[4,256,256]{2,1,0:T(8,128)(2,1)}), bf16[4,256,256]{2,1,0:T(8,128)(2,1)S(1)}, u32[]{:S(2)}, u32[]{:S(2)}) async-start(bf16[4,256,256]{2,1,0:T(8,128)(2,1)} %shard_map.119), calls=%async_computation.1 | async-start | bytes 1048576 | tf_op jit(solution)/shard_map/all_to_all | solution.py:349
  17.9 0.7 copy-start.3
  43.8 28.9 %all-to-all-start = ((bf16[4,256,256]{2,1,0:T(8,128)(2,1)}), bf16[4,256,256]{2,1,0:T(8,128)(2,1)S(1)}, u32[]{:S(2)}, u32[]{:S(2)}) async-start(bf16[4,256,256]{2,1,0:T(8,128)(2,1)} %shard_map.118), calls=%async_computation | async-start | bytes 1048576 | tf_op jit(solution)/shard_map/all_to_all | solution.py:349
  53.2 21.1 %collective-permute-start.1 = (bf16[4,256,256]{2,1,0:T(8,128)(2,1)S(1)}, bf16[4,256,256]{2,1,0:T(8,128)(2,1)S(1)}, u32[]{:S(2)}, u32[]{:S(2)}) collective-permute-start(bf16[4,256,256]{2,1,0:T(8,128)(2,1)S(1)} %all-to-all-done.1.kv0_ref), channel_id=1, source_target_pairs={{0,256},{32,288},{64,320},{96,352},{128,384},{160,416},{192,448},{... | collective-permute-start | bytes 1572872 | tf_op jit(solution)/shard_map/ppermute | solution.py:378
  54.5 19.9 %collective-permute-start = (bf16[4,256,256]{2,1,0:T(8,128)(2,1)S(1)}, bf16[4,256,256]{2,1,0:T(8,128)(2,1)S(1)}, u32[]{:S(2)}, u32[]{:S(2)}) collective-permute-start(bf16[4,256,256]{2,1,0:T(8,128)(2,1)S(1)} %all-to-all-done.1.kv0_ref), channel_id=1, source_target_pairs={{0,128},{32,160},{64,192},{96,224},{128,256},{160,288},{192,320},{... | collective-permute-start | bytes 1572872 | tf_op jit(solution)/shard_map/ppermute | solution.py:378
  55.8 0.7 copy-start.4
  104.8 37.8 %collective-permute-start.5 = (bf16[4,256,256]{2,1,0:T(8,128)(2,1)S(1)}, bf16[4,256,256]{2,1,0:T(8,128)(2,1)S(1)}, u32[]{:S(2)}, u32[]{:S(2)}) collective-permute-start(bf16[4,256,256]{2,1,0:T(8,128)(2,1)S(1)} %get-tuple-element.34), channel_id=1, source_target_pairs={{128,0},{160,32},{192,64},{224,96},{256,128},{288,160},{320,192},{... | collective-permute-start | bytes 1572872 | tf_op jit(solution)/shard_map/ppermute | solution.py:378
  114.8 27.9 %collective-permute-start.6 = (bf16[4,256,256]{2,1,0:T(8,128)(2,1)S(1)}, bf16[4,256,256]{2,1,0:T(8,128)(2,1)S(1)}, u32[]{:S(2)}, u32[]{:S(2)}) collective-permute-start(bf16[4,256,256]{2,1,0:T(8,128)(2,1)S(1)} %get-tuple-element.44), channel_id=1, source_target_pairs={{256,0},{288,32},{320,64},{352,96},{384,128},{416,160},{448,192},{... | collective-permute-start | bytes 1572872 | tf_op jit(solution)/shard_map/ppermute | solution.py:378
  116.9 14.2 %collective-permute-start.2 = (bf16[144,256]{1,0:T(8,128)(2,1)S(1)}, bf16[144,256]{1,0:T(8,128)(2,1)S(1)}, u32[]{:S(2)}, u32[]{:S(2)}) collective-permute-start(bf16[144,256]{1,0:T(8,128)(2,1)S(1)} %get-tuple-element.37), channel_id=1, source_target_pairs={{0,32},{32,64},{64,96},{96,0},{128,160},{160,192},{192,224},{224,1... | collective-permute-start | bytes 221192 | tf_op jit(solution)/shard_map/ppermute | solution.py:354
  119.3 16.1 %collective-permute-start.3 = (bf16[144,256]{1,0:T(8,128)(2,1)S(1)}, bf16[144,256]{1,0:T(8,128)(2,1)S(1)}, u32[]{:S(2)}, u32[]{:S(2)}) collective-permute-start(bf16[144,256]{1,0:T(8,128)(2,1)S(1)} %get-tuple-element.38), channel_id=1, source_target_pairs={{0,64},{32,96},{64,0},{96,32},{128,192},{160,224},{192,128},{224,1... | collective-permute-start | bytes 221192 | tf_op jit(solution)/shard_map/ppermute | solution.py:354
  126.7 15.4 %collective-permute-start.4 = (bf16[144,256]{1,0:T(8,128)(2,1)S(1)}, bf16[144,256]{1,0:T(8,128)(2,1)S(1)}, u32[]{:S(2)}, u32[]{:S(2)}) collective-permute-start(bf16[144,256]{1,0:T(8,128)(2,1)S(1)} %get-tuple-element.39), channel_id=1, source_target_pairs={{0,96},{32,0},{64,32},{96,64},{128,224},{160,128},{192,160},{224,1... | collective-permute-start | bytes 221192 | tf_op jit(solution)/shard_map/ppermute | solution.py:354
  144.0 45.3 %all-to-all-start.3 = ((bf16[4,384,256]{2,1,0:T(8,128)(2,1)}), bf16[4,384,256]{2,1,0:T(8,128)(2,1)S(1)}, u32[]{:S(2)}, u32[]{:S(2)}) async-start(bf16[4,384,256]{2,1,0:T(8,128)(2,1)} %shard_map.128), calls=%async_computation.3 | async-start | bytes 1572864 | tf_op jit(solution)/shard_map/all_to_all | solution.py:349
  148.7 3.0 %collective-permute-start.7 = (f32[1,1024]{1,0:T(1,128)S(1)}, f32[1,1024]{1,0:T(1,128)S(1)}, u32[]{:S(2)}, u32[]{:S(2)}) collective-permute-start(f32[1,1024]{1,0:T(1,128)S(1)} %shard_map.126), channel_id=1, source_target_pairs={{0,1},{1,0},{2,3},{3,2},{4,5},{5,4},{6,7},{7,6},{8,9},{9,8},{10,11... | collective-permute-start | bytes 12296 | tf_op jit(solution)/shard_map/ppermute | solution.py:372
  151.7 9.8 %collective-permute-start.10 = (f32[1,1024]{1,0:T(1,128)S(1)}, f32[1,1024]{1,0:T(1,128)S(1)}, u32[]{:S(2)}, u32[]{:S(2)}) collective-permute-start(f32[1,1024]{1,0:T(1,128)S(1)} %add.30), channel_id=1, source_target_pairs={{0,6},{1,7},{2,4},{3,5},{4,2},{5,3},{6,0},{7,1},{8,14},{9,15},{10,... | collective-permute-start | bytes 12296 | tf_op jit(solution)/shard_map/ppermute | solution.py:362
  154.7 7.0 %collective-permute-start.9 = (f32[1,1024]{1,0:T(1,128)S(1)}, f32[1,1024]{1,0:T(1,128)S(1)}, u32[]{:S(2)}, u32[]{:S(2)}) collective-permute-start(f32[1,1024]{1,0:T(1,128)S(1)} %add.30), channel_id=1, source_target_pairs={{0,4},{1,5},{2,6},{3,7},{4,0},{5,1},{6,2},{7,3},{8,12},{9,13},{10,... | collective-permute-start | bytes 12296 | tf_op jit(solution)/shard_map/ppermute | solution.py:362
  158.9 5.5 %collective-permute-start.8 = (f32[1,1024]{1,0:T(1,128)S(1)}, f32[1,1024]{1,0:T(1,128)S(1)}, u32[]{:S(2)}, u32[]{:S(2)}) collective-permute-start(f32[1,1024]{1,0:T(1,128)S(1)} %add.30), channel_id=1, source_target_pairs={{0,2},{1,3},{2,0},{3,1},{4,6},{5,7},{6,4},{7,5},{8,10},{9,11},{10,... | collective-permute-start | bytes 12296 | tf_op jit(solution)/shard_map/ppermute | solution.py:362
  164.4 9.8 %collective-permute-start.13 = (f32[1,1024]{1,0:T(1,128)S(1)}, f32[1,1024]{1,0:T(1,128)S(1)}, u32[]{:S(2)}, u32[]{:S(2)}) collective-permute-start(f32[1,1024]{1,0:T(1,128)S(1)} %add_add_fusion.2), channel_id=1, source_target_pairs={{0,384},{32,416},{64,448},{96,480},{128,256},{160,288},{192,320},{... | collective-permute-start | bytes 12296 | tf_op jit(solution)/shard_map/ppermute | solution.py:362
  166.4 7.9 %collective-permute-start.12 = (f32[1,1024]{1,0:T(1,128)S(1)}, f32[1,1024]{1,0:T(1,128)S(1)}, u32[]{:S(2)}, u32[]{:S(2)}) collective-permute-start(f32[1,1024]{1,0:T(1,128)S(1)} %add_add_fusion.2), channel_id=1, source_target_pairs={{0,256},{32,288},{64,320},{96,352},{128,384},{160,416},{192,448},{... | collective-permute-start | bytes 12296 | tf_op jit(solution)/shard_map/ppermute | solution.py:362
  170.4 5.5 %collective-permute-start.11 = (f32[1,1024]{1,0:T(1,128)S(1)}, f32[1,1024]{1,0:T(1,128)S(1)}, u32[]{:S(2)}, u32[]{:S(2)}) collective-permute-start(f32[1,1024]{1,0:T(1,128)S(1)} %add_add_fusion.2), channel_id=1, source_target_pairs={{0,128},{32,160},{64,192},{96,224},{128,0},{160,32},{192,64},{224,... | collective-permute-start | bytes 12296 | tf_op jit(solution)/shard_map/ppermute | solution.py:362
  176.0 12.1 %collective-permute-start.16 = (f32[1,1024]{1,0:T(1,128)S(1)}, f32[1,1024]{1,0:T(1,128)S(1)}, u32[]{:S(2)}, u32[]{:S(2)}) collective-permute-start(f32[1,1024]{1,0:T(1,128)S(1)} %add_add_fusion.1), channel_id=1, source_target_pairs={{0,24},{1,25},{2,26},{3,27},{4,28},{5,29},{6,30},{7,31},{8,16},{9,... | collective-permute-start | bytes 12296 | tf_op jit(solution)/shard_map/ppermute | solution.py:362
  177.9 10.2 %collective-permute-start.15 = (f32[1,1024]{1,0:T(1,128)S(1)}, f32[1,1024]{1,0:T(1,128)S(1)}, u32[]{:S(2)}, u32[]{:S(2)}) collective-permute-start(f32[1,1024]{1,0:T(1,128)S(1)} %add_add_fusion.1), channel_id=1, source_target_pairs={{0,16},{1,17},{2,18},{3,19},{4,20},{5,21},{6,22},{7,23},{8,24},{9,... | collective-permute-start | bytes 12296 | tf_op jit(solution)/shard_map/ppermute | solution.py:362
  183.8 5.5 %collective-permute-start.14 = (f32[1,1024]{1,0:T(1,128)S(1)}, f32[1,1024]{1,0:T(1,128)S(1)}, u32[]{:S(2)}, u32[]{:S(2)}) collective-permute-start(f32[1,1024]{1,0:T(1,128)S(1)} %add_add_fusion.1), channel_id=1, source_target_pairs={{0,8},{1,9},{2,10},{3,11},{4,12},{5,13},{6,14},{7,15},{8,0},{9,1},... | collective-permute-start | bytes 12296 | tf_op jit(solution)/shard_map/ppermute | solution.py:362

commit v5 on v4

--- a/solution.py
+++ b/solution.py
@@ -365,6 +365,14 @@
     return (array + others[0]) + (others[1] + others[2])
 
 
+def add_bits(array, axis, bits):
+    size = lax.axis_size(axis)
+    for bit in bits:
+        if bit < size:
+            array = array + lax.ppermute(array, axis, [(i, i ^ bit) for i in range(size)])
+    return array
+
+
 def add_pairs(array, axis):
     size = lax.axis_size(axis)
     if size == 1:
@@ -469,7 +477,7 @@
     (joined,) = call(join_kernel, [shape((ZS, 3 * ROWS, PAIR), BF16)], dq, dkv, from1, from2)
     gain_sum, joined = lax.optimization_barrier((gain_sum, joined))
     gain_sum = add_pairs(gain_sum, "own")
-    gain_sum = add_over(add_over(add_over(gain_sum, "own", 2), "seq", 4), "own", 8)
+    gain_sum = add_bits(add_bits(add_bits(gain_sum, "own", (2, 4)), "seq", (4, 8)), "own", (8, 16))
     grad_q, grad_k, grad_v, grad_gain = call(
         unpack_kernel,
         [shape((rows, width), BF16)] * 3 + [shape((1, width), F32)],

time: 191 us -> 192 us (level)
  starting transfers between devices: 86.9 us -> 78.2 us
  waiting for transfers between devices: 58.2 us -> 64.3 us
  Pallas kernels: 17.4 us -> 19.5 us
    ppermute x9 -> x6, waiting for transfers between devices: 5.65 us -> 16.1 us  [add_bits(): lax.ppermute(array, axis, [(i, i ^ bit) for i in range(size)])]
    ppermute x9 -> x6, starting transfers between devices: 29.7 us -> 22.9 us  [add_bits(): lax.ppermute(array, axis, [(i, i ^ bit) for i in range(size)])]
    ppermute x4, starting transfers between devices: 13.8 us -> 8.82 us  [shift_y(): return lax.ppermute(array, 'seq', pairs)]
    ppermute x3, waiting for transfers between devices: 11 us -> 6.68 us  [shift_z(): return lax.ppermute(array, 'seq', pairs)]
    all_to_all x3, starting transfers between devices: 29.3 us -> 32.5 us  [along_z(): lax.all_to_all(array, 'seq', 0, 0, axis_index_groups=groups, tiled=True)]
    pallas_call x12, Pallas kernels: 17.4 us -> 19.5 us  [call(): pl.pallas_call(kernel, out_shape=outs, in_specs=specs, out_specs=[pl.Bloc...]
  transfers between devices with their start and end apart: 20 -> 17, of which waited for: 9 -> 11; matrix products, arithmetic and copies ran while one was open for 0% -> 0% of each run, Pallas kernels for 4% -> 4%
where the time goes in v5:
time: 192 us; the launch traced here: 190 us
  starting transfers between devices  78.2 us (41%)
  waiting for transfers between devices  64.3 us (33%)
  blocking collectives  25.2 us (13%)
  Pallas kernels  19.5 us (10%)
    all_to_all x3, waiting for transfers between devices, along_z(): lax.all_to_all(array, 'seq', 0, 0, axis_index_groups=groups, tiled=True)  40.3 us
    all_to_all x3, starting transfers between devices, along_z(): lax.all_to_all(array, 'seq', 0, 0, axis_index_groups=groups, tiled=True)  32.5 us
    all_to_all x1, blocking collectives, along_z(): lax.all_to_all(array, 'seq', 0, 0, axis_index_groups=groups, tiled=True)  25.2 us
    ppermute x6, starting transfers between devices, add_bits(): lax.ppermute(array, axis, [(i, i ^ bit) for i in range(size)])  22.9 us
    pallas_call x12, Pallas kernels, call(): pl.pallas_call(kernel, out_shape=outs, in_specs=specs, out_specs=[pl.Bloc...  19.5 us
    ppermute x6, waiting for transfers between devices, add_bits(): lax.ppermute(array, axis, [(i, i ^ bit) for i in range(size)])  16.1 us
    ppermute x3, starting transfers between devices, shift_z(): return lax.ppermute(array, 'seq', pairs)  12.2 us
    ppermute x4, starting transfers between devices, shift_y(): return lax.ppermute(array, 'seq', pairs)  8.82 us
  transfers between devices with their start and end apart: 17, of which 11 were waited for; matrix products, arithmetic and copies ran while one was open for 0% of the time, Pallas kernels for 4%

profile of v5, /device:TPU:24, one launch (start us, length us, event | category | flops | bytes accessed | tf_op | source)
XLA Modules:
  0.0 189.8 jit_solution(9191838587696613107)
XLA Ops:
  0.6 1.9 %shard_map.119 = bf16[4,256,256]{2,1,0:T(8,128)(2,1)} custom-call(bf16[128,1024]{1,0:T(8,128)(2,1)} %bitcast.23, bf16[128,1024]{1,0:T(8,128)(2,1)} %bitcast.24), custom_call_target="tpu_custom_call" | custom-call | flops 1 | tf_op jit(solution)/shard_map/pallas_call | solution.py:336
  2.6 0.0 copy-start
  2.6 0.0 copy-start.1
  2.6 0.0 copy-start.2
  2.6 15.2 %all-to-all-start.1 = ((bf16[4,256,256]{2,1,0:T(8,128)(2,1)}), bf16[4,256,256]{2,1,0:T(8,128)(2,1)S(1)}, u32[]{:S(2)}, u32[]{:S(2)}) async-start(bf16[4,256,256]{2,1,0:T(8,128)(2,1)} %shard_map.119), calls=%async_computation.1 | async-start | bytes 1048576 | tf_op jit(solution)/shard_map/all_to_all | solution.py:349
  17.9 0.0 copy-start.3
  17.9 0.0 copy-done
  17.9 0.0 copy-done.1
  17.9 0.0 copy-done.2
  17.9 0.7 copy-done.3
  18.5 0.9 shard_map.118
  19.4 24.3 %all-to-all-done.1.kv0_ref = bf16[4,256,256]{2,1,0:T(8,128)(2,1)S(1)} async-done(((bf16[4,256,256]{2,1,0:T(8,128)(2,1)}), bf16[4,256,256]{2,1,0:T(8,128)(2,1)S(1)}, u32[]{:S(2)}, u32[]{:S(2)}) %all-to-all-start.1) | async-done | bytes 524320 | tf_op jit(solution)/shard_map/all_to_all | solution.py:349
  43.8 9.4 %all-to-all-start = ((bf16[4,256,256]{2,1,0:T(8,128)(2,1)}), bf16[4,256,256]{2,1,0:T(8,128)(2,1)S(1)}, u32[]{:S(2)}, u32[]{:S(2)}) async-start(bf16[4,256,256]{2,1,0:T(8,128)(2,1)} %shard_map.118), calls=%async_computation | async-start | bytes 1048576 | tf_op jit(solution)/shard_map/all_to_all | solution.py:349
  53.2 1.3 collective-permute-start.1
  54.5 1.3 collective-permute-start
  55.8 0.0 copy-start.4
  55.8 0.6 copy-done.4
  56.5 0.2 reduce-window.9
  56.7 0.1 pad_add_fusion.info
  56.7 16.0 %all-to-all-done.qd_ref = bf16[4,256,256]{2,1,0:T(8,128)(2,1)S(1)} async-done(((bf16[4,256,256]{2,1,0:T(8,128)(2,1)}), bf16[4,256,256]{2,1,0:T(8,128)(2,1)S(1)}, u32[]{:S(2)}, u32[]{:S(2)}) %all-to-all-start) | async-done | bytes 524320 | tf_op jit(solution)/shard_map/all_to_all | solution.py:349
  72.7 1.6 shard_map.120.sum_ref
  74.3 0.0 collective-permute-done.1.kv2_ref
  74.4 0.0 collective-permute-done.kv1_ref
  74.4 2.9 %shard_map.121 = (f32[512,256]{1,0:T(8,128)S(1)}, f32[4,16,128]{2,1,0:T(8,128)S(1)}) custom-call(s32[5]{0:T(128)S(1)} %pad_add_fusion.info, bf16[4,256,256]{2,1,0:T(8,128)(2,1)S(1)} %all-to-all-done.qd_ref, bf16[4,256,256]{2,1,0:T(8,128)(2,1)S(1)} %collective-permute-done.kv1_ref, bf16[4,256,256]{2,1,0:T(8,128)(2,1)S(1)} %collective-permute-done.1.kv2_ref, ...), custom_call_target="tpu_custom_call" | custom-call | flops 1 | tf_op jit(solution)/shard_map/pallas_call | solution.py:336
  77.3 25.2 %all_to_all.20.stats_ref = f32[4,16,128]{2,1,0:T(8,128)S(1)} all-to-all(f32[4,16,128]{2,1,0:T(8,128)S(1)} %get-tuple-element.30), channel_id=1, replica_groups={{0,32,64,96},{128,160,192,224},{256,288,320,352},{384,416,448,480},{1,3..., dimensions={0} | all-to-all | bytes 65536 | tf_op jit(solution)/shard_map/all_to_all | solution.py:349
  102.5 1.3 shard_map.122
  103.8 3.1 %shard_map.123 = (bf16[4,256,256]{2,1,0:T(8,128)(2,1)S(1)}, f32[256,512]{1,0:T(8,128)S(1)}) custom-call(s32[5]{0:T(128)S(1)} %pad_add_fusion.info, bf16[4,256,256]{2,1,0:T(8,128)(2,1)S(1)} %all-to-all-done.qd_ref, bf16[4,256,256]{2,1,0:T(8,128)(2,1)S(1)} %collective-permute-done.kv1_ref, bf16[4,128,256]{2,1,0:T(8,128)(2,1)S(1)} %get-tuple-element.32.grad_ref, ...), custom_call_target="tpu_custom_call" | custom-call | flops 1 | tf_op jit(solution)/shard_map/pallas_call | solution.py:336
  106.9 2.4 %collective-permute-start.5 = (bf16[4,256,256]{2,1,0:T(8,128)(2,1)S(1)}, bf16[4,256,256]{2,1,0:T(8,128)(2,1)S(1)}, u32[]{:S(2)}, u32[]{:S(2)}) collective-permute-start(bf16[4,256,256]{2,1,0:T(8,128)(2,1)S(1)} %get-tuple-element.34), channel_id=1, source_target_pairs={{128,0},{160,32},{192,64},{224,96},{256,128},{288,160},{320,192},{... | collective-permute-start | bytes 1572872 | tf_op jit(solution)/shard_map/ppermute | solution.py:386
  109.3 3.9 %collective-permute-start.6 = (bf16[4,256,256]{2,1,0:T(8,128)(2,1)S(1)}, bf16[4,256,256]{2,1,0:T(8,128)(2,1)S(1)}, u32[]{:S(2)}, u32[]{:S(2)}) collective-permute-start(bf16[4,256,256]{2,1,0:T(8,128)(2,1)S(1)} %get-tuple-element.44), channel_id=1, source_target_pairs={{256,0},{288,32},{320,64},{352,96},{384,128},{416,160},{448,192},{... | collective-permute-start | bytes 1572872 | tf_op jit(solution)/shard_map/ppermute | solution.py:386
  113.2 0.8 shard_map.124
  114.0 2.5 %collective-permute-start.2 = (bf16[144,256]{1,0:T(8,128)(2,1)S(1)}, bf16[144,256]{1,0:T(8,128)(2,1)S(1)}, u32[]{:S(2)}, u32[]{:S(2)}) collective-permute-start(bf16[144,256]{1,0:T(8,128)(2,1)S(1)} %get-tuple-element.37), channel_id=1, source_target_pairs={{0,32},{32,64},{64,96},{96,0},{128,160},{160,192},{192,224},{224,1... | collective-permute-start | bytes 221192 | tf_op jit(solution)/shard_map/ppermute | solution.py:354
  116.4 7.4 %collective-permute-start.3 = (bf16[144,256]{1,0:T(8,128)(2,1)S(1)}, bf16[144,256]{1,0:T(8,128)(2,1)S(1)}, u32[]{:S(2)}, u32[]{:S(2)}) collective-permute-start(bf16[144,256]{1,0:T(8,128)(2,1)S(1)} %get-tuple-element.38), channel_id=1, source_target_pairs={{0,64},{32,96},{64,0},{96,32},{128,192},{160,224},{192,128},{224,1... | collective-permute-start | bytes 221192 | tf_op jit(solution)/shard_map/ppermute | solution.py:354
  123.8 2.4 %collective-permute-start.4 = (bf16[144,256]{1,0:T(8,128)(2,1)S(1)}, bf16[144,256]{1,0:T(8,128)(2,1)S(1)}, u32[]{:S(2)}, u32[]{:S(2)}) collective-permute-start(bf16[144,256]{1,0:T(8,128)(2,1)S(1)} %get-tuple-element.39), channel_id=1, source_target_pairs={{0,96},{32,0},{64,32},{96,64},{128,224},{160,128},{192,160},{224,1... | collective-permute-start | bytes 221192 | tf_op jit(solution)/shard_map/ppermute | solution.py:354
  126.2 2.1 %shard_map.127 = (f32[256,512]{1,0:T(8,128)S(1)}, f32[4,256,256]{2,1,0:T(8,128)S(1)}) custom-call(s32[5]{0:T(128)S(1)} %pad_add_fusion.info, bf16[4,256,256]{2,1,0:T(8,128)(2,1)S(1)} %all-to-all-done.qd_ref, bf16[4,256,256]{2,1,0:T(8,128)(2,1)S(1)} %all-to-all-done.1.kv0_ref, bf16[4,128,256]{2,1,0:T(8,128)(2,1)S(1)} %get-tuple-element.32.grad_ref, ...), custom_call_target="tpu_custom_call" | custom-call | flops 1 | tf_op jit(solution)/shard_map/pallas_call | solution.py:336
  128.3 0.0 collective-permute-done.2.in1_ref
  128.3 3.2 %collective-permute-done.3.in2_ref = bf16[144,256]{1,0:T(8,128)(2,1)S(1)} collective-permute-done((bf16[144,256]{1,0:T(8,128)(2,1)S(1)}, bf16[144,256]{1,0:T(8,128)(2,1)S(1)}, u32[]{:S(2)}, u32[]{:S(2)}) %collective-permute-start.3) | collective-permute-done | bytes 73760 | tf_op jit(solution)/shard_map/ppermute | solution.py:354
  131.5 3.5 %collective-permute-done.4.in3_ref = bf16[144,256]{1,0:T(8,128)(2,1)S(1)} collective-permute-done((bf16[144,256]{1,0:T(8,128)(2,1)S(1)}, bf16[144,256]{1,0:T(8,128)(2,1)S(1)}, u32[]{:S(2)}, u32[]{:S(2)}) %collective-permute-start.4) | collective-permute-done | bytes 73760 | tf_op jit(solution)/shard_map/ppermute | solution.py:354
  135.0 0.6 shard_map.126
  135.5 0.0 collective-permute-done.5.other1_ref
  135.6 0.0 collective-permute-done.6.other2_ref
  135.6 1.3 shard_map.128
  136.9 7.8 %all-to-all-start.3 = ((bf16[4,384,256]{2,1,0:T(8,128)(2,1)}), bf16[4,384,256]{2,1,0:T(8,128)(2,1)S(1)}, u32[]{:S(2)}, u32[]{:S(2)}) async-start(bf16[4,384,256]{2,1,0:T(8,128)(2,1)} %shard_map.128), calls=%async_computation.3 | async-start | bytes 1572864 | tf_op jit(solution)/shard_map/all_to_all | solution.py:349
  144.7 1.9 %collective-permute-start.7 = (f32[1,1024]{1,0:T(1,128)S(1)}, f32[1,1024]{1,0:T(1,128)S(1)}, u32[]{:S(2)}, u32[]{:S(2)}) collective-permute-start(f32[1,1024]{1,0:T(1,128)S(1)} %shard_map.126), channel_id=1, source_target_pairs={{0,1},{1,0},{2,3},{3,2},{4,5},{5,4},{6,7},{7,6},{8,9},{9,8},{10,11... | collective-permute-start | bytes 12296 | tf_op jit(solution)/shard_map/ppermute | solution.py:380
  146.6 1.1 collective-permute-done.7
  147.7 7.2 %collective-permute-start.8 = (f32[1,1024]{1,0:T(1,128)S(1)}, f32[1,1024]{1,0:T(1,128)S(1)}, u32[]{:S(2)}, u32[]{:S(2)}) collective-permute-start(f32[1,1024]{1,0:T(1,128)S(1)} %add.21), channel_id=1, source_target_pairs={{0,2},{1,3},{2,0},{3,1},{4,6},{5,7},{6,4},{7,5},{8,10},{9,11},{10,... | collective-permute-start | bytes 12296 | tf_op jit(solution)/shard_map/ppermute | solution.py:372
  155.0 1.6 collective-permute-done.8
  156.5 5.9 %collective-permute-start.9 = (f32[1,1024]{1,0:T(1,128)S(1)}, f32[1,1024]{1,0:T(1,128)S(1)}, u32[]{:S(2)}, u32[]{:S(2)}) collective-permute-start(f32[1,1024]{1,0:T(1,128)S(1)} %add.22), channel_id=1, source_target_pairs={{0,4},{1,5},{2,6},{3,7},{4,0},{5,1},{6,2},{7,3},{8,12},{9,13},{10,... | collective-permute-start | bytes 12296 | tf_op jit(solution)/shard_map/ppermute | solution.py:372
  162.4 1.6 collective-permute-done.9
  164.0 1.9 %collective-permute-start.10 = (f32[1,1024]{1,0:T(1,128)S(1)}, f32[1,1024]{1,0:T(1,128)S(1)}, u32[]{:S(2)}, u32[]{:S(2)}) collective-permute-start(f32[1,1024]{1,0:T(1,128)S(1)} %add.23), channel_id=1, source_target_pairs={{0,128},{32,160},{64,192},{96,224},{128,0},{160,32},{192,64},{224,... | collective-permute-start | bytes 12296 | tf_op jit(solution)/shard_map/ppermute | solution.py:372
  165.9 3.6 %collective-permute-done.10 = f32[1,1024]{1,0:T(1,128)S(1)} collective-permute-done((f32[1,1024]{1,0:T(1,128)S(1)}, f32[1,1024]{1,0:T(1,128)S(1)}, u32[]{:S(2)}, u32[]{:S(2)}) %collective-permute-start.10) | collective-permute-done | bytes 4128 | tf_op jit(solution)/shard_map/ppermute | solution.py:372
  169.5 1.9 %collective-permute-start.11 = (f32[1,1024]{1,0:T(1,128)S(1)}, f32[1,1024]{1,0:T(1,128)S(1)}, u32[]{:S(2)}, u32[]{:S(2)}) collective-permute-start(f32[1,1024]{1,0:T(1,128)S(1)} %add.24), channel_id=1, source_target_pairs={{0,256},{32,288},{64,320},{96,352},{128,384},{160,416},{192,448},{... | collective-permute-start | bytes 12296 | tf_op jit(solution)/shard_map/ppermute | solution.py:372
  171.4 5.1 %collective-permute-done.11 = f32[1,1024]{1,0:T(1,128)S(1)} collective-permute-done((f32[1,1024]{1,0:T(1,128)S(1)}, f32[1,1024]{1,0:T(1,128)S(1)}, u32[]{:S(2)}, u32[]{:S(2)}) %collective-permute-start.11) | collective-permute-done | bytes 4128 | tf_op jit(solution)/shard_map/ppermute | solution.py:372
  176.5 3.4 %collective-permute-start.12 = (f32[1,1024]{1,0:T(1,128)S(1)}, f32[1,1024]{1,0:T(1,128)S(1)}, u32[]{:S(2)}, u32[]{:S(2)}) collective-permute-start(f32[1,1024]{1,0:T(1,128)S(1)} %add.25), channel_id=1, source_target_pairs={{0,8},{1,9},{2,10},{3,11},{4,12},{5,13},{6,14},{7,15},{8,0},{9,1},... | collective-permute-start | bytes 12296 | tf_op jit(solution)/shard_map/ppermute | solution.py:372
  179.8 2.5 %collective-permute-done.12 = f32[1,1024]{1,0:T(1,128)S(1)} collective-permute-done((f32[1,1024]{1,0:T(1,128)S(1)}, f32[1,1024]{1,0:T(1,128)S(1)}, u32[]{:S(2)}, u32[]{:S(2)}) %collective-permute-start.12) | collective-permute-done | bytes 4128 | tf_op jit(solution)/shard_map/ppermute | solution.py:372
  182.4 2.6 %collective-permute-start.13 = (f32[1,1024]{1,0:T(1,128)S(1)}, f32[1,1024]{1,0:T(1,128)S(1)}, u32[]{:S(2)}, u32[]{:S(2)}) collective-permute-start(f32[1,1024]{1,0:T(1,128)S(1)} %add.26), channel_id=1, source_target_pairs={{0,16},{1,17},{2,18},{3,19},{4,20},{5,21},{6,22},{7,23},{8,24},{9,... | collective-permute-start | bytes 12296 | tf_op jit(solution)/shard_map/ppermute | solution.py:372
  185.0 2.0 %shard_map.125 = (bf16[128,1024]{1,0:T(8,128)(2,1)}, bf16[128,1024]{1,0:T(8,128)(2,1)}) custom-call(s32[5]{0:T(128)S(1)} %pad_add_fusion.info, bf16[144,256]{1,0:T(8,128)(2,1)S(1)} %get-tuple-element.36.in0_ref, bf16[144,256]{1,0:T(8,128)(2,1)S(1)} %collective-permute-done.2.in1_ref, bf16[144,256]{1,0:T(8,128)(2,1)S(1)} %collective-permute-done.3.in2_ref, ...), custom_call_target="tpu_custom_call" | custom-call | flops 1 | tf_op jit(solution)/shard_map/pallas_call | solution.py:336
  187.0 1.8 collective-permute-done.13
  188.8 0.0 all-to-all-done.3.in_ref
  188.8 1.0 shard_map.129
  (7 shorter events, 0.0 us)
Async XLA Ops:
  2.6 15.3 %copy-start = (bf16[1,128,1024]{2,1,0:T(8,128)(2,1)S(1)}, bf16[1,128,1024]{2,1,0:T(8,128)(2,1)}, u32[]{:S(2)}) copy-start(bf16[1,128,1024]{2,1,0:T(8,128)(2,1)} %param.10) | copy-start | bytes 786436
  2.6 15.3 %copy-start.1 = (bf16[1,128,1024]{2,1,0:T(8,128)(2,1)S(1)}, bf16[1,128,1024]{2,1,0:T(8,128)(2,1)}, u32[]{:S(2)}) copy-start(bf16[1,128,1024]{2,1,0:T(8,128)(2,1)} %param.13) | copy-start | bytes 786436
  2.6 15.3 %copy-start.2 = (bf16[1,128,1024]{2,1,0:T(8,128)(2,1)S(1)}, bf16[1,128,1024]{2,1,0:T(8,128)(2,1)}, u32[]{:S(2)}) copy-start(bf16[1,128,1024]{2,1,0:T(8,128)(2,1)} %param.7) | copy-start | bytes 786436
  2.6 41.2 %all-to-all-start.1 = ((bf16[4,256,256]{2,1,0:T(8,128)(2,1)}), bf16[4,256,256]{2,1,0:T(8,128)(2,1)S(1)}, u32[]{:S(2)}, u32[]{:S(2)}) async-start(bf16[4,256,256]{2,1,0:T(8,128)(2,1)} %shard_map.119), calls=%async_computation.1 | async-start | bytes 1048576 | tf_op jit(solution)/shard_map/all_to_all | solution.py:349
  17.9 0.7 copy-start.3
  43.8 28.9 %all-to-all-start = ((bf16[4,256,256]{2,1,0:T(8,128)(2,1)}), bf16[4,256,256]{2,1,0:T(8,128)(2,1)S(1)}, u32[]{:S(2)}, u32[]{:S(2)}) async-start(bf16[4,256,256]{2,1,0:T(8,128)(2,1)} %shard_map.118), calls=%async_computation | async-start | bytes 1048576 | tf_op jit(solution)/shard_map/all_to_all | solution.py:349
  53.2 21.1 %collective-permute-start.1 = (bf16[4,256,256]{2,1,0:T(8,128)(2,1)S(1)}, bf16[4,256,256]{2,1,0:T(8,128)(2,1)S(1)}, u32[]{:S(2)}, u32[]{:S(2)}) collective-permute-start(bf16[4,256,256]{2,1,0:T(8,128)(2,1)S(1)} %all-to-all-done.1.kv0_ref), channel_id=1, source_target_pairs={{0,256},{32,288},{64,320},{96,352},{128,384},{160,416},{192,448},{... | collective-permute-start | bytes 1572872 | tf_op jit(solution)/shard_map/ppermute | solution.py:386
  54.5 19.8 %collective-permute-start = (bf16[4,256,256]{2,1,0:T(8,128)(2,1)S(1)}, bf16[4,256,256]{2,1,0:T(8,128)(2,1)S(1)}, u32[]{:S(2)}, u32[]{:S(2)}) collective-permute-start(bf16[4,256,256]{2,1,0:T(8,128)(2,1)S(1)} %all-to-all-done.1.kv0_ref), channel_id=1, source_target_pairs={{0,128},{32,160},{64,192},{96,224},{128,256},{160,288},{192,320},{... | collective-permute-start | bytes 1572872 | tf_op jit(solution)/shard_map/ppermute | solution.py:386
  55.8 0.7 copy-start.4
  106.9 28.6 %collective-permute-start.5 = (bf16[4,256,256]{2,1,0:T(8,128)(2,1)S(1)}, bf16[4,256,256]{2,1,0:T(8,128)(2,1)S(1)}, u32[]{:S(2)}, u32[]{:S(2)}) collective-permute-start(bf16[4,256,256]{2,1,0:T(8,128)(2,1)S(1)} %get-tuple-element.34), channel_id=1, source_target_pairs={{128,0},{160,32},{192,64},{224,96},{256,128},{288,160},{320,192},{... | collective-permute-start | bytes 1572872 | tf_op jit(solution)/shard_map/ppermute | solution.py:386
  109.3 26.3 %collective-permute-start.6 = (bf16[4,256,256]{2,1,0:T(8,128)(2,1)S(1)}, bf16[4,256,256]{2,1,0:T(8,128)(2,1)S(1)}, u32[]{:S(2)}, u32[]{:S(2)}) collective-permute-start(bf16[4,256,256]{2,1,0:T(8,128)(2,1)S(1)} %get-tuple-element.44), channel_id=1, source_target_pairs={{256,0},{288,32},{320,64},{352,96},{384,128},{416,160},{448,192},{... | collective-permute-start | bytes 1572872 | tf_op jit(solution)/shard_map/ppermute | solution.py:386
  114.0 14.3 %collective-permute-start.2 = (bf16[144,256]{1,0:T(8,128)(2,1)S(1)}, bf16[144,256]{1,0:T(8,128)(2,1)S(1)}, u32[]{:S(2)}, u32[]{:S(2)}) collective-permute-start(bf16[144,256]{1,0:T(8,128)(2,1)S(1)} %get-tuple-element.37), channel_id=1, source_target_pairs={{0,32},{32,64},{64,96},{96,0},{128,160},{160,192},{192,224},{224,1... | collective-permute-start | bytes 221192 | tf_op jit(solution)/shard_map/ppermute | solution.py:354
  116.4 15.1 %collective-permute-start.3 = (bf16[144,256]{1,0:T(8,128)(2,1)S(1)}, bf16[144,256]{1,0:T(8,128)(2,1)S(1)}, u32[]{:S(2)}, u32[]{:S(2)}) collective-permute-start(bf16[144,256]{1,0:T(8,128)(2,1)S(1)} %get-tuple-element.38), channel_id=1, source_target_pairs={{0,64},{32,96},{64,0},{96,32},{128,192},{160,224},{192,128},{224,1... | collective-permute-start | bytes 221192 | tf_op jit(solution)/shard_map/ppermute | solution.py:354
  123.8 11.2 %collective-permute-start.4 = (bf16[144,256]{1,0:T(8,128)(2,1)S(1)}, bf16[144,256]{1,0:T(8,128)(2,1)S(1)}, u32[]{:S(2)}, u32[]{:S(2)}) collective-permute-start(bf16[144,256]{1,0:T(8,128)(2,1)S(1)} %get-tuple-element.39), channel_id=1, source_target_pairs={{0,96},{32,0},{64,32},{96,64},{128,224},{160,128},{192,160},{224,1... | collective-permute-start | bytes 221192 | tf_op jit(solution)/shard_map/ppermute | solution.py:354
  136.9 51.9 %all-to-all-start.3 = ((bf16[4,384,256]{2,1,0:T(8,128)(2,1)}), bf16[4,384,256]{2,1,0:T(8,128)(2,1)S(1)}, u32[]{:S(2)}, u32[]{:S(2)}) async-start(bf16[4,384,256]{2,1,0:T(8,128)(2,1)} %shard_map.128), calls=%async_computation.3 | async-start | bytes 1572864 | tf_op jit(solution)/shard_map/all_to_all | solution.py:349
  144.7 3.0 %collective-permute-start.7 = (f32[1,1024]{1,0:T(1,128)S(1)}, f32[1,1024]{1,0:T(1,128)S(1)}, u32[]{:S(2)}, u32[]{:S(2)}) collective-permute-start(f32[1,1024]{1,0:T(1,128)S(1)} %shard_map.126), channel_id=1, source_target_pairs={{0,1},{1,0},{2,3},{3,2},{4,5},{5,4},{6,7},{7,6},{8,9},{9,8},{10,11... | collective-permute-start | bytes 12296 | tf_op jit(solution)/shard_map/ppermute | solution.py:380
  147.7 8.8 %collective-permute-start.8 = (f32[1,1024]{1,0:T(1,128)S(1)}, f32[1,1024]{1,0:T(1,128)S(1)}, u32[]{:S(2)}, u32[]{:S(2)}) collective-permute-start(f32[1,1024]{1,0:T(1,128)S(1)} %add.21), channel_id=1, source_target_pairs={{0,2},{1,3},{2,0},{3,1},{4,6},{5,7},{6,4},{7,5},{8,10},{9,11},{10,... | collective-permute-start | bytes 12296 | tf_op jit(solution)/shard_map/ppermute | solution.py:372
  156.5 7.4 %collective-permute-start.9 = (f32[1,1024]{1,0:T(1,128)S(1)}, f32[1,1024]{1,0:T(1,128)S(1)}, u32[]{:S(2)}, u32[]{:S(2)}) collective-permute-start(f32[1,1024]{1,0:T(1,128)S(1)} %add.22), channel_id=1, source_target_pairs={{0,4},{1,5},{2,6},{3,7},{4,0},{5,1},{6,2},{7,3},{8,12},{9,13},{10,... | collective-permute-start | bytes 12296 | tf_op jit(solution)/shard_map/ppermute | solution.py:372
  164.0 5.5 %collective-permute-start.10 = (f32[1,1024]{1,0:T(1,128)S(1)}, f32[1,1024]{1,0:T(1,128)S(1)}, u32[]{:S(2)}, u32[]{:S(2)}) collective-permute-start(f32[1,1024]{1,0:T(1,128)S(1)} %add.23), channel_id=1, source_target_pairs={{0,128},{32,160},{64,192},{96,224},{128,0},{160,32},{192,64},{224,... | collective-permute-start | bytes 12296 | tf_op jit(solution)/shard_map/ppermute | solution.py:372
  169.5 7.0 %collective-permute-start.11 = (f32[1,1024]{1,0:T(1,128)S(1)}, f32[1,1024]{1,0:T(1,128)S(1)}, u32[]{:S(2)}, u32[]{:S(2)}) collective-permute-start(f32[1,1024]{1,0:T(1,128)S(1)} %add.24), channel_id=1, source_target_pairs={{0,256},{32,288},{64,320},{96,352},{128,384},{160,416},{192,448},{... | collective-permute-start | bytes 12296 | tf_op jit(solution)/shard_map/ppermute | solution.py:372
  176.5 5.9 %collective-permute-start.12 = (f32[1,1024]{1,0:T(1,128)S(1)}, f32[1,1024]{1,0:T(1,128)S(1)}, u32[]{:S(2)}, u32[]{:S(2)}) collective-permute-start(f32[1,1024]{1,0:T(1,128)S(1)} %add.25), channel_id=1, source_target_pairs={{0,8},{1,9},{2,10},{3,11},{4,12},{5,13},{6,14},{7,15},{8,0},{9,1},... | collective-permute-start | bytes 12296 | tf_op jit(solution)/shard_map/ppermute | solution.py:372
  182.4 6.4 %collective-permute-start.13 = (f32[1,1024]{1,0:T(1,128)S(1)}, f32[1,1024]{1,0:T(1,128)S(1)}, u32[]{:S(2)}, u32[]{:S(2)}) collective-permute-start(f32[1,1024]{1,0:T(1,128)S(1)} %add.26), channel_id=1, source_target_pairs={{0,16},{1,17},{2,18},{3,19},{4,20},{5,21},{6,22},{7,23},{8,24},{9,... | collective-permute-start | bytes 12296 | tf_op jit(solution)/shard_map/ppermute | solution.py:372

commit v6 on v5

--- a/solution.py
+++ b/solution.py
@@ -170,7 +170,8 @@
     heads = [(by, ref, head) for by, ref in enumerate((in0_ref, in1_ref, in2_ref, in3_ref)) for head in range(2)]
     attended = []
     for by, ref, head in heads:
-        mean = to_column(ref[ROWS : ROWS + 1, head_cols(head)].astype(F32))
+        extra = ref[ROWS : ROWS + EXTRA, head_cols(head)].astype(F32)
+        mean = to_column(extra[0:1])
         attended.append(ref[0:ROWS, head_cols(head)].astype(F32) + mean)
     mean = jnp.sum(sum(attended), axis=1, keepdims=True) / width
     center = [block - mean for block in attended]

time: 192 us -> 192 us (level)
  waiting for transfers between devices: 64.3 us -> 72.2 us
  starting transfers between devices: 78.2 us -> 71.2 us
    ppermute x6, starting transfers between devices: 22.9 us -> 17.1 us  [add_bits(): lax.ppermute(array, axis, [(i, i ^ bit) for i in range(size)])]
    ppermute x3, waiting for transfers between devices: 6.68 us -> 12.1 us  [shift_z(): return lax.ppermute(array, 'seq', pairs)]
    all_to_all x3, starting transfers between devices: 32.5 us -> 28.7 us  [along_z(): lax.all_to_all(array, 'seq', 0, 0, axis_index_groups=groups, tiled=True)]
    ppermute x6, waiting for transfers between devices: 16.1 us -> 18.7 us  [add_bits(): lax.ppermute(array, axis, [(i, i ^ bit) for i in range(size)])]
    ppermute x4, starting transfers between devices: 8.82 us -> 11.3 us  [shift_y(): return lax.ppermute(array, 'seq', pairs)]
where the time goes in v6:
time: 192 us; the launch traced here: 190 us
  waiting for transfers between devices  72.2 us (38%)
  starting transfers between devices  71.2 us (37%)
  blocking collectives  25.3 us (13%)
  Pallas kernels  18.7 us (10%)
    all_to_all x3, waiting for transfers between devices, along_z(): lax.all_to_all(array, 'seq', 0, 0, axis_index_groups=groups, tiled=True)  40.3 us
    all_to_all x3, starting transfers between devices, along_z(): lax.all_to_all(array, 'seq', 0, 0, axis_index_groups=groups, tiled=True)  28.7 us
    all_to_all x1, blocking collectives, along_z(): lax.all_to_all(array, 'seq', 0, 0, axis_index_groups=groups, tiled=True)  25.3 us
    pallas_call x12, Pallas kernels, call(): pl.pallas_call(kernel, out_shape=outs, in_specs=specs, out_specs=[pl.Bloc...  18.7 us
    ppermute x6, waiting for transfers between devices, add_bits(): lax.ppermute(array, axis, [(i, i ^ bit) for i in range(size)])  18.7 us
    ppermute x6, starting transfers between devices, add_bits(): lax.ppermute(array, axis, [(i, i ^ bit) for i in range(size)])  17.1 us
    ppermute x3, starting transfers between devices, shift_z(): return lax.ppermute(array, 'seq', pairs)  12.2 us
    ppermute x3, waiting for transfers between devices, shift_z(): return lax.ppermute(array, 'seq', pairs)  12.1 us
  transfers between devices with their start and end apart: 17, of which 11 were waited for; matrix products, arithmetic and copies ran while one was open for 0% of the time, Pallas kernels for 4%

profile of v6, /device:TPU:24, one launch (start us, length us, event | category | flops | bytes accessed | tf_op | source)
XLA Modules:
  0.0 189.9 jit_solution(7677267759423082673)
XLA Ops:
  0.6 1.9 %shard_map.119 = bf16[4,256,256]{2,1,0:T(8,128)(2,1)} custom-call(bf16[128,1024]{1,0:T(8,128)(2,1)} %bitcast.23, bf16[128,1024]{1,0:T(8,128)(2,1)} %bitcast.24), custom_call_target="tpu_custom_call" | custom-call | flops 1 | tf_op jit(solution)/shard_map/pallas_call | solution.py:337
  2.6 0.0 copy-start
  2.6 0.0 copy-start.1
  2.6 0.0 copy-start.2
  2.6 15.2 %all-to-all-start.1 = ((bf16[4,256,256]{2,1,0:T(8,128)(2,1)}), bf16[4,256,256]{2,1,0:T(8,128)(2,1)S(1)}, u32[]{:S(2)}, u32[]{:S(2)}) async-start(bf16[4,256,256]{2,1,0:T(8,128)(2,1)} %shard_map.119), calls=%async_computation.1 | async-start | bytes 1048576 | tf_op jit(solution)/shard_map/all_to_all | solution.py:350
  17.9 0.0 copy-start.3
  17.9 0.0 copy-done
  17.9 0.0 copy-done.1
  17.9 0.0 copy-done.2
  17.9 0.7 copy-done.3
  18.5 0.9 shard_map.118
  19.4 24.3 %all-to-all-done.1.kv0_ref = bf16[4,256,256]{2,1,0:T(8,128)(2,1)S(1)} async-done(((bf16[4,256,256]{2,1,0:T(8,128)(2,1)}), bf16[4,256,256]{2,1,0:T(8,128)(2,1)S(1)}, u32[]{:S(2)}, u32[]{:S(2)}) %all-to-all-start.1) | async-done | bytes 524320 | tf_op jit(solution)/shard_map/all_to_all | solution.py:350
  43.8 9.4 %all-to-all-start = ((bf16[4,256,256]{2,1,0:T(8,128)(2,1)}), bf16[4,256,256]{2,1,0:T(8,128)(2,1)S(1)}, u32[]{:S(2)}, u32[]{:S(2)}) async-start(bf16[4,256,256]{2,1,0:T(8,128)(2,1)} %shard_map.118), calls=%async_computation | async-start | bytes 1048576 | tf_op jit(solution)/shard_map/all_to_all | solution.py:350
  53.2 1.3 collective-permute-start.1
  54.5 1.3 collective-permute-start
  55.8 0.0 copy-start.4
  55.8 0.6 copy-done.4
  56.5 0.2 reduce-window.9
  56.7 0.1 pad_add_fusion.info
  56.7 16.0 %all-to-all-done.qd_ref = bf16[4,256,256]{2,1,0:T(8,128)(2,1)S(1)} async-done(((bf16[4,256,256]{2,1,0:T(8,128)(2,1)}), bf16[4,256,256]{2,1,0:T(8,128)(2,1)S(1)}, u32[]{:S(2)}, u32[]{:S(2)}) %all-to-all-start) | async-done | bytes 524320 | tf_op jit(solution)/shard_map/all_to_all | solution.py:350
  72.7 1.6 shard_map.120.sum_ref
  74.3 0.0 collective-permute-done.1.kv2_ref
  74.4 0.0 collective-permute-done.kv1_ref
  74.4 2.7 %shard_map.121 = (f32[512,256]{1,0:T(8,128)S(1)}, f32[4,16,128]{2,1,0:T(8,128)S(1)}) custom-call(s32[5]{0:T(128)S(1)} %pad_add_fusion.info, bf16[4,256,256]{2,1,0:T(8,128)(2,1)S(1)} %all-to-all-done.qd_ref, bf16[4,256,256]{2,1,0:T(8,128)(2,1)S(1)} %collective-permute-done.kv1_ref, bf16[4,256,256]{2,1,0:T(8,128)(2,1)S(1)} %collective-permute-done.1.kv2_ref, ...), custom_call_target="tpu_custom_call" | custom-call | flops 1 | tf_op jit(solution)/shard_map/pallas_call | solution.py:337
  77.0 25.3 %all_to_all.20.stats_ref = f32[4,16,128]{2,1,0:T(8,128)S(1)} all-to-all(f32[4,16,128]{2,1,0:T(8,128)S(1)} %get-tuple-element.30), channel_id=1, replica_groups={{0,32,64,96},{128,160,192,224},{256,288,320,352},{384,416,448,480},{1,3..., dimensions={0} | all-to-all | bytes 65536 | tf_op jit(solution)/shard_map/all_to_all | solution.py:350
  102.3 1.3 shard_map.122
  103.6 2.5 %shard_map.123 = (bf16[4,256,256]{2,1,0:T(8,128)(2,1)S(1)}, f32[256,512]{1,0:T(8,128)S(1)}) custom-call(s32[5]{0:T(128)S(1)} %pad_add_fusion.info, bf16[4,256,256]{2,1,0:T(8,128)(2,1)S(1)} %all-to-all-done.qd_ref, bf16[4,256,256]{2,1,0:T(8,128)(2,1)S(1)} %collective-permute-done.kv1_ref, bf16[4,128,256]{2,1,0:T(8,128)(2,1)S(1)} %get-tuple-element.32.grad_ref, ...), custom_call_target="tpu_custom_call" | custom-call | flops 1 | tf_op jit(solution)/shard_map/pallas_call | solution.py:337
  106.2 3.1 %collective-permute-start.5 = (bf16[4,256,256]{2,1,0:T(8,128)(2,1)S(1)}, bf16[4,256,256]{2,1,0:T(8,128)(2,1)S(1)}, u32[]{:S(2)}, u32[]{:S(2)}) collective-permute-start(bf16[4,256,256]{2,1,0:T(8,128)(2,1)S(1)} %get-tuple-element.34), channel_id=1, source_target_pairs={{128,0},{160,32},{192,64},{224,96},{256,128},{288,160},{320,192},{... | collective-permute-start | bytes 1572872 | tf_op jit(solution)/shard_map/ppermute | solution.py:387
  109.3 5.6 %collective-permute-start.6 = (bf16[4,256,256]{2,1,0:T(8,128)(2,1)S(1)}, bf16[4,256,256]{2,1,0:T(8,128)(2,1)S(1)}, u32[]{:S(2)}, u32[]{:S(2)}) collective-permute-start(bf16[4,256,256]{2,1,0:T(8,128)(2,1)S(1)} %get-tuple-element.44), channel_id=1, source_target_pairs={{256,0},{288,32},{320,64},{352,96},{384,128},{416,160},{448,192},{... | collective-permute-start | bytes 1572872 | tf_op jit(solution)/shard_map/ppermute | solution.py:387
  114.9 0.8 shard_map.124
  115.6 2.5 %collective-permute-start.2 = (bf16[144,256]{1,0:T(8,128)(2,1)S(1)}, bf16[144,256]{1,0:T(8,128)(2,1)S(1)}, u32[]{:S(2)}, u32[]{:S(2)}) collective-permute-start(bf16[144,256]{1,0:T(8,128)(2,1)S(1)} %get-tuple-element.37), channel_id=1, source_target_pairs={{0,32},{32,64},{64,96},{96,0},{128,160},{160,192},{192,224},{224,1... | collective-permute-start | bytes 221192 | tf_op jit(solution)/shard_map/ppermute | solution.py:355
  118.1 7.4 %collective-permute-start.3 = (bf16[144,256]{1,0:T(8,128)(2,1)S(1)}, bf16[144,256]{1,0:T(8,128)(2,1)S(1)}, u32[]{:S(2)}, u32[]{:S(2)}) collective-permute-start(bf16[144,256]{1,0:T(8,128)(2,1)S(1)} %get-tuple-element.38), channel_id=1, source_target_pairs={{0,64},{32,96},{64,0},{96,32},{128,192},{160,224},{192,128},{224,1... | collective-permute-start | bytes 221192 | tf_op jit(solution)/shard_map/ppermute | solution.py:355
  125.5 2.4 %collective-permute-start.4 = (bf16[144,256]{1,0:T(8,128)(2,1)S(1)}, bf16[144,256]{1,0:T(8,128)(2,1)S(1)}, u32[]{:S(2)}, u32[]{:S(2)}) collective-permute-start(bf16[144,256]{1,0:T(8,128)(2,1)S(1)} %get-tuple-element.39), channel_id=1, source_target_pairs={{0,96},{32,0},{64,32},{96,64},{128,224},{160,128},{192,160},{224,1... | collective-permute-start | bytes 221192 | tf_op jit(solution)/shard_map/ppermute | solution.py:355
  127.9 2.1 %shard_map.127 = (f32[256,512]{1,0:T(8,128)S(1)}, f32[4,256,256]{2,1,0:T(8,128)S(1)}) custom-call(s32[5]{0:T(128)S(1)} %pad_add_fusion.info, bf16[4,256,256]{2,1,0:T(8,128)(2,1)S(1)} %all-to-all-done.qd_ref, bf16[4,256,256]{2,1,0:T(8,128)(2,1)S(1)} %all-to-all-done.1.kv0_ref, bf16[4,128,256]{2,1,0:T(8,128)(2,1)S(1)} %get-tuple-element.32.grad_ref, ...), custom_call_target="tpu_custom_call" | custom-call | flops 1 | tf_op jit(solution)/shard_map/pallas_call | solution.py:337
  130.0 0.0 collective-permute-done.2.in1_ref
  130.0 3.2 %collective-permute-done.3.in2_ref = bf16[144,256]{1,0:T(8,128)(2,1)S(1)} collective-permute-done((bf16[144,256]{1,0:T(8,128)(2,1)S(1)}, bf16[144,256]{1,0:T(8,128)(2,1)S(1)}, u32[]{:S(2)}, u32[]{:S(2)}) %collective-permute-start.3) | collective-permute-done | bytes 73760 | tf_op jit(solution)/shard_map/ppermute | solution.py:355
  133.1 8.9 %collective-permute-done.4.in3_ref = bf16[144,256]{1,0:T(8,128)(2,1)S(1)} collective-permute-done((bf16[144,256]{1,0:T(8,128)(2,1)S(1)}, bf16[144,256]{1,0:T(8,128)(2,1)S(1)}, u32[]{:S(2)}, u32[]{:S(2)}) %collective-permute-start.4) | collective-permute-done | bytes 73760 | tf_op jit(solution)/shard_map/ppermute | solution.py:355
  142.0 0.6 shard_map.126
  142.6 0.0 collective-permute-done.5.other1_ref
  142.6 0.0 collective-permute-done.6.other2_ref
  142.6 1.3 shard_map.128
  143.9 4.0 %all-to-all-start.3 = ((bf16[4,384,256]{2,1,0:T(8,128)(2,1)}), bf16[4,384,256]{2,1,0:T(8,128)(2,1)S(1)}, u32[]{:S(2)}, u32[]{:S(2)}) async-start(bf16[4,384,256]{2,1,0:T(8,128)(2,1)} %shard_map.128), calls=%async_computation.3 | async-start | bytes 1572864 | tf_op jit(solution)/shard_map/all_to_all | solution.py:350
  148.0 1.9 %collective-permute-start.7 = (f32[1,1024]{1,0:T(1,128)S(1)}, f32[1,1024]{1,0:T(1,128)S(1)}, u32[]{:S(2)}, u32[]{:S(2)}) collective-permute-start(f32[1,1024]{1,0:T(1,128)S(1)} %shard_map.126), channel_id=1, source_target_pairs={{0,1},{1,0},{2,3},{3,2},{4,5},{5,4},{6,7},{7,6},{8,9},{9,8},{10,11... | collective-permute-start | bytes 12296 | tf_op jit(solution)/shard_map/ppermute | solution.py:381
  149.9 1.1 collective-permute-done.7
  151.0 1.9 %collective-permute-start.8 = (f32[1,1024]{1,0:T(1,128)S(1)}, f32[1,1024]{1,0:T(1,128)S(1)}, u32[]{:S(2)}, u32[]{:S(2)}) collective-permute-start(f32[1,1024]{1,0:T(1,128)S(1)} %add.21), channel_id=1, source_target_pairs={{0,2},{1,3},{2,0},{3,1},{4,6},{5,7},{6,4},{7,5},{8,10},{9,11},{10,... | collective-permute-start | bytes 12296 | tf_op jit(solution)/shard_map/ppermute | solution.py:373
  153.0 3.6 %collective-permute-done.8 = f32[1,1024]{1,0:T(1,128)S(1)} collective-permute-done((f32[1,1024]{1,0:T(1,128)S(1)}, f32[1,1024]{1,0:T(1,128)S(1)}, u32[]{:S(2)}, u32[]{:S(2)}) %collective-permute-start.8) | collective-permute-done | bytes 4128 | tf_op jit(solution)/shard_map/ppermute | solution.py:373
  156.5 6.4 %collective-permute-start.9 = (f32[1,1024]{1,0:T(1,128)S(1)}, f32[1,1024]{1,0:T(1,128)S(1)}, u32[]{:S(2)}, u32[]{:S(2)}) collective-permute-start(f32[1,1024]{1,0:T(1,128)S(1)} %add.22), channel_id=1, source_target_pairs={{0,4},{1,5},{2,6},{3,7},{4,0},{5,1},{6,2},{7,3},{8,12},{9,13},{10,... | collective-permute-start | bytes 12296 | tf_op jit(solution)/shard_map/ppermute | solution.py:373
  162.9 1.6 collective-permute-done.9
  164.5 1.9 %collective-permute-start.10 = (f32[1,1024]{1,0:T(1,128)S(1)}, f32[1,1024]{1,0:T(1,128)S(1)}, u32[]{:S(2)}, u32[]{:S(2)}) collective-permute-start(f32[1,1024]{1,0:T(1,128)S(1)} %add.23), channel_id=1, source_target_pairs={{0,128},{32,160},{64,192},{96,224},{128,0},{160,32},{192,64},{224,... | collective-permute-start | bytes 12296 | tf_op jit(solution)/shard_map/ppermute | solution.py:373
  166.4 3.6 %collective-permute-done.10 = f32[1,1024]{1,0:T(1,128)S(1)} collective-permute-done((f32[1,1024]{1,0:T(1,128)S(1)}, f32[1,1024]{1,0:T(1,128)S(1)}, u32[]{:S(2)}, u32[]{:S(2)}) %collective-permute-start.10) | collective-permute-done | bytes 4128 | tf_op jit(solution)/shard_map/ppermute | solution.py:373
  170.0 1.9 %collective-permute-start.11 = (f32[1,1024]{1,0:T(1,128)S(1)}, f32[1,1024]{1,0:T(1,128)S(1)}, u32[]{:S(2)}, u32[]{:S(2)}) collective-permute-start(f32[1,1024]{1,0:T(1,128)S(1)} %add.24), channel_id=1, source_target_pairs={{0,256},{32,288},{64,320},{96,352},{128,384},{160,416},{192,448},{... | collective-permute-start | bytes 12296 | tf_op jit(solution)/shard_map/ppermute | solution.py:373
  171.9 5.1 %collective-permute-done.11 = f32[1,1024]{1,0:T(1,128)S(1)} collective-permute-done((f32[1,1024]{1,0:T(1,128)S(1)}, f32[1,1024]{1,0:T(1,128)S(1)}, u32[]{:S(2)}, u32[]{:S(2)}) %collective-permute-start.11) | collective-permute-done | bytes 4128 | tf_op jit(solution)/shard_map/ppermute | solution.py:373
  177.0 3.1 %collective-permute-start.12 = (f32[1,1024]{1,0:T(1,128)S(1)}, f32[1,1024]{1,0:T(1,128)S(1)}, u32[]{:S(2)}, u32[]{:S(2)}) collective-permute-start(f32[1,1024]{1,0:T(1,128)S(1)} %add.25), channel_id=1, source_target_pairs={{0,8},{1,9},{2,10},{3,11},{4,12},{5,13},{6,14},{7,15},{8,0},{9,1},... | collective-permute-start | bytes 12296 | tf_op jit(solution)/shard_map/ppermute | solution.py:373
  180.1 2.4 %collective-permute-done.12 = f32[1,1024]{1,0:T(1,128)S(1)} collective-permute-done((f32[1,1024]{1,0:T(1,128)S(1)}, f32[1,1024]{1,0:T(1,128)S(1)}, u32[]{:S(2)}, u32[]{:S(2)}) %collective-permute-start.12) | collective-permute-done | bytes 4128 | tf_op jit(solution)/shard_map/ppermute | solution.py:373
  182.5 1.9 %collective-permute-start.13 = (f32[1,1024]{1,0:T(1,128)S(1)}, f32[1,1024]{1,0:T(1,128)S(1)}, u32[]{:S(2)}, u32[]{:S(2)}) collective-permute-start(f32[1,1024]{1,0:T(1,128)S(1)} %add.26), channel_id=1, source_target_pairs={{0,16},{1,17},{2,18},{3,19},{4,20},{5,21},{6,22},{7,23},{8,24},{9,... | collective-permute-start | bytes 12296 | tf_op jit(solution)/shard_map/ppermute | solution.py:373
  184.4 2.0 %shard_map.125 = (bf16[128,1024]{1,0:T(8,128)(2,1)}, bf16[128,1024]{1,0:T(8,128)(2,1)}) custom-call(s32[5]{0:T(128)S(1)} %pad_add_fusion.info, bf16[144,256]{1,0:T(8,128)(2,1)S(1)} %get-tuple-element.36.in0_ref, bf16[144,256]{1,0:T(8,128)(2,1)S(1)} %collective-permute-done.2.in1_ref, bf16[144,256]{1,0:T(8,128)(2,1)S(1)} %collective-permute-done.3.in2_ref, ...), custom_call_target="tpu_custom_call" | custom-call | flops 1 | tf_op jit(solution)/shard_map/pallas_call | solution.py:337
  186.4 2.5 %collective-permute-done.13 = f32[1,1024]{1,0:T(1,128)S(1)} collective-permute-done((f32[1,1024]{1,0:T(1,128)S(1)}, f32[1,1024]{1,0:T(1,128)S(1)}, u32[]{:S(2)}, u32[]{:S(2)}) %collective-permute-start.13) | collective-permute-done | bytes 4128 | tf_op jit(solution)/shard_map/ppermute | solution.py:373
  188.9 0.0 all-to-all-done.3.in_ref
  188.9 1.0 shard_map.129
  (7 shorter events, 0.0 us)
Async XLA Ops:
  2.6 15.3 %copy-start = (bf16[1,128,1024]{2,1,0:T(8,128)(2,1)S(1)}, bf16[1,128,1024]{2,1,0:T(8,128)(2,1)}, u32[]{:S(2)}) copy-start(bf16[1,128,1024]{2,1,0:T(8,128)(2,1)} %param.10) | copy-start | bytes 786436
  2.6 15.3 %copy-start.1 = (bf16[1,128,1024]{2,1,0:T(8,128)(2,1)S(1)}, bf16[1,128,1024]{2,1,0:T(8,128)(2,1)}, u32[]{:S(2)}) copy-start(bf16[1,128,1024]{2,1,0:T(8,128)(2,1)} %param.13) | copy-start | bytes 786436
  2.6 15.3 %copy-start.2 = (bf16[1,128,1024]{2,1,0:T(8,128)(2,1)S(1)}, bf16[1,128,1024]{2,1,0:T(8,128)(2,1)}, u32[]{:S(2)}) copy-start(bf16[1,128,1024]{2,1,0:T(8,128)(2,1)} %param.7) | copy-start | bytes 786436
  2.6 41.2 %all-to-all-start.1 = ((bf16[4,256,256]{2,1,0:T(8,128)(2,1)}), bf16[4,256,256]{2,1,0:T(8,128)(2,1)S(1)}, u32[]{:S(2)}, u32[]{:S(2)}) async-start(bf16[4,256,256]{2,1,0:T(8,128)(2,1)} %shard_map.119), calls=%async_computation.1 | async-start | bytes 1048576 | tf_op jit(solution)/shard_map/all_to_all | solution.py:350
  17.9 0.7 copy-start.3
  43.8 28.9 %all-to-all-start = ((bf16[4,256,256]{2,1,0:T(8,128)(2,1)}), bf16[4,256,256]{2,1,0:T(8,128)(2,1)S(1)}, u32[]{:S(2)}, u32[]{:S(2)}) async-start(bf16[4,256,256]{2,1,0:T(8,128)(2,1)} %shard_map.118), calls=%async_computation | async-start | bytes 1048576 | tf_op jit(solution)/shard_map/all_to_all | solution.py:350
  53.2 21.1 %collective-permute-start.1 = (bf16[4,256,256]{2,1,0:T(8,128)(2,1)S(1)}, bf16[4,256,256]{2,1,0:T(8,128)(2,1)S(1)}, u32[]{:S(2)}, u32[]{:S(2)}) collective-permute-start(bf16[4,256,256]{2,1,0:T(8,128)(2,1)S(1)} %all-to-all-done.1.kv0_ref), channel_id=1, source_target_pairs={{0,256},{32,288},{64,320},{96,352},{128,384},{160,416},{192,448},{... | collective-permute-start | bytes 1572872 | tf_op jit(solution)/shard_map/ppermute | solution.py:387
  54.5 19.8 %collective-permute-start = (bf16[4,256,256]{2,1,0:T(8,128)(2,1)S(1)}, bf16[4,256,256]{2,1,0:T(8,128)(2,1)S(1)}, u32[]{:S(2)}, u32[]{:S(2)}) collective-permute-start(bf16[4,256,256]{2,1,0:T(8,128)(2,1)S(1)} %all-to-all-done.1.kv0_ref), channel_id=1, source_target_pairs={{0,128},{32,160},{64,192},{96,224},{128,256},{160,288},{192,320},{... | collective-permute-start | bytes 1572872 | tf_op jit(solution)/shard_map/ppermute | solution.py:387
  55.8 0.7 copy-start.4
  106.2 36.5 %collective-permute-start.5 = (bf16[4,256,256]{2,1,0:T(8,128)(2,1)S(1)}, bf16[4,256,256]{2,1,0:T(8,128)(2,1)S(1)}, u32[]{:S(2)}, u32[]{:S(2)}) collective-permute-start(bf16[4,256,256]{2,1,0:T(8,128)(2,1)S(1)} %get-tuple-element.34), channel_id=1, source_target_pairs={{128,0},{160,32},{192,64},{224,96},{256,128},{288,160},{320,192},{... | collective-permute-start | bytes 1572872 | tf_op jit(solution)/shard_map/ppermute | solution.py:387
  109.3 33.3 %collective-permute-start.6 = (bf16[4,256,256]{2,1,0:T(8,128)(2,1)S(1)}, bf16[4,256,256]{2,1,0:T(8,128)(2,1)S(1)}, u32[]{:S(2)}, u32[]{:S(2)}) collective-permute-start(bf16[4,256,256]{2,1,0:T(8,128)(2,1)S(1)} %get-tuple-element.44), channel_id=1, source_target_pairs={{256,0},{288,32},{320,64},{352,96},{384,128},{416,160},{448,192},{... | collective-permute-start | bytes 1572872 | tf_op jit(solution)/shard_map/ppermute | solution.py:387
  115.6 14.3 %collective-permute-start.2 = (bf16[144,256]{1,0:T(8,128)(2,1)S(1)}, bf16[144,256]{1,0:T(8,128)(2,1)S(1)}, u32[]{:S(2)}, u32[]{:S(2)}) collective-permute-start(bf16[144,256]{1,0:T(8,128)(2,1)S(1)} %get-tuple-element.37), channel_id=1, source_target_pairs={{0,32},{32,64},{64,96},{96,0},{128,160},{160,192},{192,224},{224,1... | collective-permute-start | bytes 221192 | tf_op jit(solution)/shard_map/ppermute | solution.py:355
  118.1 15.0 %collective-permute-start.3 = (bf16[144,256]{1,0:T(8,128)(2,1)S(1)}, bf16[144,256]{1,0:T(8,128)(2,1)S(1)}, u32[]{:S(2)}, u32[]{:S(2)}) collective-permute-start(bf16[144,256]{1,0:T(8,128)(2,1)S(1)} %get-tuple-element.38), channel_id=1, source_target_pairs={{0,64},{32,96},{64,0},{96,32},{128,192},{160,224},{192,128},{224,1... | collective-permute-start | bytes 221192 | tf_op jit(solution)/shard_map/ppermute | solution.py:355
  125.5 16.6 %collective-permute-start.4 = (bf16[144,256]{1,0:T(8,128)(2,1)S(1)}, bf16[144,256]{1,0:T(8,128)(2,1)S(1)}, u32[]{:S(2)}, u32[]{:S(2)}) collective-permute-start(bf16[144,256]{1,0:T(8,128)(2,1)S(1)} %get-tuple-element.39), channel_id=1, source_target_pairs={{0,96},{32,0},{64,32},{96,64},{128,224},{160,128},{192,160},{224,1... | collective-permute-start | bytes 221192 | tf_op jit(solution)/shard_map/ppermute | solution.py:355
  143.9 44.9 %all-to-all-start.3 = ((bf16[4,384,256]{2,1,0:T(8,128)(2,1)}), bf16[4,384,256]{2,1,0:T(8,128)(2,1)S(1)}, u32[]{:S(2)}, u32[]{:S(2)}) async-start(bf16[4,384,256]{2,1,0:T(8,128)(2,1)} %shard_map.128), calls=%async_computation.3 | async-start | bytes 1572864 | tf_op jit(solution)/shard_map/all_to_all | solution.py:350
  148.0 3.0 %collective-permute-start.7 = (f32[1,1024]{1,0:T(1,128)S(1)}, f32[1,1024]{1,0:T(1,128)S(1)}, u32[]{:S(2)}, u32[]{:S(2)}) collective-permute-start(f32[1,1024]{1,0:T(1,128)S(1)} %shard_map.126), channel_id=1, source_target_pairs={{0,1},{1,0},{2,3},{3,2},{4,5},{5,4},{6,7},{7,6},{8,9},{9,8},{10,11... | collective-permute-start | bytes 12296 | tf_op jit(solution)/shard_map/ppermute | solution.py:381
  151.0 5.5 %collective-permute-start.8 = (f32[1,1024]{1,0:T(1,128)S(1)}, f32[1,1024]{1,0:T(1,128)S(1)}, u32[]{:S(2)}, u32[]{:S(2)}) collective-permute-start(f32[1,1024]{1,0:T(1,128)S(1)} %add.21), channel_id=1, source_target_pairs={{0,2},{1,3},{2,0},{3,1},{4,6},{5,7},{6,4},{7,5},{8,10},{9,11},{10,... | collective-permute-start | bytes 12296 | tf_op jit(solution)/shard_map/ppermute | solution.py:373
  156.5 8.0 %collective-permute-start.9 = (f32[1,1024]{1,0:T(1,128)S(1)}, f32[1,1024]{1,0:T(1,128)S(1)}, u32[]{:S(2)}, u32[]{:S(2)}) collective-permute-start(f32[1,1024]{1,0:T(1,128)S(1)} %add.22), channel_id=1, source_target_pairs={{0,4},{1,5},{2,6},{3,7},{4,0},{5,1},{6,2},{7,3},{8,12},{9,13},{10,... | collective-permute-start | bytes 12296 | tf_op jit(solution)/shard_map/ppermute | solution.py:373
  164.5 5.5 %collective-permute-start.10 = (f32[1,1024]{1,0:T(1,128)S(1)}, f32[1,1024]{1,0:T(1,128)S(1)}, u32[]{:S(2)}, u32[]{:S(2)}) collective-permute-start(f32[1,1024]{1,0:T(1,128)S(1)} %add.23), channel_id=1, source_target_pairs={{0,128},{32,160},{64,192},{96,224},{128,0},{160,32},{192,64},{224,... | collective-permute-start | bytes 12296 | tf_op jit(solution)/shard_map/ppermute | solution.py:373
  170.0 7.0 %collective-permute-start.11 = (f32[1,1024]{1,0:T(1,128)S(1)}, f32[1,1024]{1,0:T(1,128)S(1)}, u32[]{:S(2)}, u32[]{:S(2)}) collective-permute-start(f32[1,1024]{1,0:T(1,128)S(1)} %add.24), channel_id=1, source_target_pairs={{0,256},{32,288},{64,320},{96,352},{128,384},{160,416},{192,448},{... | collective-permute-start | bytes 12296 | tf_op jit(solution)/shard_map/ppermute | solution.py:373
  177.0 5.5 %collective-permute-start.12 = (f32[1,1024]{1,0:T(1,128)S(1)}, f32[1,1024]{1,0:T(1,128)S(1)}, u32[]{:S(2)}, u32[]{:S(2)}) collective-permute-start(f32[1,1024]{1,0:T(1,128)S(1)} %add.25), channel_id=1, source_target_pairs={{0,8},{1,9},{2,10},{3,11},{4,12},{5,13},{6,14},{7,15},{8,0},{9,1},... | collective-permute-start | bytes 12296 | tf_op jit(solution)/shard_map/ppermute | solution.py:373
  182.5 6.4 %collective-permute-start.13 = (f32[1,1024]{1,0:T(1,128)S(1)}, f32[1,1024]{1,0:T(1,128)S(1)}, u32[]{:S(2)}, u32[]{:S(2)}) collective-permute-start(f32[1,1024]{1,0:T(1,128)S(1)} %add.26), channel_id=1, source_target_pairs={{0,16},{1,17},{2,18},{3,19},{4,20},{5,21},{6,22},{7,23},{8,24},{9,... | collective-permute-start | bytes 12296 | tf_op jit(solution)/shard_map/ppermute | solution.py:373

commit v7 on v6

--- a/solution.py
+++ b/solution.py
@@ -338,7 +338,7 @@
         kernel,
         out_shape=outs,
         in_specs=specs,
-        out_specs=[pl.BlockSpec(memory_space=pltpu.VMEM)] * len(outs),
+        out_specs=[pl.BlockSpec(memory_space=space)] * len(outs),
         scratch_shapes=scratch,
         compiler_params=pltpu.CompilerParams(vmem_limit_bytes=limit),
         cost_estimate=pl.CostEstimate(flops=flops, bytes_accessed=0, transcendentals=0),

time: 192 us -> 206 us (1.073)
  Pallas kernels: 18.7 us -> 34.6 us
  waiting for transfers between devices: 72.2 us -> 66.2 us
  starting transfers between devices: 71.2 us -> 75.9 us
    pallas_call x12, Pallas kernels: 18.7 us -> 34.6 us  [call(): pl.pallas_call(kernel, out_shape=outs, in_specs=specs, out_specs=[pl.Bloc...]
    ppermute x6, starting transfers between devices: 17.1 us -> 23.7 us  [add_bits(): lax.ppermute(array, axis, [(i, i ^ bit) for i in range(size)])]
    ppermute x6, waiting for transfers between devices: 18.7 us -> 14.3 us  [add_bits(): lax.ppermute(array, axis, [(i, i ^ bit) for i in range(size)])]
  transfers between devices with their start and end apart: 17 -> 17, of which waited for: 11 -> 12; matrix products, arithmetic and copies ran while one was open for 0% -> 0% of each run, Pallas kernels for 4% -> 4%
where the time goes in v7:
time: 206 us; the launch traced here: 204 us
  starting transfers between devices  75.9 us (37%)
  waiting for transfers between devices  66.2 us (32%)
  Pallas kernels  34.6 us (17%)
  blocking collectives  25.2 us (12%)
    all_to_all x3, waiting for transfers between devices, along_z(): lax.all_to_all(array, 'seq', 0, 0, axis_index_groups=groups, tiled=True)  40.3 us
    pallas_call x12, Pallas kernels, call(): pl.pallas_call(kernel, out_shape=outs, in_specs=specs, out_specs=[pl.Bloc...  34.6 us
    all_to_all x3, starting transfers between devices, along_z(): lax.all_to_all(array, 'seq', 0, 0, axis_index_groups=groups, tiled=True)  28.3 us
    all_to_all x1, blocking collectives, along_z(): lax.all_to_all(array, 'seq', 0, 0, axis_index_groups=groups, tiled=True)  25.2 us
    ppermute x6, starting transfers between devices, add_bits(): lax.ppermute(array, axis, [(i, i ^ bit) for i in range(size)])  23.7 us
    ppermute x6, waiting for transfers between devices, add_bits(): lax.ppermute(array, axis, [(i, i ^ bit) for i in range(size)])  14.3 us
    ppermute x3, starting transfers between devices, shift_z(): return lax.ppermute(array, 'seq', pairs)  12.3 us
    ppermute x3, waiting for transfers between devices, shift_z(): return lax.ppermute(array, 'seq', pairs)  10.4 us
  transfers between devices with their start and end apart: 17, of which 12 were waited for; matrix products, arithmetic and copies ran while one was open for 0% of the time, Pallas kernels for 4%

profile of v7, /device:TPU:24, one launch (start us, length us, event | category | flops | bytes accessed | tf_op | source)
XLA Modules:
  0.0 204.5 jit_solution(16584783178454851414)
XLA Ops:
  0.6 17.1 %shard_map.119 = bf16[4,256,256]{2,1,0:T(8,128)(2,1)} custom-call(bf16[128,1024]{1,0:T(8,128)(2,1)} %bitcast.23, bf16[128,1024]{1,0:T(8,128)(2,1)} %bitcast.24), custom_call_target="tpu_custom_call" | custom-call | flops 1 | tf_op jit(solution)/shard_map/pallas_call | solution.py:337
  17.7 0.0 copy-start
  17.7 0.0 copy-start.1
  17.7 0.0 copy-start.2
  17.7 15.2 %all-to-all-start.1 = ((bf16[4,256,256]{2,1,0:T(8,128)(2,1)}), bf16[4,256,256]{2,1,0:T(8,128)(2,1)S(1)}, u32[]{:S(2)}, u32[]{:S(2)}) async-start(bf16[4,256,256]{2,1,0:T(8,128)(2,1)} %shard_map.119), calls=%async_computation.1 | async-start | bytes 1048576 | tf_op jit(solution)/shard_map/all_to_all | solution.py:350
  33.0 0.0 copy-start.3
  33.0 0.0 copy-done
  33.0 0.0 copy-done.1
  33.0 0.0 copy-done.2
  33.0 0.7 copy-done.3
  33.6 0.9 shard_map.118
  34.5 24.3 %all-to-all-done.1.kv0_ref = bf16[4,256,256]{2,1,0:T(8,128)(2,1)S(1)} async-done(((bf16[4,256,256]{2,1,0:T(8,128)(2,1)}), bf16[4,256,256]{2,1,0:T(8,128)(2,1)S(1)}, u32[]{:S(2)}, u32[]{:S(2)}) %all-to-all-start.1) | async-done | bytes 524320 | tf_op jit(solution)/shard_map/all_to_all | solution.py:350
  58.9 9.4 %all-to-all-start = ((bf16[4,256,256]{2,1,0:T(8,128)(2,1)}), bf16[4,256,256]{2,1,0:T(8,128)(2,1)S(1)}, u32[]{:S(2)}, u32[]{:S(2)}) async-start(bf16[4,256,256]{2,1,0:T(8,128)(2,1)} %shard_map.118), calls=%async_computation | async-start | bytes 1048576 | tf_op jit(solution)/shard_map/all_to_all | solution.py:350
  68.3 1.3 collective-permute-start.1
  69.6 1.3 collective-permute-start
  70.9 0.0 copy-start.4
  70.9 0.6 copy-done.4
  71.6 0.2 reduce-window.9
  71.8 0.1 pad_add_fusion.info
  71.8 16.0 %all-to-all-done.qd_ref = bf16[4,256,256]{2,1,0:T(8,128)(2,1)S(1)} async-done(((bf16[4,256,256]{2,1,0:T(8,128)(2,1)}), bf16[4,256,256]{2,1,0:T(8,128)(2,1)S(1)}, u32[]{:S(2)}, u32[]{:S(2)}) %all-to-all-start) | async-done | bytes 524320 | tf_op jit(solution)/shard_map/all_to_all | solution.py:350
  87.8 1.6 shard_map.120.sum_ref
  89.5 0.0 collective-permute-done.1.kv2_ref
  89.5 0.0 collective-permute-done.kv1_ref
  89.5 2.9 %shard_map.121 = (f32[512,256]{1,0:T(8,128)S(1)}, f32[4,16,128]{2,1,0:T(8,128)S(1)}) custom-call(s32[5]{0:T(128)S(1)} %pad_add_fusion.info, bf16[4,256,256]{2,1,0:T(8,128)(2,1)S(1)} %all-to-all-done.qd_ref, bf16[4,256,256]{2,1,0:T(8,128)(2,1)S(1)} %collective-permute-done.kv1_ref, bf16[4,256,256]{2,1,0:T(8,128)(2,1)S(1)} %collective-permute-done.1.kv2_ref, ...), custom_call_target="tpu_custom_call" | custom-call | flops 1 | tf_op jit(solution)/shard_map/pallas_call | solution.py:337
  92.4 25.2 %all_to_all.20.stats_ref = f32[4,16,128]{2,1,0:T(8,128)S(1)} all-to-all(f32[4,16,128]{2,1,0:T(8,128)S(1)} %get-tuple-element.30), channel_id=1, replica_groups={{0,32,64,96},{128,160,192,224},{256,288,320,352},{384,416,448,480},{1,3..., dimensions={0} | all-to-all | bytes 65536 | tf_op jit(solution)/shard_map/all_to_all | solution.py:350
  117.6 1.3 shard_map.122
  119.0 3.1 %shard_map.123 = (bf16[4,256,256]{2,1,0:T(8,128)(2,1)S(1)}, f32[256,512]{1,0:T(8,128)S(1)}) custom-call(s32[5]{0:T(128)S(1)} %pad_add_fusion.info, bf16[4,256,256]{2,1,0:T(8,128)(2,1)S(1)} %all-to-all-done.qd_ref, bf16[4,256,256]{2,1,0:T(8,128)(2,1)S(1)} %collective-permute-done.kv1_ref, bf16[4,128,256]{2,1,0:T(8,128)(2,1)S(1)} %get-tuple-element.32.grad_ref, ...), custom_call_target="tpu_custom_call" | custom-call | flops 1 | tf_op jit(solution)/shard_map/pallas_call | solution.py:337
  122.0 2.1 %collective-permute-start.5 = (bf16[4,256,256]{2,1,0:T(8,128)(2,1)S(1)}, bf16[4,256,256]{2,1,0:T(8,128)(2,1)S(1)}, u32[]{:S(2)}, u32[]{:S(2)}) collective-permute-start(bf16[4,256,256]{2,1,0:T(8,128)(2,1)S(1)} %get-tuple-element.34), channel_id=1, source_target_pairs={{128,0},{160,32},{192,64},{224,96},{256,128},{288,160},{320,192},{... | collective-permute-start | bytes 1572872 | tf_op jit(solution)/shard_map/ppermute | solution.py:387
  124.1 5.0 %collective-permute-start.6 = (bf16[4,256,256]{2,1,0:T(8,128)(2,1)S(1)}, bf16[4,256,256]{2,1,0:T(8,128)(2,1)S(1)}, u32[]{:S(2)}, u32[]{:S(2)}) collective-permute-start(bf16[4,256,256]{2,1,0:T(8,128)(2,1)S(1)} %get-tuple-element.44), channel_id=1, source_target_pairs={{256,0},{288,32},{320,64},{352,96},{384,128},{416,160},{448,192},{... | collective-permute-start | bytes 1572872 | tf_op jit(solution)/shard_map/ppermute | solution.py:387
  129.1 0.8 shard_map.124
  129.9 2.6 %collective-permute-start.2 = (bf16[144,256]{1,0:T(8,128)(2,1)S(1)}, bf16[144,256]{1,0:T(8,128)(2,1)S(1)}, u32[]{:S(2)}, u32[]{:S(2)}) collective-permute-start(bf16[144,256]{1,0:T(8,128)(2,1)S(1)} %get-tuple-element.37), channel_id=1, source_target_pairs={{0,32},{32,64},{64,96},{96,0},{128,160},{160,192},{192,224},{224,1... | collective-permute-start | bytes 221192 | tf_op jit(solution)/shard_map/ppermute | solution.py:355
  132.5 7.2 %collective-permute-start.3 = (bf16[144,256]{1,0:T(8,128)(2,1)S(1)}, bf16[144,256]{1,0:T(8,128)(2,1)S(1)}, u32[]{:S(2)}, u32[]{:S(2)}) collective-permute-start(bf16[144,256]{1,0:T(8,128)(2,1)S(1)} %get-tuple-element.38), channel_id=1, source_target_pairs={{0,64},{32,96},{64,0},{96,32},{128,192},{160,224},{192,128},{224,1... | collective-permute-start | bytes 221192 | tf_op jit(solution)/shard_map/ppermute | solution.py:355
  139.8 2.5 %collective-permute-start.4 = (bf16[144,256]{1,0:T(8,128)(2,1)S(1)}, bf16[144,256]{1,0:T(8,128)(2,1)S(1)}, u32[]{:S(2)}, u32[]{:S(2)}) collective-permute-start(bf16[144,256]{1,0:T(8,128)(2,1)S(1)} %get-tuple-element.39), channel_id=1, source_target_pairs={{0,96},{32,0},{64,32},{96,64},{128,224},{160,128},{192,160},{224,1... | collective-permute-start | bytes 221192 | tf_op jit(solution)/shard_map/ppermute | solution.py:355
  142.3 2.1 %shard_map.127 = (f32[256,512]{1,0:T(8,128)S(1)}, f32[4,256,256]{2,1,0:T(8,128)S(1)}) custom-call(s32[5]{0:T(128)S(1)} %pad_add_fusion.info, bf16[4,256,256]{2,1,0:T(8,128)(2,1)S(1)} %all-to-all-done.qd_ref, bf16[4,256,256]{2,1,0:T(8,128)(2,1)S(1)} %all-to-all-done.1.kv0_ref, bf16[4,128,256]{2,1,0:T(8,128)(2,1)S(1)} %get-tuple-element.32.grad_ref, ...), custom_call_target="tpu_custom_call" | custom-call | flops 1 | tf_op jit(solution)/shard_map/pallas_call | solution.py:337
  144.4 0.6 collective-permute-done.2.in1_ref
  145.0 2.6 %collective-permute-done.3.in2_ref = bf16[144,256]{1,0:T(8,128)(2,1)S(1)} collective-permute-done((bf16[144,256]{1,0:T(8,128)(2,1)S(1)}, bf16[144,256]{1,0:T(8,128)(2,1)S(1)}, u32[]{:S(2)}, u32[]{:S(2)}) %collective-permute-start.3) | collective-permute-done | bytes 73760 | tf_op jit(solution)/shard_map/ppermute | solution.py:355
  147.6 7.2 %collective-permute-done.4.in3_ref = bf16[144,256]{1,0:T(8,128)(2,1)S(1)} collective-permute-done((bf16[144,256]{1,0:T(8,128)(2,1)S(1)}, bf16[144,256]{1,0:T(8,128)(2,1)S(1)}, u32[]{:S(2)}, u32[]{:S(2)}) %collective-permute-start.4) | collective-permute-done | bytes 73760 | tf_op jit(solution)/shard_map/ppermute | solution.py:355
  154.8 0.6 shard_map.126
  155.3 0.0 collective-permute-done.5.other1_ref
  155.3 0.0 collective-permute-done.6.other2_ref
  155.4 1.3 shard_map.128
  156.7 3.7 %all-to-all-start.3 = ((bf16[4,384,256]{2,1,0:T(8,128)(2,1)}), bf16[4,384,256]{2,1,0:T(8,128)(2,1)S(1)}, u32[]{:S(2)}, u32[]{:S(2)}) async-start(bf16[4,384,256]{2,1,0:T(8,128)(2,1)} %shard_map.128), calls=%async_computation.3 | async-start | bytes 1572864 | tf_op jit(solution)/shard_map/all_to_all | solution.py:350
  160.4 1.9 collective-permute-start.7
  162.3 1.1 collective-permute-done.7
  163.4 4.7 %collective-permute-start.8 = (f32[1,1024]{1,0:T(1,128)S(1)}, f32[1,1024]{1,0:T(1,128)S(1)}, u32[]{:S(2)}, u32[]{:S(2)}) collective-permute-start(f32[1,1024]{1,0:T(1,128)S(1)} %add.21), channel_id=1, source_target_pairs={{0,2},{1,3},{2,0},{3,1},{4,6},{5,7},{6,4},{7,5},{8,10},{9,11},{10,... | collective-permute-start | bytes 12296 | tf_op jit(solution)/shard_map/ppermute | solution.py:373
  168.2 1.6 collective-permute-done.8
  169.7 7.7 %collective-permute-start.9 = (f32[1,1024]{1,0:T(1,128)S(1)}, f32[1,1024]{1,0:T(1,128)S(1)}, u32[]{:S(2)}, u32[]{:S(2)}) collective-permute-start(f32[1,1024]{1,0:T(1,128)S(1)} %add.22), channel_id=1, source_target_pairs={{0,4},{1,5},{2,6},{3,7},{4,0},{5,1},{6,2},{7,3},{8,12},{9,13},{10,... | collective-permute-start | bytes 12296 | tf_op jit(solution)/shard_map/ppermute | solution.py:373
  177.4 1.6 collective-permute-done.9
  179.0 1.9 collective-permute-start.10
  180.9 3.6 %collective-permute-done.10 = f32[1,1024]{1,0:T(1,128)S(1)} collective-permute-done((f32[1,1024]{1,0:T(1,128)S(1)}, f32[1,1024]{1,0:T(1,128)S(1)}, u32[]{:S(2)}, u32[]{:S(2)}) %collective-permute-start.10) | collective-permute-done | bytes 4128 | tf_op jit(solution)/shard_map/ppermute | solution.py:373
  184.5 1.9 collective-permute-start.11
  186.4 5.1 %collective-permute-done.11 = f32[1,1024]{1,0:T(1,128)S(1)} collective-permute-done((f32[1,1024]{1,0:T(1,128)S(1)}, f32[1,1024]{1,0:T(1,128)S(1)}, u32[]{:S(2)}, u32[]{:S(2)}) %collective-permute-start.11) | collective-permute-done | bytes 4128 | tf_op jit(solution)/shard_map/ppermute | solution.py:373
  191.5 4.0 %collective-permute-start.12 = (f32[1,1024]{1,0:T(1,128)S(1)}, f32[1,1024]{1,0:T(1,128)S(1)}, u32[]{:S(2)}, u32[]{:S(2)}) collective-permute-start(f32[1,1024]{1,0:T(1,128)S(1)} %add.25), channel_id=1, source_target_pairs={{0,8},{1,9},{2,10},{3,11},{4,12},{5,13},{6,14},{7,15},{8,0},{9,1},... | collective-permute-start | bytes 12296 | tf_op jit(solution)/shard_map/ppermute | solution.py:373
  195.5 1.6 collective-permute-done.12
  197.1 3.4 %collective-permute-start.13 = (f32[1,1024]{1,0:T(1,128)S(1)}, f32[1,1024]{1,0:T(1,128)S(1)}, u32[]{:S(2)}, u32[]{:S(2)}) collective-permute-start(f32[1,1024]{1,0:T(1,128)S(1)} %add.26), channel_id=1, source_target_pairs={{0,16},{1,17},{2,18},{3,19},{4,20},{5,21},{6,22},{7,23},{8,24},{9,... | collective-permute-start | bytes 12296 | tf_op jit(solution)/shard_map/ppermute | solution.py:373
  200.5 2.0 shard_map.125
  202.5 1.0 collective-permute-done.13
  203.5 0.0 all-to-all-done.3.in_ref
  203.5 1.0 shard_map.129
  (7 shorter events, 0.0 us)
Async XLA Ops:
  17.7 15.3 %copy-start = (bf16[1,128,1024]{2,1,0:T(8,128)(2,1)S(1)}, bf16[1,128,1024]{2,1,0:T(8,128)(2,1)}, u32[]{:S(2)}) copy-start(bf16[1,128,1024]{2,1,0:T(8,128)(2,1)} %param.10) | copy-start | bytes 786436
  17.7 15.3 %copy-start.1 = (bf16[1,128,1024]{2,1,0:T(8,128)(2,1)S(1)}, bf16[1,128,1024]{2,1,0:T(8,128)(2,1)}, u32[]{:S(2)}) copy-start(bf16[1,128,1024]{2,1,0:T(8,128)(2,1)} %param.13) | copy-start | bytes 786436
  17.7 15.3 %copy-start.2 = (bf16[1,128,1024]{2,1,0:T(8,128)(2,1)S(1)}, bf16[1,128,1024]{2,1,0:T(8,128)(2,1)}, u32[]{:S(2)}) copy-start(bf16[1,128,1024]{2,1,0:T(8,128)(2,1)} %param.7) | copy-start | bytes 786436
  17.7 41.2 %all-to-all-start.1 = ((bf16[4,256,256]{2,1,0:T(8,128)(2,1)}), bf16[4,256,256]{2,1,0:T(8,128)(2,1)S(1)}, u32[]{:S(2)}, u32[]{:S(2)}) async-start(bf16[4,256,256]{2,1,0:T(8,128)(2,1)} %shard_map.119), calls=%async_computation.1 | async-start | bytes 1048576 | tf_op jit(solution)/shard_map/all_to_all | solution.py:350
  33.0 0.7 copy-start.3
  58.9 28.9 %all-to-all-start = ((bf16[4,256,256]{2,1,0:T(8,128)(2,1)}), bf16[4,256,256]{2,1,0:T(8,128)(2,1)S(1)}, u32[]{:S(2)}, u32[]{:S(2)}) async-start(bf16[4,256,256]{2,1,0:T(8,128)(2,1)} %shard_map.118), calls=%async_computation | async-start | bytes 1048576 | tf_op jit(solution)/shard_map/all_to_all | solution.py:350
  68.3 21.1 %collective-permute-start.1 = (bf16[4,256,256]{2,1,0:T(8,128)(2,1)S(1)}, bf16[4,256,256]{2,1,0:T(8,128)(2,1)S(1)}, u32[]{:S(2)}, u32[]{:S(2)}) collective-permute-start(bf16[4,256,256]{2,1,0:T(8,128)(2,1)S(1)} %all-to-all-done.1.kv0_ref), channel_id=1, source_target_pairs={{0,256},{32,288},{64,320},{96,352},{128,384},{160,416},{192,448},{... | collective-permute-start | bytes 1572872 | tf_op jit(solution)/shard_map/ppermute | solution.py:387
  69.6 19.8 %collective-permute-start = (bf16[4,256,256]{2,1,0:T(8,128)(2,1)S(1)}, bf16[4,256,256]{2,1,0:T(8,128)(2,1)S(1)}, u32[]{:S(2)}, u32[]{:S(2)}) collective-permute-start(bf16[4,256,256]{2,1,0:T(8,128)(2,1)S(1)} %all-to-all-done.1.kv0_ref), channel_id=1, source_target_pairs={{0,128},{32,160},{64,192},{96,224},{128,256},{160,288},{192,320},{... | collective-permute-start | bytes 1572872 | tf_op jit(solution)/shard_map/ppermute | solution.py:387
  70.9 0.7 copy-start.4
  122.0 33.3 %collective-permute-start.5 = (bf16[4,256,256]{2,1,0:T(8,128)(2,1)S(1)}, bf16[4,256,256]{2,1,0:T(8,128)(2,1)S(1)}, u32[]{:S(2)}, u32[]{:S(2)}) collective-permute-start(bf16[4,256,256]{2,1,0:T(8,128)(2,1)S(1)} %get-tuple-element.34), channel_id=1, source_target_pairs={{128,0},{160,32},{192,64},{224,96},{256,128},{288,160},{320,192},{... | collective-permute-start | bytes 1572872 | tf_op jit(solution)/shard_map/ppermute | solution.py:387
  124.1 31.2 %collective-permute-start.6 = (bf16[4,256,256]{2,1,0:T(8,128)(2,1)S(1)}, bf16[4,256,256]{2,1,0:T(8,128)(2,1)S(1)}, u32[]{:S(2)}, u32[]{:S(2)}) collective-permute-start(bf16[4,256,256]{2,1,0:T(8,128)(2,1)S(1)} %get-tuple-element.44), channel_id=1, source_target_pairs={{256,0},{288,32},{320,64},{352,96},{384,128},{416,160},{448,192},{... | collective-permute-start | bytes 1572872 | tf_op jit(solution)/shard_map/ppermute | solution.py:387
  129.9 15.0 %collective-permute-start.2 = (bf16[144,256]{1,0:T(8,128)(2,1)S(1)}, bf16[144,256]{1,0:T(8,128)(2,1)S(1)}, u32[]{:S(2)}, u32[]{:S(2)}) collective-permute-start(bf16[144,256]{1,0:T(8,128)(2,1)S(1)} %get-tuple-element.37), channel_id=1, source_target_pairs={{0,32},{32,64},{64,96},{96,0},{128,160},{160,192},{192,224},{224,1... | collective-permute-start | bytes 221192 | tf_op jit(solution)/shard_map/ppermute | solution.py:355
  132.5 15.1 %collective-permute-start.3 = (bf16[144,256]{1,0:T(8,128)(2,1)S(1)}, bf16[144,256]{1,0:T(8,128)(2,1)S(1)}, u32[]{:S(2)}, u32[]{:S(2)}) collective-permute-start(bf16[144,256]{1,0:T(8,128)(2,1)S(1)} %get-tuple-element.38), channel_id=1, source_target_pairs={{0,64},{32,96},{64,0},{96,32},{128,192},{160,224},{192,128},{224,1... | collective-permute-start | bytes 221192 | tf_op jit(solution)/shard_map/ppermute | solution.py:355
  139.8 15.0 %collective-permute-start.4 = (bf16[144,256]{1,0:T(8,128)(2,1)S(1)}, bf16[144,256]{1,0:T(8,128)(2,1)S(1)}, u32[]{:S(2)}, u32[]{:S(2)}) collective-permute-start(bf16[144,256]{1,0:T(8,128)(2,1)S(1)} %get-tuple-element.39), channel_id=1, source_target_pairs={{0,96},{32,0},{64,32},{96,64},{128,224},{160,128},{192,160},{224,1... | collective-permute-start | bytes 221192 | tf_op jit(solution)/shard_map/ppermute | solution.py:355
  156.7 46.8 %all-to-all-start.3 = ((bf16[4,384,256]{2,1,0:T(8,128)(2,1)}), bf16[4,384,256]{2,1,0:T(8,128)(2,1)S(1)}, u32[]{:S(2)}, u32[]{:S(2)}) async-start(bf16[4,384,256]{2,1,0:T(8,128)(2,1)} %shard_map.128), calls=%async_computation.3 | async-start | bytes 1572864 | tf_op jit(solution)/shard_map/all_to_all | solution.py:350
  160.4 3.0 %collective-permute-start.7 = (f32[1,1024]{1,0:T(1,128)S(1)}, f32[1,1024]{1,0:T(1,128)S(1)}, u32[]{:S(2)}, u32[]{:S(2)}) collective-permute-start(f32[1,1024]{1,0:T(1,128)S(1)} %shard_map.126), channel_id=1, source_target_pairs={{0,1},{1,0},{2,3},{3,2},{4,5},{5,4},{6,7},{7,6},{8,9},{9,8},{10,11... | collective-permute-start | bytes 12296 | tf_op jit(solution)/shard_map/ppermute | solution.py:381
  163.4 6.3 %collective-permute-start.8 = (f32[1,1024]{1,0:T(1,128)S(1)}, f32[1,1024]{1,0:T(1,128)S(1)}, u32[]{:S(2)}, u32[]{:S(2)}) collective-permute-start(f32[1,1024]{1,0:T(1,128)S(1)} %add.21), channel_id=1, source_target_pairs={{0,2},{1,3},{2,0},{3,1},{4,6},{5,7},{6,4},{7,5},{8,10},{9,11},{10,... | collective-permute-start | bytes 12296 | tf_op jit(solution)/shard_map/ppermute | solution.py:373
  169.7 9.2 %collective-permute-start.9 = (f32[1,1024]{1,0:T(1,128)S(1)}, f32[1,1024]{1,0:T(1,128)S(1)}, u32[]{:S(2)}, u32[]{:S(2)}) collective-permute-start(f32[1,1024]{1,0:T(1,128)S(1)} %add.22), channel_id=1, source_target_pairs={{0,4},{1,5},{2,6},{3,7},{4,0},{5,1},{6,2},{7,3},{8,12},{9,13},{10,... | collective-permute-start | bytes 12296 | tf_op jit(solution)/shard_map/ppermute | solution.py:373
  179.0 5.5 %collective-permute-start.10 = (f32[1,1024]{1,0:T(1,128)S(1)}, f32[1,1024]{1,0:T(1,128)S(1)}, u32[]{:S(2)}, u32[]{:S(2)}) collective-permute-start(f32[1,1024]{1,0:T(1,128)S(1)} %add.23), channel_id=1, source_target_pairs={{0,128},{32,160},{64,192},{96,224},{128,0},{160,32},{192,64},{224,... | collective-permute-start | bytes 12296 | tf_op jit(solution)/shard_map/ppermute | solution.py:373
  184.5 7.0 %collective-permute-start.11 = (f32[1,1024]{1,0:T(1,128)S(1)}, f32[1,1024]{1,0:T(1,128)S(1)}, u32[]{:S(2)}, u32[]{:S(2)}) collective-permute-start(f32[1,1024]{1,0:T(1,128)S(1)} %add.24), channel_id=1, source_target_pairs={{0,256},{32,288},{64,320},{96,352},{128,384},{160,416},{192,448},{... | collective-permute-start | bytes 12296 | tf_op jit(solution)/shard_map/ppermute | solution.py:373
  191.5 5.6 %collective-permute-start.12 = (f32[1,1024]{1,0:T(1,128)S(1)}, f32[1,1024]{1,0:T(1,128)S(1)}, u32[]{:S(2)}, u32[]{:S(2)}) collective-permute-start(f32[1,1024]{1,0:T(1,128)S(1)} %add.25), channel_id=1, source_target_pairs={{0,8},{1,9},{2,10},{3,11},{4,12},{5,13},{6,14},{7,15},{8,0},{9,1},... | collective-permute-start | bytes 12296 | tf_op jit(solution)/shard_map/ppermute | solution.py:373
  197.1 6.4 %collective-permute-start.13 = (f32[1,1024]{1,0:T(1,128)S(1)}, f32[1,1024]{1,0:T(1,128)S(1)}, u32[]{:S(2)}, u32[]{:S(2)}) collective-permute-start(f32[1,1024]{1,0:T(1,128)S(1)} %add.26), channel_id=1, source_target_pairs={{0,16},{1,17},{2,18},{3,19},{4,20},{5,21},{6,22},{7,23},{8,24},{9,... | collective-permute-start | bytes 12296 | tf_op jit(solution)/shard_map/ppermute | solution.py:373
